TPU v7x, 256 devices: a whole 4x4x8 slice. The times are simulated.
256 devices in a mesh: row: 16 (over x_hi, y, core), col: 16 (over x_lo, z).
Axes of the slice: x: 4 (x_hi: 2, x_lo: 2; x = x_hi * 2 + x_lo), y: 4, z: 8, core: 2. Of those that a mesh axis runs over, the one named last changes fastest.
Arguments:
- pair: bfloat16 [2048, 2048, 128], P('row', 'col'), may hold values from -6 to 6
- ln_gain: float32 [128], replicated, may hold values from 0.5 to 1.5
- ln_bias: float32 [128], replicated, may hold values from -3 to 3
- w_proj: bfloat16 [128, 512], replicated, may hold values from -0.5 to 0.5
- w_gate: bfloat16 [128, 128], replicated, may hold values from -0.5 to 0.5
- out_gain: float32 [128], replicated, may hold values from 0.5 to 1.5
- out_bias: float32 [128], replicated, may hold values from -3 to 3
- w_out: bfloat16 [128, 128], replicated, may hold values from -0.5 to 0.5
Outputs:
- update: bfloat16 [2048, 2048, 128], P('row', 'col')
All inputs are finite; a program needn't handle non-finite values.
Results may differ from a plain program's by a relative error of at most 0.0053.
Values may be sent and summed in bfloat16 or wider, within the bound.
No kernel may reach another device: no remote copies, remote signals or barrier semaphores. Data moves between devices by JAX's collectives and lax.ppermute only.
A program may use at most 128 MiB of HBM per device.

v0:
```python
import functools

import jax
import jax.numpy as jnp
from jax import lax
from jax.experimental import pallas as pl
from jax.experimental.pallas import tpu as pltpu
from jax.sharding import PartitionSpec as P

EPSILON = 1e-05
F32, BF16 = jnp.float32, jnp.bfloat16
NT = (((1,), (1,)), ((), ()))
TN = (((0,), (0,)), ((), ()))
AXES = ("row", "col")
ROWS = 32


def place(r, c):
    return (r % 16) * 16 + c % 16


def everyone(move):
    return [(place(r, c), place(*move(r, c))) for r in range(16) for c in range(16)]


def side(row):
    return row % 16 // 8


def scatter_pairs(a):
    return [(place(c, c + d), place(c ^ (2 * a), c + d)) for c in range(16) for d in range(3)]


def across_pairs(third):
    pairs = []
    for r in range(16):
        for c in range(16):
            even = (r - c) % 2 == 0
            d = 2 if third else 0 if even else 1
            if (even or not third) and side(r) == side(c - d):
                pairs.append((place(r, c), place(r ^ 8, c)))
    return pairs


def shift_pairs():
    return everyone(lambda r, c: (r, c - 2) if (r - c) % 2 == 0 else (r ^ 1, c - 1))


def back(r, c):
    return (r, c - 1)


def swap(r, c):
    return (r ^ 1, c)


def after(value, *others):
    return lax.optimization_barrier((value,) + others)[0]


def send(value, pairs):
    return lax.ppermute(value, AXES, pairs)


def sigmoid(x):
    return 0.5 * jnp.tanh(0.5 * x) + 0.5


def normed_rows(x, gain, bias):
    mean_of = jnp.full((128, 128), 1 / 128, BF16)
    centred = x.astype(F32) - jnp.dot(x, mean_of, preferred_element_type=F32)
    square = centred * centred
    high = square.astype(BF16)
    low = (square - high.astype(F32)).astype(BF16)
    variance = jnp.dot(high, mean_of, preferred_element_type=F32) + jnp.dot(
        low, mean_of, preferred_element_type=F32
    )
    return (centred * lax.rsqrt(variance + EPSILON) * gain + bias).astype(BF16)


def left_kernel(x_ref, gain_ref, bias_ref, wt_ref, wg_ref, left_ref, gate_ref, scratch):
    n = normed_rows(x_ref[...].reshape(16 * 128, 128), gain_ref[...], bias_ref[...])
    gate_ref[...] = sigmoid(jnp.dot(n, wg_ref[...], preferred_element_type=F32)).reshape(16, 128, 128)
    p = lax.dot_general(wt_ref[...], n, NT, preferred_element_type=F32)
    v = sigmoid(p[:128]) * p[128:]
    for i in range(16):
        scratch[i * 128 : (i + 1) * 128, :] = v[:, i * 128 : (i + 1) * 128]

    def turn(h, _):
        left_ref[h] = scratch[pl.ds(h, 16, stride=128), :].astype(BF16)
        return 0

    lax.fori_loop(0, 128, turn, 0, unroll=16)


def whole(a):
    return pl.BlockSpec(a.shape, lambda *_: (0,) * a.ndim)


def left_and_gate(pair, start, rows, gain, bias, wt, w_gate):
    first = start // 16
    return pl.pallas_call(
        left_kernel,
        out_shape=[
            jax.ShapeDtypeStruct((128, rows, 128), BF16),
            jax.ShapeDtypeStruct((rows, 128, 128), F32),
        ],
        grid=(rows // 16,),
        in_specs=[
            pl.BlockSpec((16, 128, 128), lambda i: (first + i, 0, 0)),
            whole(gain),
            whole(bias),
            whole(wt),
            whole(w_gate),
        ],
        out_specs=[
            pl.BlockSpec((128, 16, 128), lambda i: (0, i, 0)),
            pl.BlockSpec((16, 128, 128), lambda i: (i, 0, 0)),
        ],
        scratch_shapes=[pltpu.VMEM((16 * 128, 128), F32)],
        compiler_params=pltpu.CompilerParams(vmem_limit_bytes=48 << 20),
        cost_estimate=pl.CostEstimate(
            flops=rows * 128 * 128 * 2 * 768, bytes_accessed=rows * 128 * 128 * 8, transcendentals=rows * 128 * 256
        ),
    )(pair, gain, bias, wt, w_gate)


def right_kernel(x_ref, gain_ref, bias_ref, wt_ref, right_ref, scratch):
    d = pl.program_id(0)
    n = normed_rows(x_ref[...].reshape(16 * 128, 128), gain_ref[...], bias_ref[...])
    p = lax.dot_general(wt_ref[...], n, NT, preferred_element_type=F32)
    v = sigmoid(p[:64]) * p[64:]
    for j in range(16):
        scratch[j * 64 : (j + 1) * 64, :] = v[:, j * 128 : (j + 1) * 128]

    def turn(h, _):
        right_ref[h] = scratch[pl.ds(h, 16, stride=64), :].astype(BF16)
        return 0

    lax.fori_loop(0, 64, turn, 0, unroll=16)


def right_piece(pieces, gain, bias, wt):
    return pl.pallas_call(
        right_kernel,
        out_shape=jax.ShapeDtypeStruct((64, 16, 384), BF16),
        grid=(3,),
        in_specs=[pl.BlockSpec((16, 128, 128), lambda d: (d, 0, 0)), whole(gain), whole(bias), whole(wt)],
        out_specs=pl.BlockSpec((64, 16, 128), lambda d: (0, 0, d)),
        scratch_shapes=[pltpu.VMEM((16 * 64, 128), F32)],
        compiler_params=pltpu.CompilerParams(vmem_limit_bytes=32 << 20),
        cost_estimate=pl.CostEstimate(flops=48 * 128 * 128 * 2 * 384, bytes_accessed=3 << 20, transcendentals=48 * 128 * 64),
    )(pieces, gain, bias, wt)


STEP = 8


def final_kernel(place_ref, *refs, subs, aliased):
    count = len(subs)
    lefts = [refs[4 * s : 4 * s + 3] for s in range(count)]
    gates = [refs[4 * s + 3] for s in range(count)]
    rest = refs[4 * count :]
    rights, rest = rest[:16], rest[16:]
    gain_ref, bias_ref, w_ref = rest[:3]
    out_ref, scratch = rest[3 + aliased :]
    rows = sum(subs)
    step = pl.program_id(0)
    block, core = place_ref[0], place_ref[1]
    for half in range(2):
        which = core if half == 0 else 1 - core
        for t in range(STEP):
            left = jnp.concatenate(
                [jnp.concatenate([ref[which, t] for ref in sub], axis=-1) for sub in lefts], axis=0
            )
            right = jnp.concatenate([rights[2 * n + half][t] for n in range(8)], axis=0)
            h = which * 64 + step * STEP + t
            scratch[pl.ds(pl.multiple_of(h * rows, rows), rows), :] = lax.dot_general(
                left, right, NT, preferred_element_type=F32
            )

    @pl.when(step == 64 // STEP - 1)
    def _():
        base = 0
        for sub, gate_ref in zip(subs, gates):

            def some_rows(q, _, base=base, gate_ref=gate_ref):
                parts = []
                for e in range(8):
                    x = scratch[pl.ds(base + q * 8 + e, 128, stride=rows), :]
                    centred = x - jnp.mean(x, axis=0, keepdims=True)
                    variance = jnp.mean(centred * centred, axis=0, keepdims=True)
                    parts.append(
                        (centred * lax.rsqrt(variance + EPSILON) * gain_ref[...] + bias_ref[...]).astype(BF16)
                    )
                y = jnp.concatenate(parts, axis=1)
                out = lax.dot_general(y, w_ref[...], TN, preferred_element_type=F32)
                for e in range(8):
                    for n in range(8):
                        chip = block ^ n
                        at = pl.ds(pl.multiple_of(chip % 4 * 32 + chip // 4 * 16, 16), 16)
                        mine = out[e * 128 + n * 16 : e * 128 + n * 16 + 16]
                        out_ref[base + q * 8 + e, at, :] = (gate_ref[q * 8 + e, at, :] * mine).astype(BF16)
                return 0

            lax.fori_loop(0, sub // 8, some_rows, 0)
            base += sub


def final(where, groups, rights, gain, bias, w_out, update, block):
    subs = tuple(g[3].shape[0] for g in groups)
    rows = sum(subs)
    operands, specs = [], []
    for l0, l1, l2, gate in groups:
        for l in (l0, l1, l2):
            operands.append(l.reshape(2, 64, gate.shape[0], 128))
            specs.append(pl.BlockSpec((2, STEP, gate.shape[0], 128), lambda s, _: (0, s, 0, 0)))
        operands.append(gate)
        specs.append(whole(gate))
    operands += rights
    specs += [pl.BlockSpec((STEP, 16, 384), lambda s, _: (s, 0, 0))] * 16
    operands += [gain, bias, w_out]
    specs += [whole(gain), whole(bias), whole(w_out)]
    aliases = {}
    if update is not None:
        aliases = {1 + len(operands): 0}
        operands.append(update)
        specs.append(pl.BlockSpec(memory_space=pl.ANY))
    return pl.pallas_call(
        functools.partial(final_kernel, subs=subs, aliased=len(aliases)),
        out_shape=jax.ShapeDtypeStruct((128, 128, 128), BF16),
        grid_spec=pltpu.PrefetchScalarGridSpec(
            num_scalar_prefetch=1,
            grid=(64 // STEP,),
            in_specs=specs,
            out_specs=pl.BlockSpec((rows, 128, 128), lambda s, _: (block, 0, 0)),
            scratch_shapes=[pltpu.VMEM((128 * rows, 128), F32)],
        ),
        input_output_aliases=aliases,
        compiler_params=pltpu.CompilerParams(vmem_limit_bytes=56 << 20),
        cost_estimate=pl.CostEstimate(
            flops=rows * 128 * 128 * 2 * 512, bytes_accessed=(14 << 20) + rows * 128 * 128 * 12, transcendentals=0
        ),
    )(where, *operands)


def shards(pair, ln_gain, ln_bias, w_proj, w_gate, out_gain, out_bias, w_out):
    row, col = lax.axis_index("row"), lax.axis_index("col")
    core, chip = row % 2, row // 2
    gain, bias = ln_gain[None, :], ln_bias[None, :]

    wt_left = w_proj[:, :256].T

    def left_of(q, source):
        return left_and_gate(source, ROWS * q, ROWS, gain, bias, wt_left, w_gate)

    def one_back(value):
        return send(value, everyone(back))

    quarters = [pair[:32]] + [send(pair[32 * a : 32 * a + 32], scatter_pairs(a)) for a in (1, 2, 3)]
    lefts = [left_of(q, pair) for q in range(3)]
    once = [one_back(lefts[0][0]), one_back(lefts[1][0])]
    once.append(one_back(after(lefts[2][0], once[0])))
    quarters[1] = after(quarters[1], lefts[1][0])
    even = core == col % 2
    y, x_side = chip % 4, chip // 4

    def quarter_of(d):
        away = y ^ ((col - d) % 16 // 2 % 4)
        picked = quarters[0]
        for a in range(1, 4):
            picked = jnp.where(away == a, quarters[a], picked)
        return picked

    one = jnp.where(even, quarter_of(0), quarter_of(1))
    two = quarter_of(2)
    one_across = send(one[16:], across_pairs(False))
    two_across = send(two[16:], across_pairs(True))
    d_one = jnp.where(even, 0, 1)
    one = jnp.where(x_side == (col - d_one) % 16 // 8, one[:16], one_across)
    two = jnp.where(x_side == (col - 2) % 16 // 8, two[:16], two_across)
    moving = jnp.where(even, two, one)
    shifted = send(moving, shift_pairs())
    swapped_one = send(one, everyone(swap))
    lefts.append(left_of(3, after(pair, moving)))
    once.append(one_back(lefts[3][0]))
    shifted = after(shifted, once[1], once[2], swapped_one, lefts[3][0])
    twice = [one_back(after(once[0], shifted))]
    swapped = send(shifted, everyone(swap))
    first, swapped_first = one, swapped_one
    raw = jnp.concatenate(
        [
            jnp.where(even, first, swapped_first),
            jnp.where(even, swapped, shifted),
            jnp.where(even, shifted, swapped),
        ],
        axis=0,
    )
    half = [lax.dynamic_slice_in_dim(w_proj, 256 + 128 * v + 64 * core, 64, 1) for v in range(2)]
    mine = right_piece(raw, gain, bias, jnp.concatenate(half, axis=1).T)
    got = {0: mine}

    def exchange(value, n):
        return send(value, everyone(lambda r, c: (r ^ (2 * n), c)))

    for n in (4, 1, 3):
        got[n] = exchange(mine, n)
    twice.append(one_back(after(once[1], mine)))
    stage = after(got[4], got[1], got[3], once[3])
    got[5], got[7] = exchange(stage, 1), exchange(stage, 3)
    got[2] = exchange(after(mine, stage), 2)
    twice.append(one_back(after(once[2], stage)))
    stage = after(got[4], got[5], got[7], got[2], twice[0])
    got[6] = exchange(stage, 2)
    twice.append(one_back(after(once[3], stage)))
    rights = []
    for n in range(8):
        rights += [got[n], send(got[n], everyone(swap))]

    where = jnp.stack([chip ^ (col // 2), core]).astype(jnp.int32)
    out_g = jnp.broadcast_to(out_gain[:, None], (128, 128))
    out_b = jnp.broadcast_to(out_bias[:, None], (128, 128))

    groups = [(lefts[q][0], once[q], twice[q], lefts[q][1]) for q in range(4)]
    update = final(after(where, twice[2]), groups[:2], rights, out_g, out_b, w_out, None, 0)
    return final(where, groups[2:], rights, out_g, out_b, w_out, update, 1)


def solution(mesh):
    in_specs = (P("row", "col", None), P(), P(), P(), P(), P(), P(), P())
    out_specs = P("row", "col", None)
    return jax.shard_map(shards, mesh=mesh, in_specs=in_specs, out_specs=out_specs, check_vma=False)
```

profile of v0, /device:TPU:241, one launch (start us, length us, event | category | flops | bytes accessed | tf_op | source)
XLA Modules:
  0.0 301.9 jit_solution(17473195941922005689)
XLA Ops:
  0.0 3.7 %fusion.1 = (bf16[32,128,128]{2,1,0:T(8,128)(2,1)}, bf16[32,128,128]{2,1,0:T(8,128)(2,1)}, bf16[32,128,128]{2,1,0:T(8,128)(2,1)}) fusion(bf16[128,128,128]{2,1,0:T(8,128)(2,1)} %x_ref.6), kind=kLoop, calls=%fused_computation.13 | loop fusion | bytes 6291456 | tf_op jit(solution)/shard_map/slice | solution.py:260
  11.4 4.9 %shard_map.83 = (bf16[128,32,128]{2,1,0:T(8,128)(2,1)S(1)}, f32[32,128,128]{2,1,0:T(8,128)S(1)}) custom-call(bf16[128,128,128]{2,1,0:T(8,128)(2,1)} %x_ref.6, f32[1,128]{1,0:T(1,128)S(1)} %bitcast.26, f32[1,128]{1,0:T(1,128)S(1)} %bitcast.31, bf16[256,128]{1,0:T(8,128)(2,1)S(1)} %bitcast.19, bf16[128,128]{1,0:T(8,128)(2,1)S(1)} %copy-done.8), custom_call_target="tpu_custom_call" | custom-call | flops 805306368 | bytes 4194304 | tf_op jit(solution)/shard_map/pallas_call | solution.py:102
  18.4 4.9 %shard_map.84 = (bf16[128,32,128]{2,1,0:T(8,128)(2,1)S(1)}, f32[32,128,128]{2,1,0:T(8,128)S(1)}) custom-call(bf16[128,128,128]{2,1,0:T(8,128)(2,1)} %x_ref.6, f32[1,128]{1,0:T(1,128)S(1)} %bitcast.27, f32[1,128]{1,0:T(1,128)S(1)} %bitcast.32, bf16[256,128]{1,0:T(8,128)(2,1)S(1)} %bitcast.20, bf16[128,128]{1,0:T(8,128)(2,1)S(1)} %copy-done.8), custom_call_target="tpu_custom_call" | custom-call | flops 805306368 | bytes 4194304 | tf_op jit(solution)/shard_map/pallas_call | solution.py:102
  23.3 6.6 %collective-permute-done.4 = bf16[32,128,128]{2,1,0:T(8,128)(2,1)S(1)} collective-permute-done((bf16[32,128,128]{2,1,0:T(8,128)(2,1)}, bf16[32,128,128]{2,1,0:T(8,128)(2,1)S(1)}, u32[]{:S(2)}, u32[]{:S(2)}) %collective-permute-start.4) | collective-permute-done | bytes 1048608 | tf_op jit(solution)/shard_map/ppermute | solution.py:62
  39.5 20.4 %collective-permute-start.9 = (bf16[128,32,128]{2,1,0:T(8,128)(2,1)S(1)}, bf16[128,32,128]{2,1,0:T(8,128)(2,1)}, u32[]{:S(2)}, u32[]{:S(2)}) collective-permute-start(bf16[128,32,128]{2,1,0:T(8,128)(2,1)S(1)} %get-tuple-element.28), channel_id=1, source_target_pairs={{0,15},{1,0},{2,1},{3,2},{4,3},{5,4},{6,5},{7,6},{8,7},{9,8},{10,9... | collective-permute-start | bytes 3145736 | tf_op jit(solution)/shard_map/ppermute | solution.py:62
  59.9 5.7 %shard_map.82 = (bf16[128,32,128]{2,1,0:T(8,128)(2,1)}, f32[32,128,128]{2,1,0:T(8,128)S(1)}) custom-call(bf16[128,128,128]{2,1,0:T(8,128)(2,1)} %x_ref.6, f32[1,128]{1,0:T(1,128)S(1)} %bitcast.28, f32[1,128]{1,0:T(1,128)S(1)} %bitcast.33, bf16[256,128]{1,0:T(8,128)(2,1)S(1)} %bitcast.21, bf16[128,128]{1,0:T(8,128)(2,1)S(1)} %copy-done.8), custom_call_target="tpu_custom_call" | custom-call | flops 805306368 | bytes 4194304 | tf_op jit(solution)/shard_map/pallas_call | solution.py:102
  68.4 28.3 %collective-permute-done.7 = bf16[16,128,128]{2,1,0:T(8,128)(2,1)} collective-permute-done((bf16[16,128,128]{2,1,0:T(8,128)(2,1)}, bf16[16,128,128]{2,1,0:T(8,128)(2,1)}, u32[]{:S(2)}, u32[]{:S(2)}) %collective-permute-start.7) | collective-permute-done | bytes 524320 | tf_op jit(solution)/shard_map/ppermute | solution.py:62
  96.7 5.7 %collective-permute-done.5 = bf16[16,128,128]{2,1,0:T(8,128)(2,1)} collective-permute-done((bf16[16,128,128]{2,1,0:T(8,128)(2,1)}, bf16[16,128,128]{2,1,0:T(8,128)(2,1)}, u32[]{:S(2)}, u32[]{:S(2)}) %collective-permute-start.5) | collective-permute-done | bytes 524320 | tf_op jit(solution)/shard_map/ppermute | solution.py:62
  103.8 4.9 %shard_map.85 = (bf16[128,32,128]{2,1,0:T(8,128)(2,1)S(1)}, f32[32,128,128]{2,1,0:T(8,128)S(1)}) custom-call(bf16[128,128,128]{2,1,0:T(8,128)(2,1)} %x_ref.6, f32[1,128]{1,0:T(1,128)S(1)} %bitcast.29, f32[1,128]{1,0:T(1,128)S(1)} %bitcast.34, bf16[256,128]{1,0:T(8,128)(2,1)S(1)} %bitcast.22, bf16[128,128]{1,0:T(8,128)(2,1)S(1)} %copy-done.8), custom_call_target="tpu_custom_call" | custom-call | flops 805306368 | bytes 4194304 | tf_op jit(solution)/shard_map/pallas_call | solution.py:102
  110.1 9.4 %collective-permute-done.8 = bf16[16,128,128]{2,1,0:T(8,128)(2,1)} collective-permute-done((bf16[16,128,128]{2,1,0:T(8,128)(2,1)S(1)}, bf16[16,128,128]{2,1,0:T(8,128)(2,1)}, u32[]{:S(2)}, u32[]{:S(2)}) %collective-permute-start.8) | collective-permute-done | bytes 524320 | tf_op jit(solution)/shard_map/ppermute | solution.py:62
  119.5 3.1 %collective-permute-start.10 = (bf16[16,128,128]{2,1,0:T(8,128)(2,1)}, bf16[16,128,128]{2,1,0:T(8,128)(2,1)}, u32[]{:S(2)}, u32[]{:S(2)}) collective-permute-start(bf16[16,128,128]{2,1,0:T(8,128)(2,1)} %collective-permute-done.8), channel_id=1, source_target_pairs={{0,16},{1,17},{2,18},{3,19},{4,20},{5,21},{6,22},{7,23},{8,24},{9,... | collective-permute-start | bytes 1572872 | tf_op jit(solution)/shard_map/ppermute | solution.py:62
  126.4 4.1 %shard_map.86.refs_8_ = bf16[64,16,384]{2,1,0:T(8,128)(2,1)S(1)} custom-call(bf16[48,128,128]{2,1,0:T(8,128)(2,1)S(1)} %pad_maximum_fusion.x_ref, f32[1,128]{1,0:T(1,128)S(1)} %bitcast.30, f32[1,128]{1,0:T(1,128)S(1)} %bitcast.35, bf16[128,128]{1,0:T(8,128)(2,1)S(1)} %maximum_bitcast_fusion.wt_ref), custom_call_target="tpu_custom_call" | custom-call | flops 603979776 | bytes 3145728 | tf_op jit(solution)/shard_map/pallas_call | solution.py:144
  130.5 6.4 %collective-permute-start.13 = (bf16[64,16,384]{2,1,0:T(8,128)(2,1)S(1)}, bf16[64,16,384]{2,1,0:T(8,128)(2,1)S(1)}, u32[]{:S(2)}, u32[]{:S(2)}) collective-permute-start(bf16[64,16,384]{2,1,0:T(8,128)(2,1)S(1)} %shard_map.86.refs_8_), channel_id=1, source_target_pairs={{0,96},{1,97},{2,98},{3,99},{4,100},{5,101},{6,102},{7,103},{8,104... | collective-permute-start | bytes 2359304 | tf_op jit(solution)/shard_map/ppermute | solution.py:62
  138.2 12.0 %collective-permute-done.14 = bf16[128,32,128]{2,1,0:T(8,128)(2,1)} collective-permute-done((bf16[128,32,128]{2,1,0:T(8,128)(2,1)S(1)}, bf16[128,32,128]{2,1,0:T(8,128)(2,1)}, u32[]{:S(2)}, u32[]{:S(2)}) %collective-permute-start.14) | collective-permute-done | bytes 1048608 | tf_op jit(solution)/shard_map/ppermute | solution.py:62
  150.2 3.4 %collective-permute-done.13.refs_14_ = bf16[64,16,384]{2,1,0:T(8,128)(2,1)S(1)} collective-permute-done((bf16[64,16,384]{2,1,0:T(8,128)(2,1)S(1)}, bf16[64,16,384]{2,1,0:T(8,128)(2,1)S(1)}, u32[]{:S(2)}, u32[]{:S(2)}) %collective-permute-start.13) | collective-permute-done | bytes 786464 | tf_op jit(solution)/shard_map/ppermute | solution.py:62
  154.5 37.4 %collective-permute-done.11.refs_16_ = bf16[64,16,384]{2,1,0:T(8,128)(2,1)S(1)} collective-permute-done((bf16[64,16,384]{2,1,0:T(8,128)(2,1)S(1)}, bf16[64,16,384]{2,1,0:T(8,128)(2,1)S(1)}, u32[]{:S(2)}, u32[]{:S(2)}) %collective-permute-start.11) | collective-permute-done | bytes 786464 | tf_op jit(solution)/shard_map/ppermute | solution.py:62
  191.9 3.7 %collective-permute-start.18 = (bf16[64,16,384]{2,1,0:T(8,128)(2,1)S(1)}, bf16[64,16,384]{2,1,0:T(8,128)(2,1)S(1)}, u32[]{:S(2)}, u32[]{:S(2)}) collective-permute-start(bf16[64,16,384]{2,1,0:T(8,128)(2,1)S(1)} %shard_map.86.refs_8_), channel_id=1, source_target_pairs={{0,64},{1,65},{2,66},{3,67},{4,68},{5,69},{6,70},{7,71},{8,72},{9,... | collective-permute-start | bytes 2359304 | tf_op jit(solution)/shard_map/ppermute | solution.py:62
  200.0 13.1 %collective-permute-done.18.refs_12_ = bf16[64,16,384]{2,1,0:T(8,128)(2,1)S(1)} collective-permute-done((bf16[64,16,384]{2,1,0:T(8,128)(2,1)S(1)}, bf16[64,16,384]{2,1,0:T(8,128)(2,1)S(1)}, u32[]{:S(2)}, u32[]{:S(2)}) %collective-permute-start.18) | collective-permute-done | bytes 786464 | tf_op jit(solution)/shard_map/ppermute | solution.py:62
  213.1 17.4 %collective-permute-done.17.refs_22_ = bf16[64,16,384]{2,1,0:T(8,128)(2,1)S(1)} collective-permute-done((bf16[64,16,384]{2,1,0:T(8,128)(2,1)S(1)}, bf16[64,16,384]{2,1,0:T(8,128)(2,1)S(1)}, u32[]{:S(2)}, u32[]{:S(2)}) %collective-permute-start.17) | collective-permute-done | bytes 786464 | tf_op jit(solution)/shard_map/ppermute | solution.py:62
  237.9 6.4 %collective-permute-done.15 = bf16[128,32,128]{2,1,0:T(8,128)(2,1)S(1)} collective-permute-done((bf16[128,32,128]{2,1,0:T(8,128)(2,1)}, bf16[128,32,128]{2,1,0:T(8,128)(2,1)S(1)}, u32[]{:S(2)}, u32[]{:S(2)}) %collective-permute-start.15) | collective-permute-done | bytes 1048608 | tf_op jit(solution)/shard_map/ppermute | solution.py:62
  244.3 2.9 collective-permute-start.26
  247.2 7.7 %collective-permute-done.27.refs_20_ = bf16[64,16,384]{2,1,0:T(8,128)(2,1)} collective-permute-done((bf16[64,16,384]{2,1,0:T(8,128)(2,1)S(1)}, bf16[64,16,384]{2,1,0:T(8,128)(2,1)}, u32[]{:S(2)}, u32[]{:S(2)}) %collective-permute-start.27) | collective-permute-done | bytes 786464 | tf_op jit(solution)/shard_map/ppermute | solution.py:62
  260.2 20.7 %shard_map.87.refs_27_ = bf16[128,128,128]{2,1,0:T(8,128)(2,1)} custom-call(s32[2]{0:T(128)} %pad_add_fusion.place_ref, bf16[2,64,32,128]{3,2,1,0:T(8,128)(2,1)} %bitcast.23, bf16[2,64,32,128]{3,2,1,0:T(8,128)(2,1)} %bitcast.13.refs_1_, bf16[2,64,32,128]{3,2,1,0:T(8,128)(2,1)} %bitcast.14.refs_2_, f32[32,128,128]{2,1,0:T(8,128)} %copy-done.1, ...), custom_call_target="tpu_custom_call" | custom-call | flops 1073741824 | bytes 27262976 | tf_op jit(solution)/shard_map/pallas_call | solution.py:229
  280.9 20.8 %shard_map.88 = bf16[128,128,128]{2,1,0:T(8,128)(2,1)} custom-call(s32[2]{0:T(128)} %pad_add_fusion.place_ref, bf16[2,64,32,128]{3,2,1,0:T(8,128)(2,1)} %bitcast.5.refs_0_, bf16[2,64,32,128]{3,2,1,0:T(8,128)(2,1)} %bitcast.6.refs_1_, bf16[2,64,32,128]{3,2,1,0:T(8,128)(2,1)} %bitcast.37, f32[32,128,128]{2,1,0:T(8,128)} %copy-done.3, ...), custom_call_target="tpu_custom_call", output_to_operand_aliasing={{}: (28, {})} | custom-call | flops 1073741824 | bytes 27262976 | tf_op jit(solution)/shard_map/pallas_call | solution.py:229
  (117 shorter events, 47.6 us)
Async XLA Ops:
  3.7 26.2 %collective-permute-start.4 = (bf16[32,128,128]{2,1,0:T(8,128)(2,1)}, bf16[32,128,128]{2,1,0:T(8,128)(2,1)S(1)}, u32[]{:S(2)}, u32[]{:S(2)}) collective-permute-start(bf16[32,128,128]{2,1,0:T(8,128)(2,1)} %get-tuple-element.49), channel_id=1, source_target_pairs={{0,32},{1,33},{2,34},{17,49},{18,50},{19,51},{34,2},{35,3},{36,4},... | collective-permute-start | bytes 3145736 | tf_op jit(solution)/shard_map/ppermute | solution.py:62
  6.6 23.3 %collective-permute-start.3 = (bf16[32,128,128]{2,1,0:T(8,128)(2,1)}, bf16[32,128,128]{2,1,0:T(8,128)(2,1)}, u32[]{:S(2)}, u32[]{:S(2)}) collective-permute-start(bf16[32,128,128]{2,1,0:T(8,128)(2,1)} %get-tuple-element.50), channel_id=1, source_target_pairs={{0,64},{1,65},{2,66},{17,81},{18,82},{19,83},{34,98},{35,99},{36,1... | collective-permute-start | bytes 3145736 | tf_op jit(solution)/shard_map/ppermute | solution.py:62
  9.0 21.9 %collective-permute-start.2 = (bf16[32,128,128]{2,1,0:T(8,128)(2,1)}, bf16[32,128,128]{2,1,0:T(8,128)(2,1)}, u32[]{:S(2)}, u32[]{:S(2)}) collective-permute-start(bf16[32,128,128]{2,1,0:T(8,128)(2,1)} %get-tuple-element.51), channel_id=1, source_target_pairs={{0,96},{1,97},{2,98},{17,113},{18,114},{19,115},{34,66},{35,67},{3... | collective-permute-start | bytes 3145736 | tf_op jit(solution)/shard_map/ppermute | solution.py:62
  17.6 49.4 %collective-permute-start = (bf16[128,32,128]{2,1,0:T(8,128)(2,1)S(1)}, bf16[128,32,128]{2,1,0:T(8,128)(2,1)}, u32[]{:S(2)}, u32[]{:S(2)}) collective-permute-start(bf16[128,32,128]{2,1,0:T(8,128)(2,1)S(1)} %get-tuple-element.26), channel_id=1, source_target_pairs={{0,15},{1,0},{2,1},{3,2},{4,3},{5,4},{6,5},{7,6},{8,7},{9,8},{10,9... | collective-permute-start | bytes 3145736 | tf_op jit(solution)/shard_map/ppermute | solution.py:62
  35.2 61.4 %collective-permute-start.7 = (bf16[16,128,128]{2,1,0:T(8,128)(2,1)}, bf16[16,128,128]{2,1,0:T(8,128)(2,1)}, u32[]{:S(2)}, u32[]{:S(2)}) collective-permute-start(bf16[16,128,128]{2,1,0:T(8,128)(2,1)} %slice.39), channel_id=1, source_target_pairs={{2,130},{4,132},{6,134},{8,136},{19,147},{21,149},{23,151},{25,153... | collective-permute-start | bytes 1572872 | tf_op jit(solution)/shard_map/ppermute | solution.py:62
  37.4 65.0 %collective-permute-start.5 = (bf16[16,128,128]{2,1,0:T(8,128)(2,1)}, bf16[16,128,128]{2,1,0:T(8,128)(2,1)}, u32[]{:S(2)}, u32[]{:S(2)}) collective-permute-start(bf16[16,128,128]{2,1,0:T(8,128)(2,1)} %slice.37), channel_id=1, source_target_pairs={{0,128},{1,129},{2,130},{3,131},{4,132},{5,133},{6,134},{7,135},{1... | collective-permute-start | bytes 1572872 | tf_op jit(solution)/shard_map/ppermute | solution.py:62
  39.5 70.6 %collective-permute-start.9 = (bf16[128,32,128]{2,1,0:T(8,128)(2,1)S(1)}, bf16[128,32,128]{2,1,0:T(8,128)(2,1)}, u32[]{:S(2)}, u32[]{:S(2)}) collective-permute-start(bf16[128,32,128]{2,1,0:T(8,128)(2,1)S(1)} %get-tuple-element.28), channel_id=1, source_target_pairs={{0,15},{1,0},{2,1},{3,2},{4,3},{5,4},{6,5},{7,6},{8,7},{9,8},{10,9... | collective-permute-start | bytes 3145736 | tf_op jit(solution)/shard_map/ppermute | solution.py:62
  67.0 52.5 %collective-permute-start.1 = (bf16[128,32,128]{2,1,0:T(8,128)(2,1)}, bf16[128,32,128]{2,1,0:T(8,128)(2,1)}, u32[]{:S(2)}, u32[]{:S(2)}) collective-permute-start(bf16[128,32,128]{2,1,0:T(8,128)(2,1)} %get-tuple-element.27), channel_id=1, source_target_pairs={{0,15},{1,0},{2,1},{3,2},{4,3},{5,4},{6,5},{7,6},{8,7},{9,8},{10,9... | collective-permute-start | bytes 3145736 | tf_op jit(solution)/shard_map/ppermute | solution.py:62
  103.6 15.9 %collective-permute-start.8 = (bf16[16,128,128]{2,1,0:T(8,128)(2,1)S(1)}, bf16[16,128,128]{2,1,0:T(8,128)(2,1)}, u32[]{:S(2)}, u32[]{:S(2)}) collective-permute-start(bf16[16,128,128]{2,1,0:T(8,128)(2,1)S(1)} %get-tuple-element.45), channel_id=1, source_target_pairs={{0,14},{1,16},{2,0},{3,18},{4,2},{5,20},{6,4},{7,22},{8,6},{9,24},... | collective-permute-start | bytes 1572872 | tf_op jit(solution)/shard_map/ppermute | solution.py:62
  122.9 27.3 %collective-permute-start.14 = (bf16[128,32,128]{2,1,0:T(8,128)(2,1)S(1)}, bf16[128,32,128]{2,1,0:T(8,128)(2,1)}, u32[]{:S(2)}, u32[]{:S(2)}) collective-permute-start(bf16[128,32,128]{2,1,0:T(8,128)(2,1)S(1)} %get-tuple-element.31), channel_id=1, source_target_pairs={{0,15},{1,0},{2,1},{3,2},{4,3},{5,4},{6,5},{7,6},{8,7},{9,8},{10,9... | collective-permute-start | bytes 3145736 | tf_op jit(solution)/shard_map/ppermute | solution.py:62
  130.5 23.0 %collective-permute-start.13 = (bf16[64,16,384]{2,1,0:T(8,128)(2,1)S(1)}, bf16[64,16,384]{2,1,0:T(8,128)(2,1)S(1)}, u32[]{:S(2)}, u32[]{:S(2)}) collective-permute-start(bf16[64,16,384]{2,1,0:T(8,128)(2,1)S(1)} %shard_map.86.refs_8_), channel_id=1, source_target_pairs={{0,96},{1,97},{2,98},{3,99},{4,100},{5,101},{6,102},{7,103},{8,104... | collective-permute-start | bytes 2359304 | tf_op jit(solution)/shard_map/ppermute | solution.py:62
  136.9 17.5 %collective-permute-start.12 = (bf16[64,16,384]{2,1,0:T(8,128)(2,1)S(1)}, bf16[64,16,384]{2,1,0:T(8,128)(2,1)S(1)}, u32[]{:S(2)}, u32[]{:S(2)}) collective-permute-start(bf16[64,16,384]{2,1,0:T(8,128)(2,1)S(1)} %shard_map.86.refs_8_), channel_id=1, source_target_pairs={{0,32},{1,33},{2,34},{3,35},{4,36},{5,37},{6,38},{7,39},{8,40},{9,... | collective-permute-start | bytes 2359304 | tf_op jit(solution)/shard_map/ppermute | solution.py:62
  136.9 54.9 %collective-permute-start.11 = (bf16[64,16,384]{2,1,0:T(8,128)(2,1)S(1)}, bf16[64,16,384]{2,1,0:T(8,128)(2,1)S(1)}, u32[]{:S(2)}, u32[]{:S(2)}) collective-permute-start(bf16[64,16,384]{2,1,0:T(8,128)(2,1)S(1)} %shard_map.86.refs_8_), channel_id=1, source_target_pairs={{0,128},{1,129},{2,130},{3,131},{4,132},{5,133},{6,134},{7,135},{8... | collective-permute-start | bytes 2359304 | tf_op jit(solution)/shard_map/ppermute | solution.py:62
  137.0 62.0 %collective-permute-start.19 = (bf16[128,32,128]{2,1,0:T(8,128)(2,1)}, bf16[128,32,128]{2,1,0:T(8,128)(2,1)}, u32[]{:S(2)}, u32[]{:S(2)}) collective-permute-start(bf16[128,32,128]{2,1,0:T(8,128)(2,1)} %collective-permute-done), channel_id=1, source_target_pairs={{0,15},{1,0},{2,1},{3,2},{4,3},{5,4},{6,5},{7,6},{8,7},{9,8},{10,9... | collective-permute-start | bytes 3145736 | tf_op jit(solution)/shard_map/ppermute | solution.py:62
  191.9 21.2 %collective-permute-start.18 = (bf16[64,16,384]{2,1,0:T(8,128)(2,1)S(1)}, bf16[64,16,384]{2,1,0:T(8,128)(2,1)S(1)}, u32[]{:S(2)}, u32[]{:S(2)}) collective-permute-start(bf16[64,16,384]{2,1,0:T(8,128)(2,1)S(1)} %shard_map.86.refs_8_), channel_id=1, source_target_pairs={{0,64},{1,65},{2,66},{3,67},{4,68},{5,69},{6,70},{7,71},{8,72},{9,... | collective-permute-start | bytes 2359304 | tf_op jit(solution)/shard_map/ppermute | solution.py:62
  195.6 38.9 %collective-permute-start.30 = (bf16[128,32,128]{2,1,0:T(8,128)(2,1)}, bf16[128,32,128]{2,1,0:T(8,128)(2,1)S(1)}, u32[]{:S(2)}, u32[]{:S(2)}) collective-permute-start(bf16[128,32,128]{2,1,0:T(8,128)(2,1)} %collective-permute-done.9), channel_id=1, source_target_pairs={{0,15},{1,0},{2,1},{3,2},{4,3},{5,4},{6,5},{7,6},{8,7},{9,8},{10,9... | collective-permute-start | bytes 3145736 | tf_op jit(solution)/shard_map/ppermute | solution.py:62
  195.6 35.0 %collective-permute-start.17 = (bf16[64,16,384]{2,1,0:T(8,128)(2,1)S(1)}, bf16[64,16,384]{2,1,0:T(8,128)(2,1)S(1)}, u32[]{:S(2)}, u32[]{:S(2)}) collective-permute-start(bf16[64,16,384]{2,1,0:T(8,128)(2,1)S(1)} %collective-permute-done.11.refs_16_), channel_id=1, source_target_pairs={{0,96},{1,97},{2,98},{3,99},{4,100},{5,101},{6,102},{7,103},{8,104... | collective-permute-start | bytes 2359304 | tf_op jit(solution)/shard_map/ppermute | solution.py:62
  197.3 35.8 %collective-permute-start.16 = (bf16[64,16,384]{2,1,0:T(8,128)(2,1)S(1)}, bf16[64,16,384]{2,1,0:T(8,128)(2,1)}, u32[]{:S(2)}, u32[]{:S(2)}) collective-permute-start(bf16[64,16,384]{2,1,0:T(8,128)(2,1)S(1)} %collective-permute-done.11.refs_16_), channel_id=1, source_target_pairs={{0,32},{1,33},{2,34},{3,35},{4,36},{5,37},{6,38},{7,39},{8,40},{9,... | collective-permute-start | bytes 2359304 | tf_op jit(solution)/shard_map/ppermute | solution.py:62
  199.0 35.5 %collective-permute-start.21 = (bf16[64,16,384]{2,1,0:T(8,128)(2,1)S(1)}, bf16[64,16,384]{2,1,0:T(8,128)(2,1)S(1)}, u32[]{:S(2)}, u32[]{:S(2)}) collective-permute-start(bf16[64,16,384]{2,1,0:T(8,128)(2,1)S(1)} %shard_map.86.refs_8_), channel_id=1, source_target_pairs={{0,16},{1,17},{2,18},{3,19},{4,20},{5,21},{6,22},{7,23},{8,24},{9,... | collective-permute-start | bytes 2359304 | tf_op jit(solution)/shard_map/ppermute | solution.py:62
  213.1 31.2 %collective-permute-start.15 = (bf16[128,32,128]{2,1,0:T(8,128)(2,1)}, bf16[128,32,128]{2,1,0:T(8,128)(2,1)S(1)}, u32[]{:S(2)}, u32[]{:S(2)}) collective-permute-start(bf16[128,32,128]{2,1,0:T(8,128)(2,1)} %collective-permute-done.1), channel_id=1, source_target_pairs={{0,15},{1,0},{2,1},{3,2},{4,3},{5,4},{6,5},{7,6},{8,7},{9,8},{10,9... | collective-permute-start | bytes 3145736 | tf_op jit(solution)/shard_map/ppermute | solution.py:62
  234.6 20.3 %collective-permute-start.27 = (bf16[64,16,384]{2,1,0:T(8,128)(2,1)S(1)}, bf16[64,16,384]{2,1,0:T(8,128)(2,1)}, u32[]{:S(2)}, u32[]{:S(2)}) collective-permute-start(bf16[64,16,384]{2,1,0:T(8,128)(2,1)S(1)} %collective-permute-done.11.refs_16_), channel_id=1, source_target_pairs={{0,64},{1,65},{2,66},{3,67},{4,68},{5,69},{6,70},{7,71},{8,72},{9,... | collective-permute-start | bytes 2359304 | tf_op jit(solution)/shard_map/ppermute | solution.py:62
  234.6 46.3 %collective-permute-start.20 = (bf16[128,32,128]{2,1,0:T(8,128)(2,1)}, bf16[128,32,128]{2,1,0:T(8,128)(2,1)}, u32[]{:S(2)}, u32[]{:S(2)}) collective-permute-start(bf16[128,32,128]{2,1,0:T(8,128)(2,1)} %collective-permute-done.14), channel_id=1, source_target_pairs={{0,15},{1,0},{2,1},{3,2},{4,3},{5,4},{6,5},{7,6},{8,7},{9,8},{10,9... | collective-permute-start | bytes 3145736 | tf_op jit(solution)/shard_map/ppermute | solution.py:62
  236.4 20.7 %collective-permute-start.23 = (bf16[64,16,384]{2,1,0:T(8,128)(2,1)S(1)}, bf16[64,16,384]{2,1,0:T(8,128)(2,1)}, u32[]{:S(2)}, u32[]{:S(2)}) collective-permute-start(bf16[64,16,384]{2,1,0:T(8,128)(2,1)S(1)} %collective-permute-done.18.refs_12_), channel_id=1, source_target_pairs={{0,16},{1,17},{2,18},{3,19},{4,20},{5,21},{6,22},{7,23},{8,24},{9,... | collective-permute-start | bytes 2359304 | tf_op jit(solution)/shard_map/ppermute | solution.py:62
  237.5 19.6 %collective-permute-start.29 = (bf16[64,16,384]{2,1,0:T(8,128)(2,1)S(1)}, bf16[64,16,384]{2,1,0:T(8,128)(2,1)}, u32[]{:S(2)}, u32[]{:S(2)}) collective-permute-start(bf16[64,16,384]{2,1,0:T(8,128)(2,1)S(1)} %collective-permute-done.17.refs_22_), channel_id=1, source_target_pairs={{0,16},{1,17},{2,18},{3,19},{4,20},{5,21},{6,22},{7,23},{8,24},{9,... | collective-permute-start | bytes 2359304 | tf_op jit(solution)/shard_map/ppermute | solution.py:62
  (35 other events, 982.9 us)
where the time goes:
time: 303 us; the launch traced here: 302 us
  waiting for transfers between devices  154 us (51%)
  Pallas kernels  66 us (22%)
  starting transfers between devices  63.3 us (21%)
  local copies, waits for them, and re-layouts  12.4 us (4%)
  other arithmetic  5.88 us (2%)
    ppermute x31, waiting for transfers between devices, send(): return lax.ppermute(value, AXES, pairs)  154 us
    ppermute x31, starting transfers between devices, send(): return lax.ppermute(value, AXES, pairs)  63.3 us
    pallas_call x2, Pallas kernels, final(): pl.pallas_call(functools.partial(final_kernel, subs=subs, aliased=len(ali...  41.5 us
    pallas_call x4, Pallas kernels, left_and_gate(): pl.pallas_call(left_kernel, out_shape=[jax.ShapeDtypeStruct((128, rows, 1...  20.4 us
  transfers between devices with their start and end apart: 31, of which 16 were waited for; matrix products, arithmetic and copies ran while one was open for 3% of the time, Pallas kernels for 15%

commit v1 on v0

--- a/solution.py
+++ b/solution.py
@@ -12,7 +12,7 @@
 NT = (((1,), (1,)), ((), ()))
 TN = (((0,), (0,)), ((), ()))
 AXES = ("row", "col")
-ROWS = 32
+BIG, SMALL = (0, 80), (80, 48)
 
 
 def place(r, c):
@@ -251,17 +251,16 @@
 
     wt_left = w_proj[:, :256].T
 
-    def left_of(q, source):
-        return left_and_gate(source, ROWS * q, ROWS, gain, bias, wt_left, w_gate)
+    def left_of(part, source):
+        return left_and_gate(source, *part, gain, bias, wt_left, w_gate)
 
     def one_back(value):
         return send(value, everyone(back))
 
     quarters = [pair[:32]] + [send(pair[32 * a : 32 * a + 32], scatter_pairs(a)) for a in (1, 2, 3)]
-    lefts = [left_of(q, pair) for q in range(3)]
-    once = [one_back(lefts[0][0]), one_back(lefts[1][0])]
-    once.append(one_back(after(lefts[2][0], once[0])))
-    quarters[1] = after(quarters[1], lefts[1][0])
+    big, big_gate = left_of(BIG, pair)
+    big_once = one_back(big)
+    quarters[1] = after(quarters[1], big)
     even = core == col % 2
     y, x_side = chip % 4, chip // 4
 
@@ -282,10 +281,10 @@
     moving = jnp.where(even, two, one)
     shifted = send(moving, shift_pairs())
     swapped_one = send(one, everyone(swap))
-    lefts.append(left_of(3, after(pair, moving)))
-    once.append(one_back(lefts[3][0]))
-    shifted = after(shifted, once[1], once[2], swapped_one, lefts[3][0])
-    twice = [one_back(after(once[0], shifted))]
+    small, small_gate = left_of(SMALL, after(pair, moving))
+    small_once = one_back(small)
+    shifted = after(shifted, big_once, swapped_one, small)
+    big_twice = one_back(after(big_once, shifted))
     swapped = send(shifted, everyone(swap))
     first, swapped_first = one, swapped_one
     raw = jnp.concatenate(
@@ -305,25 +304,23 @@
 
     for n in (4, 1, 3):
         got[n] = exchange(mine, n)
-    twice.append(one_back(after(once[1], mine)))
-    stage = after(got[4], got[1], got[3], once[3])
+    stage = after(got[4], got[1], got[3], small_once)
     got[5], got[7] = exchange(stage, 1), exchange(stage, 3)
     got[2] = exchange(after(mine, stage), 2)
-    twice.append(one_back(after(once[2], stage)))
-    stage = after(got[4], got[5], got[7], got[2], twice[0])
+    small_twice = one_back(after(small_once, stage))
+    stage = after(got[4], got[5], got[7], got[2])
     got[6] = exchange(stage, 2)
-    twice.append(one_back(after(once[3], stage)))
     rights = []
     for n in range(8):
-        rights += [got[n], send(got[n], everyone(swap))]
+        given = after(got[6], big_twice) if n == 6 else got[n]
+        rights += [got[n], send(given, everyone(swap))]
 
     where = jnp.stack([chip ^ (col // 2), core]).astype(jnp.int32)
     out_g = jnp.broadcast_to(out_gain[:, None], (128, 128))
     out_b = jnp.broadcast_to(out_bias[:, None], (128, 128))
 
-    groups = [(lefts[q][0], once[q], twice[q], lefts[q][1]) for q in range(4)]
-    update = final(after(where, twice[2]), groups[:2], rights, out_g, out_b, w_out, None, 0)
-    return final(where, groups[2:], rights, out_g, out_b, w_out, update, 1)
+    groups = [(big, big_once, big_twice, big_gate), (small, small_once, small_twice, small_gate)]
+    return final(where, groups, rights, out_g, out_b, w_out, None, 0)
 
 
 def solution(mesh):

time: 303 us -> 355 us (1.17)
  the two profiles are of different devices: /device:TPU:241 before, /device:TPU:8 now
where the time goes in v1:
time: 355 us
  starting transfers between devices  166 us (47%)
  waiting for transfers between devices  115 us (32%)
  Pallas kernels  52.2 us (15%)
  local copies, waits for them, and re-layouts  14.5 us (4%)
  other arithmetic  5.95 us (2%)
    ppermute x27, starting transfers between devices, send(): return lax.ppermute(value, AXES, pairs)  166 us
    ppermute x27, waiting for transfers between devices, send(): return lax.ppermute(value, AXES, pairs)  115 us
    pallas_call x1, Pallas kernels, final(): pl.pallas_call(functools.partial(final_kernel, subs=subs, aliased=len(ali...  29.6 us
    pallas_call x2, Pallas kernels, left_and_gate(): pl.pallas_call(left_kernel, out_shape=[jax.ShapeDtypeStruct((128, rows, 1...  18.5 us
    unnamed x49, local copies, waits for them, and re-layouts  7.47 us
  transfers between devices with their start and end apart: 27, of which 10 were waited for; matrix products, arithmetic and copies ran while one was open for 2% of the time, Pallas kernels for 6%

profile of v1, /device:TPU:8, one launch (start us, length us, event | category | flops | bytes accessed | tf_op | source)
XLA Modules:
  0.0 354.9 jit_solution(11564939808339826887)
XLA Ops:
  0.0 3.7 %fusion.1 = (bf16[32,128,128]{2,1,0:T(8,128)(2,1)}, bf16[32,128,128]{2,1,0:T(8,128)(2,1)}, bf16[32,128,128]{2,1,0:T(8,128)(2,1)}) fusion(bf16[128,128,128]{2,1,0:T(8,128)(2,1)} %x_ref.2), kind=kLoop, calls=%fused_computation.13 | loop fusion | bytes 6291456 | tf_op jit(solution)/shard_map/slice | solution.py:260
  6.7 1.7 collective-permute-start.1
  8.5 11.7 %shard_map.82 = (bf16[128,80,128]{2,1,0:T(8,128)(2,1)S(1)}, f32[80,128,128]{2,1,0:T(8,128)}) custom-call(bf16[128,128,128]{2,1,0:T(8,128)(2,1)} %x_ref.2, f32[1,128]{1,0:T(1,128)S(1)} %bitcast.17, f32[1,128]{1,0:T(1,128)S(1)} %bitcast.20, bf16[256,128]{1,0:T(8,128)(2,1)S(1)} %bitcast.15, bf16[128,128]{1,0:T(8,128)(2,1)S(1)} %copy-done.6), custom_call_target="tpu_custom_call" | custom-call | flops 2013265920 | bytes 10485760 | tf_op jit(solution)/shard_map/pallas_call | solution.py:102
  20.2 7.2 %collective-permute-start = (bf16[128,80,128]{2,1,0:T(8,128)(2,1)S(1)}, bf16[128,80,128]{2,1,0:T(8,128)(2,1)}, u32[]{:S(2)}, u32[]{:S(2)}) collective-permute-start(bf16[128,80,128]{2,1,0:T(8,128)(2,1)S(1)} %get-tuple-element.18), channel_id=1, source_target_pairs={{0,15},{1,0},{2,1},{3,2},{4,3},{5,4},{6,5},{7,6},{8,7},{9,8},{10,9... | collective-permute-start | bytes 7864328 | tf_op jit(solution)/shard_map/ppermute | solution.py:62
  27.3 2.5 select_select_fusion
  33.9 32.7 %collective-permute-start.5 = (bf16[16,128,128]{2,1,0:T(8,128)(2,1)}, bf16[16,128,128]{2,1,0:T(8,128)(2,1)}, u32[]{:S(2)}, u32[]{:S(2)}) collective-permute-start(bf16[16,128,128]{2,1,0:T(8,128)(2,1)} %slice.39), channel_id=1, source_target_pairs={{0,128},{1,129},{2,130},{3,131},{4,132},{5,133},{6,134},{7,135},{1... | collective-permute-start | bytes 1572872 | tf_op jit(solution)/shard_map/ppermute | solution.py:62
  66.6 9.2 %collective-permute-done.4 = bf16[16,128,128]{2,1,0:T(8,128)(2,1)S(1)} collective-permute-done((bf16[16,128,128]{2,1,0:T(8,128)(2,1)}, bf16[16,128,128]{2,1,0:T(8,128)(2,1)S(1)}, u32[]{:S(2)}, u32[]{:S(2)}) %collective-permute-start.4) | collective-permute-done | bytes 524320 | tf_op jit(solution)/shard_map/ppermute | solution.py:62
  78.2 5.6 %collective-permute-start.6 = (bf16[16,128,128]{2,1,0:T(8,128)(2,1)S(1)}, bf16[16,128,128]{2,1,0:T(8,128)(2,1)}, u32[]{:S(2)}, u32[]{:S(2)}) collective-permute-start(bf16[16,128,128]{2,1,0:T(8,128)(2,1)S(1)} %get-tuple-element.31), channel_id=1, source_target_pairs={{0,14},{1,16},{2,0},{3,18},{4,2},{5,20},{6,4},{7,22},{8,6},{9,24},... | collective-permute-start | bytes 1572872 | tf_op jit(solution)/shard_map/ppermute | solution.py:62
  83.8 18.5 %collective-permute-start.7 = (bf16[16,128,128]{2,1,0:T(8,128)(2,1)S(1)}, bf16[16,128,128]{2,1,0:T(8,128)(2,1)S(1)}, u32[]{:S(2)}, u32[]{:S(2)}) collective-permute-start(bf16[16,128,128]{2,1,0:T(8,128)(2,1)S(1)} %get-tuple-element.32), channel_id=1, source_target_pairs={{0,16},{1,17},{2,18},{3,19},{4,20},{5,21},{6,22},{7,23},{8,24},{9,... | collective-permute-start | bytes 1572872 | tf_op jit(solution)/shard_map/ppermute | solution.py:62
  102.2 6.8 %shard_map.83 = (bf16[128,48,128]{2,1,0:T(8,128)(2,1)S(1)}, f32[48,128,128]{2,1,0:T(8,128)S(1)}) custom-call(bf16[128,128,128]{2,1,0:T(8,128)(2,1)} %x_ref.2, f32[1,128]{1,0:T(1,128)S(1)} %bitcast.18, f32[1,128]{1,0:T(1,128)S(1)} %bitcast.21, bf16[256,128]{1,0:T(8,128)(2,1)S(1)} %bitcast.16, bf16[128,128]{1,0:T(8,128)(2,1)S(1)} %copy-done.6), custom_call_target="tpu_custom_call" | custom-call | flops 1207959552 | bytes 6291456 | tf_op jit(solution)/shard_map/pallas_call | solution.py:102
  113.0 6.8 %collective-permute-start.9 = (bf16[128,48,128]{2,1,0:T(8,128)(2,1)}, bf16[128,48,128]{2,1,0:T(8,128)(2,1)}, u32[]{:S(2)}, u32[]{:S(2)}) collective-permute-start(bf16[128,48,128]{2,1,0:T(8,128)(2,1)} %copy-done.3), channel_id=1, source_target_pairs={{0,15},{1,0},{2,1},{3,2},{4,3},{5,4},{6,5},{7,6},{8,7},{9,8},{10,9... | collective-permute-start | bytes 4718600 | tf_op jit(solution)/shard_map/ppermute | solution.py:62
  122.4 4.1 %shard_map.84.refs_8_ = bf16[64,16,384]{2,1,0:T(8,128)(2,1)S(1)} custom-call(bf16[48,128,128]{2,1,0:T(8,128)(2,1)S(1)} %pad_maximum_fusion.x_ref, f32[1,128]{1,0:T(1,128)S(1)} %bitcast.19, f32[1,128]{1,0:T(1,128)S(1)} %bitcast.22, bf16[128,128]{1,0:T(8,128)(2,1)S(1)} %maximum_bitcast_fusion.wt_ref), custom_call_target="tpu_custom_call" | custom-call | flops 603979776 | bytes 3145728 | tf_op jit(solution)/shard_map/pallas_call | solution.py:144
  128.1 1.9 collective-permute-start.12
  130.1 24.9 %collective-permute-done.9 = bf16[128,48,128]{2,1,0:T(8,128)(2,1)} collective-permute-done((bf16[128,48,128]{2,1,0:T(8,128)(2,1)}, bf16[128,48,128]{2,1,0:T(8,128)(2,1)}, u32[]{:S(2)}, u32[]{:S(2)}) %collective-permute-start.9) | collective-permute-done | bytes 1572896 | tf_op jit(solution)/shard_map/ppermute | solution.py:62
  155.1 2.6 collective-permute-start.17
  157.7 2.4 collective-permute-start.21
  160.1 17.4 %collective-permute-done.17.refs_12_ = bf16[64,16,384]{2,1,0:T(8,128)(2,1)} collective-permute-done((bf16[64,16,384]{2,1,0:T(8,128)(2,1)S(1)}, bf16[64,16,384]{2,1,0:T(8,128)(2,1)}, u32[]{:S(2)}, u32[]{:S(2)}) %collective-permute-start.17) | collective-permute-done | bytes 786464 | tf_op jit(solution)/shard_map/ppermute | solution.py:62
  177.5 15.6 %collective-permute-done.23.refs_22_ = bf16[64,16,384]{2,1,0:T(8,128)(2,1)} collective-permute-done((bf16[64,16,384]{2,1,0:T(8,128)(2,1)S(1)}, bf16[64,16,384]{2,1,0:T(8,128)(2,1)}, u32[]{:S(2)}, u32[]{:S(2)}) %collective-permute-start.23) | collective-permute-done | bytes 786464 | tf_op jit(solution)/shard_map/ppermute | solution.py:62
  193.2 2.1 collective-permute-start.24
  195.8 15.1 %collective-permute-done.8 = bf16[128,80,128]{2,1,0:T(8,128)(2,1)S(1)} collective-permute-done((bf16[128,80,128]{2,1,0:T(8,128)(2,1)}, bf16[128,80,128]{2,1,0:T(8,128)(2,1)S(1)}, u32[]{:S(2)}, u32[]{:S(2)}) %collective-permute-start.8) | collective-permute-done | bytes 2621472 | tf_op jit(solution)/shard_map/ppermute | solution.py:62
  211.0 3.1 collective-permute-done.24.refs_20_
  214.1 76.3 %collective-permute-start.14 = (bf16[128,48,128]{2,1,0:T(8,128)(2,1)}, bf16[128,48,128]{2,1,0:T(8,128)(2,1)S(1)}, u32[]{:S(2)}, u32[]{:S(2)}) collective-permute-start(bf16[128,48,128]{2,1,0:T(8,128)(2,1)} %collective-permute-done.9), channel_id=1, source_target_pairs={{0,15},{1,0},{2,1},{3,2},{4,3},{5,4},{6,5},{7,6},{8,7},{9,8},{10,9... | collective-permute-start | bytes 4718600 | tf_op jit(solution)/shard_map/ppermute | solution.py:62
  295.4 28.2 %collective-permute-done.14 = bf16[128,48,128]{2,1,0:T(8,128)(2,1)S(1)} collective-permute-done((bf16[128,48,128]{2,1,0:T(8,128)(2,1)}, bf16[128,48,128]{2,1,0:T(8,128)(2,1)S(1)}, u32[]{:S(2)}, u32[]{:S(2)}) %collective-permute-start.14) | collective-permute-done | bytes 1572896 | tf_op jit(solution)/shard_map/ppermute | solution.py:62
  325.1 29.6 %shard_map.85 = bf16[128,128,128]{2,1,0:T(8,128)(2,1)} custom-call(s32[2]{0:T(128)} %pad_add_fusion.place_ref, bf16[2,64,80,128]{3,2,1,0:T(8,128)(2,1)} %bitcast.13, bf16[2,64,80,128]{3,2,1,0:T(8,128)(2,1)} %bitcast.6.refs_1_, bf16[2,64,80,128]{3,2,1,0:T(8,128)(2,1)} %bitcast.23, f32[80,128,128]{2,1,0:T(8,128)} %get-tuple-element.24.refs_3_, ...), custom_call_target="tpu_custom_call" | custom-call | flops 2147483648 | bytes 39845888 | tf_op jit(solution)/shard_map/pallas_call | solution.py:229
  (98 shorter events, 24.8 us)
Async XLA Ops:
  3.7 23.6 %collective-permute-start.3 = (bf16[32,128,128]{2,1,0:T(8,128)(2,1)}, bf16[32,128,128]{2,1,0:T(8,128)(2,1)}, u32[]{:S(2)}, u32[]{:S(2)}) collective-permute-start(bf16[32,128,128]{2,1,0:T(8,128)(2,1)} %get-tuple-element.35), channel_id=1, source_target_pairs={{0,32},{1,33},{2,34},{17,49},{18,50},{19,51},{34,2},{35,3},{36,4},... | collective-permute-start | bytes 3145736 | tf_op jit(solution)/shard_map/ppermute | solution.py:62
  5.0 22.3 %collective-permute-start.2 = (bf16[32,128,128]{2,1,0:T(8,128)(2,1)}, bf16[32,128,128]{2,1,0:T(8,128)(2,1)}, u32[]{:S(2)}, u32[]{:S(2)}) collective-permute-start(bf16[32,128,128]{2,1,0:T(8,128)(2,1)} %get-tuple-element.36), channel_id=1, source_target_pairs={{0,64},{1,65},{2,66},{17,81},{18,82},{19,83},{34,98},{35,99},{36,1... | collective-permute-start | bytes 3145736 | tf_op jit(solution)/shard_map/ppermute | solution.py:62
  6.7 20.7 %collective-permute-start.1 = (bf16[32,128,128]{2,1,0:T(8,128)(2,1)}, bf16[32,128,128]{2,1,0:T(8,128)(2,1)}, u32[]{:S(2)}, u32[]{:S(2)}) collective-permute-start(bf16[32,128,128]{2,1,0:T(8,128)(2,1)} %get-tuple-element.37), channel_id=1, source_target_pairs={{0,96},{1,97},{2,98},{17,113},{18,114},{19,115},{34,66},{35,67},{3... | collective-permute-start | bytes 3145736 | tf_op jit(solution)/shard_map/ppermute | solution.py:62
  20.2 91.8 %collective-permute-start = (bf16[128,80,128]{2,1,0:T(8,128)(2,1)S(1)}, bf16[128,80,128]{2,1,0:T(8,128)(2,1)}, u32[]{:S(2)}, u32[]{:S(2)}) collective-permute-start(bf16[128,80,128]{2,1,0:T(8,128)(2,1)S(1)} %get-tuple-element.18), channel_id=1, source_target_pairs={{0,15},{1,0},{2,1},{3,2},{4,3},{5,4},{6,5},{7,6},{8,7},{9,8},{10,9... | collective-permute-start | bytes 7864328 | tf_op jit(solution)/shard_map/ppermute | solution.py:62
  32.6 43.2 %collective-permute-start.4 = (bf16[16,128,128]{2,1,0:T(8,128)(2,1)}, bf16[16,128,128]{2,1,0:T(8,128)(2,1)S(1)}, u32[]{:S(2)}, u32[]{:S(2)}) collective-permute-start(bf16[16,128,128]{2,1,0:T(8,128)(2,1)} %slice.37), channel_id=1, source_target_pairs={{2,130},{4,132},{6,134},{8,136},{19,147},{21,149},{23,151},{25,153... | collective-permute-start | bytes 1572872 | tf_op jit(solution)/shard_map/ppermute | solution.py:62
  33.9 42.8 %collective-permute-start.5 = (bf16[16,128,128]{2,1,0:T(8,128)(2,1)}, bf16[16,128,128]{2,1,0:T(8,128)(2,1)}, u32[]{:S(2)}, u32[]{:S(2)}) collective-permute-start(bf16[16,128,128]{2,1,0:T(8,128)(2,1)} %slice.39), channel_id=1, source_target_pairs={{0,128},{1,129},{2,130},{3,131},{4,132},{5,133},{6,134},{7,135},{1... | collective-permute-start | bytes 1572872 | tf_op jit(solution)/shard_map/ppermute | solution.py:62
  78.2 33.7 %collective-permute-start.6 = (bf16[16,128,128]{2,1,0:T(8,128)(2,1)S(1)}, bf16[16,128,128]{2,1,0:T(8,128)(2,1)}, u32[]{:S(2)}, u32[]{:S(2)}) collective-permute-start(bf16[16,128,128]{2,1,0:T(8,128)(2,1)S(1)} %get-tuple-element.31), channel_id=1, source_target_pairs={{0,14},{1,16},{2,0},{3,18},{4,2},{5,20},{6,4},{7,22},{8,6},{9,24},... | collective-permute-start | bytes 1572872 | tf_op jit(solution)/shard_map/ppermute | solution.py:62
  83.8 28.2 %collective-permute-start.7 = (bf16[16,128,128]{2,1,0:T(8,128)(2,1)S(1)}, bf16[16,128,128]{2,1,0:T(8,128)(2,1)S(1)}, u32[]{:S(2)}, u32[]{:S(2)}) collective-permute-start(bf16[16,128,128]{2,1,0:T(8,128)(2,1)S(1)} %get-tuple-element.32), channel_id=1, source_target_pairs={{0,16},{1,17},{2,18},{3,19},{4,20},{5,21},{6,22},{7,23},{8,24},{9,... | collective-permute-start | bytes 1572872 | tf_op jit(solution)/shard_map/ppermute | solution.py:62
  112.7 8.3 %collective-permute-start.10 = (bf16[16,128,128]{2,1,0:T(8,128)(2,1)}, bf16[16,128,128]{2,1,0:T(8,128)(2,1)S(1)}, u32[]{:S(2)}, u32[]{:S(2)}) collective-permute-start(bf16[16,128,128]{2,1,0:T(8,128)(2,1)} %collective-permute-done.6), channel_id=1, source_target_pairs={{0,16},{1,17},{2,18},{3,19},{4,20},{5,21},{6,22},{7,23},{8,24},{9,... | collective-permute-start | bytes 1572872 | tf_op jit(solution)/shard_map/ppermute | solution.py:62
  113.0 42.1 %collective-permute-start.9 = (bf16[128,48,128]{2,1,0:T(8,128)(2,1)}, bf16[128,48,128]{2,1,0:T(8,128)(2,1)}, u32[]{:S(2)}, u32[]{:S(2)}) collective-permute-start(bf16[128,48,128]{2,1,0:T(8,128)(2,1)} %copy-done.3), channel_id=1, source_target_pairs={{0,15},{1,0},{2,1},{3,2},{4,3},{5,4},{6,5},{7,6},{8,7},{9,8},{10,9... | collective-permute-start | bytes 4718600 | tf_op jit(solution)/shard_map/ppermute | solution.py:62
  119.9 91.1 %collective-permute-start.8 = (bf16[128,80,128]{2,1,0:T(8,128)(2,1)}, bf16[128,80,128]{2,1,0:T(8,128)(2,1)S(1)}, u32[]{:S(2)}, u32[]{:S(2)}) collective-permute-start(bf16[128,80,128]{2,1,0:T(8,128)(2,1)} %collective-permute-done), channel_id=1, source_target_pairs={{0,15},{1,0},{2,1},{3,2},{4,3},{5,4},{6,5},{7,6},{8,7},{9,8},{10,9... | collective-permute-start | bytes 7864328 | tf_op jit(solution)/shard_map/ppermute | solution.py:62
  126.5 28.6 %collective-permute-start.13 = (bf16[64,16,384]{2,1,0:T(8,128)(2,1)S(1)}, bf16[64,16,384]{2,1,0:T(8,128)(2,1)S(1)}, u32[]{:S(2)}, u32[]{:S(2)}) collective-permute-start(bf16[64,16,384]{2,1,0:T(8,128)(2,1)S(1)} %shard_map.84.refs_8_), channel_id=1, source_target_pairs={{0,96},{1,97},{2,98},{3,99},{4,100},{5,101},{6,102},{7,103},{8,104... | collective-permute-start | bytes 2359304 | tf_op jit(solution)/shard_map/ppermute | solution.py:62
  128.1 27.0 %collective-permute-start.12 = (bf16[64,16,384]{2,1,0:T(8,128)(2,1)S(1)}, bf16[64,16,384]{2,1,0:T(8,128)(2,1)S(1)}, u32[]{:S(2)}, u32[]{:S(2)}) collective-permute-start(bf16[64,16,384]{2,1,0:T(8,128)(2,1)S(1)} %shard_map.84.refs_8_), channel_id=1, source_target_pairs={{0,32},{1,33},{2,34},{3,35},{4,36},{5,37},{6,38},{7,39},{8,40},{9,... | collective-permute-start | bytes 2359304 | tf_op jit(solution)/shard_map/ppermute | solution.py:62
  130.0 25.1 %collective-permute-start.11 = (bf16[64,16,384]{2,1,0:T(8,128)(2,1)S(1)}, bf16[64,16,384]{2,1,0:T(8,128)(2,1)S(1)}, u32[]{:S(2)}, u32[]{:S(2)}) collective-permute-start(bf16[64,16,384]{2,1,0:T(8,128)(2,1)S(1)} %shard_map.84.refs_8_), channel_id=1, source_target_pairs={{0,128},{1,129},{2,130},{3,131},{4,132},{5,133},{6,134},{7,135},{8... | collective-permute-start | bytes 2359304 | tf_op jit(solution)/shard_map/ppermute | solution.py:62
  155.1 22.4 %collective-permute-start.17 = (bf16[64,16,384]{2,1,0:T(8,128)(2,1)S(1)}, bf16[64,16,384]{2,1,0:T(8,128)(2,1)}, u32[]{:S(2)}, u32[]{:S(2)}) collective-permute-start(bf16[64,16,384]{2,1,0:T(8,128)(2,1)S(1)} %shard_map.84.refs_8_), channel_id=1, source_target_pairs={{0,64},{1,65},{2,66},{3,67},{4,68},{5,69},{6,70},{7,71},{8,72},{9,... | collective-permute-start | bytes 2359304 | tf_op jit(solution)/shard_map/ppermute | solution.py:62
  157.7 35.4 %collective-permute-start.23 = (bf16[64,16,384]{2,1,0:T(8,128)(2,1)S(1)}, bf16[64,16,384]{2,1,0:T(8,128)(2,1)}, u32[]{:S(2)}, u32[]{:S(2)}) collective-permute-start(bf16[64,16,384]{2,1,0:T(8,128)(2,1)S(1)} %collective-permute-done.11.refs_16_), channel_id=1, source_target_pairs={{0,96},{1,97},{2,98},{3,99},{4,100},{5,101},{6,102},{7,103},{8,104... | collective-permute-start | bytes 2359304 | tf_op jit(solution)/shard_map/ppermute | solution.py:62
  157.7 35.5 %collective-permute-start.21 = (bf16[64,16,384]{2,1,0:T(8,128)(2,1)S(1)}, bf16[64,16,384]{2,1,0:T(8,128)(2,1)}, u32[]{:S(2)}, u32[]{:S(2)}) collective-permute-start(bf16[64,16,384]{2,1,0:T(8,128)(2,1)S(1)} %collective-permute-done.11.refs_16_), channel_id=1, source_target_pairs={{0,32},{1,33},{2,34},{3,35},{4,36},{5,37},{6,38},{7,39},{8,40},{9,... | collective-permute-start | bytes 2359304 | tf_op jit(solution)/shard_map/ppermute | solution.py:62
  193.2 20.9 %collective-permute-start.24 = (bf16[64,16,384]{2,1,0:T(8,128)(2,1)S(1)}, bf16[64,16,384]{2,1,0:T(8,128)(2,1)}, u32[]{:S(2)}, u32[]{:S(2)}) collective-permute-start(bf16[64,16,384]{2,1,0:T(8,128)(2,1)S(1)} %collective-permute-done.11.refs_16_), channel_id=1, source_target_pairs={{0,64},{1,65},{2,66},{3,67},{4,68},{5,69},{6,70},{7,71},{8,72},{9,... | collective-permute-start | bytes 2359304 | tf_op jit(solution)/shard_map/ppermute | solution.py:62
  195.3 95.1 %collective-permute-start.15 = (bf16[64,16,384]{2,1,0:T(8,128)(2,1)S(1)}, bf16[64,16,384]{2,1,0:T(8,128)(2,1)S(1)}, u32[]{:S(2)}, u32[]{:S(2)}) collective-permute-start(bf16[64,16,384]{2,1,0:T(8,128)(2,1)S(1)} %shard_map.84.refs_8_), channel_id=1, source_target_pairs={{0,16},{1,17},{2,18},{3,19},{4,20},{5,21},{6,22},{7,23},{8,24},{9,... | collective-permute-start | bytes 2359304 | tf_op jit(solution)/shard_map/ppermute | solution.py:62
  195.3 95.2 %collective-permute-start.19 = (bf16[64,16,384]{2,1,0:T(8,128)(2,1)S(1)}, bf16[64,16,384]{2,1,0:T(8,128)(2,1)S(1)}, u32[]{:S(2)}, u32[]{:S(2)}) collective-permute-start(bf16[64,16,384]{2,1,0:T(8,128)(2,1)S(1)} %collective-permute-done.13.refs_14_), channel_id=1, source_target_pairs={{0,16},{1,17},{2,18},{3,19},{4,20},{5,21},{6,22},{7,23},{8,24},{9,... | collective-permute-start | bytes 2359304 | tf_op jit(solution)/shard_map/ppermute | solution.py:62
  195.8 95.3 %collective-permute-start.16 = (bf16[64,16,384]{2,1,0:T(8,128)(2,1)S(1)}, bf16[64,16,384]{2,1,0:T(8,128)(2,1)S(1)}, u32[]{:S(2)}, u32[]{:S(2)}) collective-permute-start(bf16[64,16,384]{2,1,0:T(8,128)(2,1)S(1)} %collective-permute-done.12.refs_10_), channel_id=1, source_target_pairs={{0,16},{1,17},{2,18},{3,19},{4,20},{5,21},{6,22},{7,23},{8,24},{9,... | collective-permute-start | bytes 2359304 | tf_op jit(solution)/shard_map/ppermute | solution.py:62
  211.0 80.3 %collective-permute-start.20 = (bf16[64,16,384]{2,1,0:T(8,128)(2,1)S(1)}, bf16[64,16,384]{2,1,0:T(8,128)(2,1)S(1)}, u32[]{:S(2)}, u32[]{:S(2)}) collective-permute-start(bf16[64,16,384]{2,1,0:T(8,128)(2,1)S(1)} %collective-permute-done.11.refs_16_), channel_id=1, source_target_pairs={{0,16},{1,17},{2,18},{3,19},{4,20},{5,21},{6,22},{7,23},{8,24},{9,... | collective-permute-start | bytes 2359304 | tf_op jit(solution)/shard_map/ppermute | solution.py:62
  214.1 109.4 %collective-permute-start.14 = (bf16[128,48,128]{2,1,0:T(8,128)(2,1)}, bf16[128,48,128]{2,1,0:T(8,128)(2,1)S(1)}, u32[]{:S(2)}, u32[]{:S(2)}) collective-permute-start(bf16[128,48,128]{2,1,0:T(8,128)(2,1)} %collective-permute-done.9), channel_id=1, source_target_pairs={{0,15},{1,0},{2,1},{3,2},{4,3},{5,4},{6,5},{7,6},{8,7},{9,8},{10,9... | collective-permute-start | bytes 4718600 | tf_op jit(solution)/shard_map/ppermute | solution.py:62
  292.9 30.7 %collective-permute-start.25 = (bf16[64,16,384]{2,1,0:T(8,128)(2,1)}, bf16[64,16,384]{2,1,0:T(8,128)(2,1)}, u32[]{:S(2)}, u32[]{:S(2)}) collective-permute-start(bf16[64,16,384]{2,1,0:T(8,128)(2,1)} %collective-permute-done.24.refs_20_), channel_id=1, source_target_pairs={{0,16},{1,17},{2,18},{3,19},{4,20},{5,21},{6,22},{7,23},{8,24},{9,... | collective-permute-start | bytes 2359304 | tf_op jit(solution)/shard_map/ppermute | solution.py:62
  (27 other events, 1225.1 us)

commit v2 on v1

--- a/solution.py
+++ b/solution.py
@@ -84,10 +84,10 @@
     p = lax.dot_general(wt_ref[...], n, NT, preferred_element_type=F32)
     v = sigmoid(p[:128]) * p[128:]
     for i in range(16):
-        scratch[i * 128 : (i + 1) * 128, :] = v[:, i * 128 : (i + 1) * 128]
+        scratch[i * 136 : i * 136 + 128, :] = v[:, i * 128 : (i + 1) * 128]
 
     def turn(h, _):
-        left_ref[h] = scratch[pl.ds(h, 16, stride=128), :].astype(BF16)
+        left_ref[h] = scratch[pl.ds(h, 16, stride=136), :].astype(BF16)
         return 0
 
     lax.fori_loop(0, 128, turn, 0, unroll=16)
@@ -117,7 +117,7 @@
             pl.BlockSpec((128, 16, 128), lambda i: (0, i, 0)),
             pl.BlockSpec((16, 128, 128), lambda i: (i, 0, 0)),
         ],
-        scratch_shapes=[pltpu.VMEM((16 * 128, 128), F32)],
+        scratch_shapes=[pltpu.VMEM((16 * 136, 128), F32)],
         compiler_params=pltpu.CompilerParams(vmem_limit_bytes=48 << 20),
         cost_estimate=pl.CostEstimate(
             flops=rows * 128 * 128 * 2 * 768, bytes_accessed=rows * 128 * 128 * 8, transcendentals=rows * 128 * 256
@@ -131,10 +131,10 @@
     p = lax.dot_general(wt_ref[...], n, NT, preferred_element_type=F32)
     v = sigmoid(p[:64]) * p[64:]
     for j in range(16):
-        scratch[j * 64 : (j + 1) * 64, :] = v[:, j * 128 : (j + 1) * 128]
+        scratch[j * 72 : j * 72 + 64, :] = v[:, j * 128 : (j + 1) * 128]
 
     def turn(h, _):
-        right_ref[h] = scratch[pl.ds(h, 16, stride=64), :].astype(BF16)
+        right_ref[h] = scratch[pl.ds(h, 16, stride=72), :].astype(BF16)
         return 0
 
     lax.fori_loop(0, 64, turn, 0, unroll=16)
@@ -147,7 +147,7 @@
         grid=(3,),
         in_specs=[pl.BlockSpec((16, 128, 128), lambda d: (d, 0, 0)), whole(gain), whole(bias), whole(wt)],
         out_specs=pl.BlockSpec((64, 16, 128), lambda d: (0, 0, d)),
-        scratch_shapes=[pltpu.VMEM((16 * 64, 128), F32)],
+        scratch_shapes=[pltpu.VMEM((16 * 72, 128), F32)],
         compiler_params=pltpu.CompilerParams(vmem_limit_bytes=32 << 20),
         cost_estimate=pl.CostEstimate(flops=48 * 128 * 128 * 2 * 384, bytes_accessed=3 << 20, transcendentals=48 * 128 * 64),
     )(pieces, gain, bias, wt)
@@ -175,7 +175,7 @@
             )
             right = jnp.concatenate([rights[2 * n + half][t] for n in range(8)], axis=0)
             h = which * 64 + step * STEP + t
-            scratch[pl.ds(pl.multiple_of(h * rows, rows), rows), :] = lax.dot_general(
+            scratch[pl.ds(h * (rows + 1), rows), :] = lax.dot_general(
                 left, right, NT, preferred_element_type=F32
             )
 
@@ -186,8 +186,8 @@
 
             def some_rows(q, _, base=base, gate_ref=gate_ref):
                 parts = []
-                for e in range(8):
-                    x = scratch[pl.ds(base + q * 8 + e, 128, stride=rows), :]
+                for e in range(16):
+                    x = scratch[pl.ds(base + q * 16 + e, 128, stride=rows + 1), :]
                     centred = x - jnp.mean(x, axis=0, keepdims=True)
                     variance = jnp.mean(centred * centred, axis=0, keepdims=True)
                     parts.append(
@@ -195,15 +195,15 @@
                     )
                 y = jnp.concatenate(parts, axis=1)
                 out = lax.dot_general(y, w_ref[...], TN, preferred_element_type=F32)
-                for e in range(8):
+                for e in range(16):
                     for n in range(8):
                         chip = block ^ n
                         at = pl.ds(pl.multiple_of(chip % 4 * 32 + chip // 4 * 16, 16), 16)
                         mine = out[e * 128 + n * 16 : e * 128 + n * 16 + 16]
-                        out_ref[base + q * 8 + e, at, :] = (gate_ref[q * 8 + e, at, :] * mine).astype(BF16)
+                        out_ref[base + q * 16 + e, at, :] = (gate_ref[q * 16 + e, at, :] * mine).astype(BF16)
                 return 0
 
-            lax.fori_loop(0, sub // 8, some_rows, 0)
+            lax.fori_loop(0, sub // 16, some_rows, 0)
             base += sub
 
 
@@ -234,7 +234,7 @@
             grid=(64 // STEP,),
             in_specs=specs,
             out_specs=pl.BlockSpec((rows, 128, 128), lambda s, _: (block, 0, 0)),
-            scratch_shapes=[pltpu.VMEM((128 * rows, 128), F32)],
+            scratch_shapes=[pltpu.VMEM((128 * (rows + 1), 128), F32)],
         ),
         input_output_aliases=aliases,
         compiler_params=pltpu.CompilerParams(vmem_limit_bytes=56 << 20),
@@ -260,7 +260,8 @@
     quarters = [pair[:32]] + [send(pair[32 * a : 32 * a + 32], scatter_pairs(a)) for a in (1, 2, 3)]
     big, big_gate = left_of(BIG, pair)
     big_once = one_back(big)
-    quarters[1] = after(quarters[1], big)
+    small, small_gate = left_of(SMALL, pair)
+    quarters[1] = after(quarters[1], big, small)
     even = core == col % 2
     y, x_side = chip % 4, chip // 4
 
@@ -281,10 +282,8 @@
     moving = jnp.where(even, two, one)
     shifted = send(moving, shift_pairs())
     swapped_one = send(one, everyone(swap))
-    small, small_gate = left_of(SMALL, after(pair, moving))
-    small_once = one_back(small)
+    small_once = one_back(after(small, swapped_one))
     shifted = after(shifted, big_once, swapped_one, small)
-    big_twice = one_back(after(big_once, shifted))
     swapped = send(shifted, everyone(swap))
     first, swapped_first = one, swapped_one
     raw = jnp.concatenate(
@@ -302,18 +301,19 @@
     def exchange(value, n):
         return send(value, everyone(lambda r, c: (r ^ (2 * n), c)))
 
+    swapped_mine = send(mine, everyone(swap))
     for n in (4, 1, 3):
         got[n] = exchange(mine, n)
+    small_twice = one_back(after(small_once, swapped_mine))
     stage = after(got[4], got[1], got[3], small_once)
     got[5], got[7] = exchange(stage, 1), exchange(stage, 3)
     got[2] = exchange(after(mine, stage), 2)
-    small_twice = one_back(after(small_once, stage))
-    stage = after(got[4], got[5], got[7], got[2])
+    big_twice = one_back(after(big_once, stage))
+    stage = after(got[4], got[5], got[7], got[2], small_twice)
     got[6] = exchange(stage, 2)
-    rights = []
-    for n in range(8):
-        given = after(got[6], big_twice) if n == 6 else got[n]
-        rights += [got[n], send(given, everyone(swap))]
+    rights = [mine, swapped_mine]
+    for n in range(1, 8):
+        rights += [got[n], send(got[n], everyone(swap))]
 
     where = jnp.stack([chip ^ (col // 2), core]).astype(jnp.int32)
     out_g = jnp.broadcast_to(out_gain[:, None], (128, 128))

time: 355 us -> 294 us (0.83)
  waiting for transfers between devices: 115 us -> 88.8 us
  starting transfers between devices: 166 us -> 147 us
  Pallas kernels: 52.2 us -> 40.4 us
  local copies, waits for them, and re-layouts: 14.5 us -> 8.5 us
    ppermute x27, waiting for transfers between devices: 115 us -> 88.8 us  [send(): return lax.ppermute(value, AXES, pairs)]
    ppermute x27, starting transfers between devices: 166 us -> 147 us  [send(): return lax.ppermute(value, AXES, pairs)]
    pallas_call x1, Pallas kernels: 29.6 us -> 22 us  [final(): pl.pallas_call(functools.partial(final_kernel, subs=subs, aliased=len(ali...]
    unnamed x49 -> x47, local copies, waits for them, and re-layouts: 7.47 us -> 2.41 us
  transfers between devices with their start and end apart: 27 -> 27, of which waited for: 10 -> 8; matrix products, arithmetic and copies ran while one was open for 2% -> 3% of each run, Pallas kernels for 6% -> 6%
where the time goes in v2:
time: 294 us; the launch traced here: 292 us
  starting transfers between devices  147 us (50%)
  waiting for transfers between devices  88.8 us (30%)
  Pallas kernels  40.4 us (14%)
  local copies, waits for them, and re-layouts  8.5 us (3%)
  other arithmetic  7.64 us (3%)
    ppermute x27, starting transfers between devices, send(): return lax.ppermute(value, AXES, pairs)  147 us
    ppermute x27, waiting for transfers between devices, send(): return lax.ppermute(value, AXES, pairs)  88.8 us
    pallas_call x1, Pallas kernels, final(): pl.pallas_call(functools.partial(final_kernel, subs=subs, aliased=len(ali...  22 us
    pallas_call x2, Pallas kernels, left_and_gate(): pl.pallas_call(left_kernel, out_shape=[jax.ShapeDtypeStruct((128, rows, 1...  15 us
  transfers between devices with their start and end apart: 27, of which 8 were waited for; matrix products, arithmetic and copies ran while one was open for 3% of the time, Pallas kernels for 6%

profile of v2, /device:TPU:8, one launch (start us, length us, event | category | flops | bytes accessed | tf_op | source)
XLA Modules:
  0.0 292.4 jit_solution(15992805086356939668)
XLA Ops:
  0.0 3.7 %fusion.1 = (bf16[32,128,128]{2,1,0:T(8,128)(2,1)}, bf16[32,128,128]{2,1,0:T(8,128)(2,1)}, bf16[32,128,128]{2,1,0:T(8,128)(2,1)}) fusion(bf16[128,128,128]{2,1,0:T(8,128)(2,1)} %x_ref.3), kind=kLoop, calls=%fused_computation.13 | loop fusion | bytes 6291456 | tf_op jit(solution)/shard_map/slice | solution.py:260
  8.5 9.5 %shard_map.82 = (bf16[128,80,128]{2,1,0:T(8,128)(2,1)S(1)}, f32[80,128,128]{2,1,0:T(8,128)}) custom-call(bf16[128,128,128]{2,1,0:T(8,128)(2,1)} %x_ref.3, f32[1,128]{1,0:T(1,128)S(1)} %bitcast.17, f32[1,128]{1,0:T(1,128)S(1)} %bitcast.20, bf16[256,128]{1,0:T(8,128)(2,1)S(1)} %bitcast.15, bf16[128,128]{1,0:T(8,128)(2,1)S(1)} %copy-done.6), custom_call_target="tpu_custom_call" | custom-call | flops 2013265920 | bytes 10485760 | tf_op jit(solution)/shard_map/pallas_call | solution.py:102
  18.0 7.1 %collective-permute-start = (bf16[128,80,128]{2,1,0:T(8,128)(2,1)S(1)}, bf16[128,80,128]{2,1,0:T(8,128)(2,1)}, u32[]{:S(2)}, u32[]{:S(2)}) collective-permute-start(bf16[128,80,128]{2,1,0:T(8,128)(2,1)S(1)} %get-tuple-element.17), channel_id=1, source_target_pairs={{0,15},{1,0},{2,1},{3,2},{4,3},{5,4},{6,5},{7,6},{8,7},{9,8},{10,9... | collective-permute-start | bytes 7864328 | tf_op jit(solution)/shard_map/ppermute | solution.py:62
  25.1 5.5 %shard_map.83 = (bf16[128,48,128]{2,1,0:T(8,128)(2,1)S(1)}, f32[48,128,128]{2,1,0:T(8,128)S(1)}) custom-call(bf16[128,128,128]{2,1,0:T(8,128)(2,1)} %x_ref.3, f32[1,128]{1,0:T(1,128)S(1)} %bitcast.18, f32[1,128]{1,0:T(1,128)S(1)} %bitcast.21, bf16[256,128]{1,0:T(8,128)(2,1)S(1)} %bitcast.16, bf16[128,128]{1,0:T(8,128)(2,1)S(1)} %copy-done.6), custom_call_target="tpu_custom_call" | custom-call | flops 1207959552 | bytes 6291456 | tf_op jit(solution)/shard_map/pallas_call | solution.py:102
  30.6 4.2 %select_select_fusion.1 = (bf16[32,128,128]{2,1,0:T(8,128)(2,1)S(1)}, bf16[32,128,128]{2,1,0:T(8,128)(2,1)S(1)}) fusion(bf16[32,128,128]{2,1,0:T(8,128)(2,1)} %collective-permute-done.1, bf16[32,128,128]{2,1,0:T(8,128)(2,1)} %collective-permute-done.2, bf16[32,128,128]{2,1,0:T(8,128)(2,1)} %collective-permute-done.3, pred[]{:T(512)S(6)} %eq.55, pred[]{:T(512)S(6)} %eq.54, ...), kind=kLoop, calls=%fused_computation.2 | loop fusion | flops 5242880 | bytes 6291466 | tf_op jit(solution)/shard_map/jit(_where)/select_n | solution.py:275
  38.3 28.6 %collective-permute-start.4 = (bf16[16,128,128]{2,1,0:T(8,128)(2,1)S(1)}, bf16[16,128,128]{2,1,0:T(8,128)(2,1)}, u32[]{:S(2)}, u32[]{:S(2)}) collective-permute-start(bf16[16,128,128]{2,1,0:T(8,128)(2,1)S(1)} %slice.37), channel_id=1, source_target_pairs={{0,128},{1,129},{2,130},{3,131},{4,132},{5,133},{6,134},{7,135},{1... | collective-permute-start | bytes 1572872 | tf_op jit(solution)/shard_map/ppermute | solution.py:62
  66.9 9.1 %collective-permute-done.6 = bf16[16,128,128]{2,1,0:T(8,128)(2,1)} collective-permute-done((bf16[16,128,128]{2,1,0:T(8,128)(2,1)}, bf16[16,128,128]{2,1,0:T(8,128)(2,1)}, u32[]{:S(2)}, u32[]{:S(2)}) %collective-permute-start.6) | collective-permute-done | bytes 524320 | tf_op jit(solution)/shard_map/ppermute | solution.py:62
  77.4 5.8 %collective-permute-start.7 = (bf16[16,128,128]{2,1,0:T(8,128)(2,1)S(1)}, bf16[16,128,128]{2,1,0:T(8,128)(2,1)}, u32[]{:S(2)}, u32[]{:S(2)}) collective-permute-start(bf16[16,128,128]{2,1,0:T(8,128)(2,1)S(1)} %get-tuple-element.29), channel_id=1, source_target_pairs={{0,14},{1,16},{2,0},{3,18},{4,2},{5,20},{6,4},{7,22},{8,6},{9,24},... | collective-permute-start | bytes 1572872 | tf_op jit(solution)/shard_map/ppermute | solution.py:62
  83.2 16.8 %collective-permute-start.5 = (bf16[16,128,128]{2,1,0:T(8,128)(2,1)S(1)}, bf16[16,128,128]{2,1,0:T(8,128)(2,1)S(1)}, u32[]{:S(2)}, u32[]{:S(2)}) collective-permute-start(bf16[16,128,128]{2,1,0:T(8,128)(2,1)S(1)} %get-tuple-element.30), channel_id=1, source_target_pairs={{0,16},{1,17},{2,18},{3,19},{4,20},{5,21},{6,22},{7,23},{8,24},{9,... | collective-permute-start | bytes 1572872 | tf_op jit(solution)/shard_map/ppermute | solution.py:62
  102.3 4.6 %collective-permute-start.8 = (bf16[16,128,128]{2,1,0:T(8,128)(2,1)}, bf16[16,128,128]{2,1,0:T(8,128)(2,1)S(1)}, u32[]{:S(2)}, u32[]{:S(2)}) collective-permute-start(bf16[16,128,128]{2,1,0:T(8,128)(2,1)} %collective-permute-done.7), channel_id=1, source_target_pairs={{0,16},{1,17},{2,18},{3,19},{4,20},{5,21},{6,22},{7,23},{8,24},{9,... | collective-permute-start | bytes 1572872 | tf_op jit(solution)/shard_map/ppermute | solution.py:62
  107.2 10.3 %collective-permute-start.12 = (bf16[128,48,128]{2,1,0:T(8,128)(2,1)}, bf16[128,48,128]{2,1,0:T(8,128)(2,1)S(1)}, u32[]{:S(2)}, u32[]{:S(2)}) collective-permute-start(bf16[128,48,128]{2,1,0:T(8,128)(2,1)} %copy-done.3), channel_id=1, source_target_pairs={{0,15},{1,0},{2,1},{3,2},{4,3},{5,4},{6,5},{7,6},{8,7},{9,8},{10,9... | collective-permute-start | bytes 4718600 | tf_op jit(solution)/shard_map/ppermute | solution.py:62
  118.9 3.4 %shard_map.84.refs_8_ = bf16[64,16,384]{2,1,0:T(8,128)(2,1)S(1)} custom-call(bf16[48,128,128]{2,1,0:T(8,128)(2,1)S(1)} %pad_maximum_fusion.x_ref, f32[1,128]{1,0:T(1,128)S(1)} %bitcast.19, f32[1,128]{1,0:T(1,128)S(1)} %bitcast.22, bf16[128,128]{1,0:T(8,128)(2,1)S(1)} %maximum_bitcast_fusion.wt_ref), custom_call_target="tpu_custom_call" | custom-call | flops 603979776 | bytes 3145728 | tf_op jit(solution)/shard_map/pallas_call | solution.py:144
  124.8 1.9 collective-permute-start.10
  126.7 25.0 %collective-permute-done.12 = bf16[128,48,128]{2,1,0:T(8,128)(2,1)S(1)} collective-permute-done((bf16[128,48,128]{2,1,0:T(8,128)(2,1)}, bf16[128,48,128]{2,1,0:T(8,128)(2,1)S(1)}, u32[]{:S(2)}, u32[]{:S(2)}) %collective-permute-start.12) | collective-permute-done | bytes 1572896 | tf_op jit(solution)/shard_map/ppermute | solution.py:62
  151.7 4.6 %collective-permute-start.15 = (bf16[128,48,128]{2,1,0:T(8,128)(2,1)S(1)}, bf16[128,48,128]{2,1,0:T(8,128)(2,1)S(1)}, u32[]{:S(2)}, u32[]{:S(2)}) collective-permute-start(bf16[128,48,128]{2,1,0:T(8,128)(2,1)S(1)} %collective-permute-done.12), channel_id=1, source_target_pairs={{0,15},{1,0},{2,1},{3,2},{4,3},{5,4},{6,5},{7,6},{8,7},{9,8},{10,9... | collective-permute-start | bytes 4718600 | tf_op jit(solution)/shard_map/ppermute | solution.py:62
  156.4 50.3 %collective-permute-start.13 = (bf16[128,80,128]{2,1,0:T(8,128)(2,1)}, bf16[128,80,128]{2,1,0:T(8,128)(2,1)}, u32[]{:S(2)}, u32[]{:S(2)}) collective-permute-start(bf16[128,80,128]{2,1,0:T(8,128)(2,1)} %collective-permute-done), channel_id=1, source_target_pairs={{0,15},{1,0},{2,1},{3,2},{4,3},{5,4},{6,5},{7,6},{8,7},{9,8},{10,9... | collective-permute-start | bytes 7864328 | tf_op jit(solution)/shard_map/ppermute | solution.py:62
  206.7 2.3 collective-permute-start.17
  209.0 2.4 collective-permute-start.21
  211.4 17.4 %collective-permute-done.17.refs_12_ = bf16[64,16,384]{2,1,0:T(8,128)(2,1)} collective-permute-done((bf16[64,16,384]{2,1,0:T(8,128)(2,1)S(1)}, bf16[64,16,384]{2,1,0:T(8,128)(2,1)}, u32[]{:S(2)}, u32[]{:S(2)}) %collective-permute-start.17) | collective-permute-done | bytes 786464 | tf_op jit(solution)/shard_map/ppermute | solution.py:62
  228.8 15.5 %collective-permute-done.23.refs_22_ = bf16[64,16,384]{2,1,0:T(8,128)(2,1)} collective-permute-done((bf16[64,16,384]{2,1,0:T(8,128)(2,1)S(1)}, bf16[64,16,384]{2,1,0:T(8,128)(2,1)}, u32[]{:S(2)}, u32[]{:S(2)}) %collective-permute-start.23) | collective-permute-done | bytes 786464 | tf_op jit(solution)/shard_map/ppermute | solution.py:62
  244.8 2.4 collective-permute-start.24
  248.0 18.1 %collective-permute-done.24.refs_20_ = bf16[64,16,384]{2,1,0:T(8,128)(2,1)} collective-permute-done((bf16[64,16,384]{2,1,0:T(8,128)(2,1)S(1)}, bf16[64,16,384]{2,1,0:T(8,128)(2,1)}, u32[]{:S(2)}, u32[]{:S(2)}) %collective-permute-start.24) | collective-permute-done | bytes 786464 | tf_op jit(solution)/shard_map/ppermute | solution.py:62
  266.9 2.0 collective-permute-done.25.refs_21_
  270.3 22.0 %shard_map.85 = bf16[128,128,128]{2,1,0:T(8,128)(2,1)} custom-call(s32[2]{0:T(128)} %pad_add_fusion.place_ref, bf16[2,64,80,128]{3,2,1,0:T(8,128)(2,1)} %bitcast.13, bf16[2,64,80,128]{3,2,1,0:T(8,128)(2,1)} %bitcast.6.refs_1_, bf16[2,64,80,128]{3,2,1,0:T(8,128)(2,1)} %bitcast.8.refs_2_, f32[80,128,128]{2,1,0:T(8,128)} %get-tuple-element.24.refs_3_, ...), custom_call_target="tpu_custom_call" | custom-call | flops 2147483648 | bytes 39845888 | tf_op jit(solution)/shard_map/pallas_call | solution.py:229
  (96 shorter events, 19.5 us)
Async XLA Ops:
  3.7 26.9 %collective-permute-start.3 = (bf16[32,128,128]{2,1,0:T(8,128)(2,1)}, bf16[32,128,128]{2,1,0:T(8,128)(2,1)}, u32[]{:S(2)}, u32[]{:S(2)}) collective-permute-start(bf16[32,128,128]{2,1,0:T(8,128)(2,1)} %get-tuple-element.33), channel_id=1, source_target_pairs={{0,32},{1,33},{2,34},{17,49},{18,50},{19,51},{34,2},{35,3},{36,4},... | collective-permute-start | bytes 3145736 | tf_op jit(solution)/shard_map/ppermute | solution.py:62
  5.0 25.6 %collective-permute-start.2 = (bf16[32,128,128]{2,1,0:T(8,128)(2,1)}, bf16[32,128,128]{2,1,0:T(8,128)(2,1)}, u32[]{:S(2)}, u32[]{:S(2)}) collective-permute-start(bf16[32,128,128]{2,1,0:T(8,128)(2,1)} %get-tuple-element.34), channel_id=1, source_target_pairs={{0,64},{1,65},{2,66},{17,81},{18,82},{19,83},{34,98},{35,99},{36,1... | collective-permute-start | bytes 3145736 | tf_op jit(solution)/shard_map/ppermute | solution.py:62
  6.7 23.9 %collective-permute-start.1 = (bf16[32,128,128]{2,1,0:T(8,128)(2,1)}, bf16[32,128,128]{2,1,0:T(8,128)(2,1)}, u32[]{:S(2)}, u32[]{:S(2)}) collective-permute-start(bf16[32,128,128]{2,1,0:T(8,128)(2,1)} %get-tuple-element.35), channel_id=1, source_target_pairs={{0,96},{1,97},{2,98},{17,113},{18,114},{19,115},{34,66},{35,67},{3... | collective-permute-start | bytes 3145736 | tf_op jit(solution)/shard_map/ppermute | solution.py:62
  18.0 83.5 %collective-permute-start = (bf16[128,80,128]{2,1,0:T(8,128)(2,1)S(1)}, bf16[128,80,128]{2,1,0:T(8,128)(2,1)}, u32[]{:S(2)}, u32[]{:S(2)}) collective-permute-start(bf16[128,80,128]{2,1,0:T(8,128)(2,1)S(1)} %get-tuple-element.17), channel_id=1, source_target_pairs={{0,15},{1,0},{2,1},{3,2},{4,3},{5,4},{6,5},{7,6},{8,7},{9,8},{10,9... | collective-permute-start | bytes 7864328 | tf_op jit(solution)/shard_map/ppermute | solution.py:62
  37.0 38.9 %collective-permute-start.6 = (bf16[16,128,128]{2,1,0:T(8,128)(2,1)}, bf16[16,128,128]{2,1,0:T(8,128)(2,1)}, u32[]{:S(2)}, u32[]{:S(2)}) collective-permute-start(bf16[16,128,128]{2,1,0:T(8,128)(2,1)} %slice.39), channel_id=1, source_target_pairs={{2,130},{4,132},{6,134},{8,136},{19,147},{21,149},{23,151},{25,153... | collective-permute-start | bytes 1572872 | tf_op jit(solution)/shard_map/ppermute | solution.py:62
  38.3 37.7 %collective-permute-start.4 = (bf16[16,128,128]{2,1,0:T(8,128)(2,1)S(1)}, bf16[16,128,128]{2,1,0:T(8,128)(2,1)}, u32[]{:S(2)}, u32[]{:S(2)}) collective-permute-start(bf16[16,128,128]{2,1,0:T(8,128)(2,1)S(1)} %slice.37), channel_id=1, source_target_pairs={{0,128},{1,129},{2,130},{3,131},{4,132},{5,133},{6,134},{7,135},{1... | collective-permute-start | bytes 1572872 | tf_op jit(solution)/shard_map/ppermute | solution.py:62
  77.4 22.6 %collective-permute-start.7 = (bf16[16,128,128]{2,1,0:T(8,128)(2,1)S(1)}, bf16[16,128,128]{2,1,0:T(8,128)(2,1)}, u32[]{:S(2)}, u32[]{:S(2)}) collective-permute-start(bf16[16,128,128]{2,1,0:T(8,128)(2,1)S(1)} %get-tuple-element.29), channel_id=1, source_target_pairs={{0,14},{1,16},{2,0},{3,18},{4,2},{5,20},{6,4},{7,22},{8,6},{9,24},... | collective-permute-start | bytes 1572872 | tf_op jit(solution)/shard_map/ppermute | solution.py:62
  83.2 18.3 %collective-permute-start.5 = (bf16[16,128,128]{2,1,0:T(8,128)(2,1)S(1)}, bf16[16,128,128]{2,1,0:T(8,128)(2,1)S(1)}, u32[]{:S(2)}, u32[]{:S(2)}) collective-permute-start(bf16[16,128,128]{2,1,0:T(8,128)(2,1)S(1)} %get-tuple-element.30), channel_id=1, source_target_pairs={{0,16},{1,17},{2,18},{3,19},{4,20},{5,21},{6,22},{7,23},{8,24},{9,... | collective-permute-start | bytes 1572872 | tf_op jit(solution)/shard_map/ppermute | solution.py:62
  102.3 15.3 %collective-permute-start.8 = (bf16[16,128,128]{2,1,0:T(8,128)(2,1)}, bf16[16,128,128]{2,1,0:T(8,128)(2,1)S(1)}, u32[]{:S(2)}, u32[]{:S(2)}) collective-permute-start(bf16[16,128,128]{2,1,0:T(8,128)(2,1)} %collective-permute-done.7), channel_id=1, source_target_pairs={{0,16},{1,17},{2,18},{3,19},{4,20},{5,21},{6,22},{7,23},{8,24},{9,... | collective-permute-start | bytes 1572872 | tf_op jit(solution)/shard_map/ppermute | solution.py:62
  107.2 44.5 %collective-permute-start.12 = (bf16[128,48,128]{2,1,0:T(8,128)(2,1)}, bf16[128,48,128]{2,1,0:T(8,128)(2,1)S(1)}, u32[]{:S(2)}, u32[]{:S(2)}) collective-permute-start(bf16[128,48,128]{2,1,0:T(8,128)(2,1)} %copy-done.3), channel_id=1, source_target_pairs={{0,15},{1,0},{2,1},{3,2},{4,3},{5,4},{6,5},{7,6},{8,7},{9,8},{10,9... | collective-permute-start | bytes 4718600 | tf_op jit(solution)/shard_map/ppermute | solution.py:62
  122.4 29.3 %collective-permute-start.14 = (bf16[64,16,384]{2,1,0:T(8,128)(2,1)S(1)}, bf16[64,16,384]{2,1,0:T(8,128)(2,1)S(1)}, u32[]{:S(2)}, u32[]{:S(2)}) collective-permute-start(bf16[64,16,384]{2,1,0:T(8,128)(2,1)S(1)} %shard_map.84.refs_8_), channel_id=1, source_target_pairs={{0,16},{1,17},{2,18},{3,19},{4,20},{5,21},{6,22},{7,23},{8,24},{9,... | collective-permute-start | bytes 2359304 | tf_op jit(solution)/shard_map/ppermute | solution.py:62
  123.2 33.1 %collective-permute-start.11 = (bf16[64,16,384]{2,1,0:T(8,128)(2,1)S(1)}, bf16[64,16,384]{2,1,0:T(8,128)(2,1)S(1)}, u32[]{:S(2)}, u32[]{:S(2)}) collective-permute-start(bf16[64,16,384]{2,1,0:T(8,128)(2,1)S(1)} %shard_map.84.refs_8_), channel_id=1, source_target_pairs={{0,96},{1,97},{2,98},{3,99},{4,100},{5,101},{6,102},{7,103},{8,104... | collective-permute-start | bytes 2359304 | tf_op jit(solution)/shard_map/ppermute | solution.py:62
  124.8 31.5 %collective-permute-start.10 = (bf16[64,16,384]{2,1,0:T(8,128)(2,1)S(1)}, bf16[64,16,384]{2,1,0:T(8,128)(2,1)S(1)}, u32[]{:S(2)}, u32[]{:S(2)}) collective-permute-start(bf16[64,16,384]{2,1,0:T(8,128)(2,1)S(1)} %shard_map.84.refs_8_), channel_id=1, source_target_pairs={{0,32},{1,33},{2,34},{3,35},{4,36},{5,37},{6,38},{7,39},{8,40},{9,... | collective-permute-start | bytes 2359304 | tf_op jit(solution)/shard_map/ppermute | solution.py:62
  126.7 29.6 %collective-permute-start.9 = (bf16[64,16,384]{2,1,0:T(8,128)(2,1)S(1)}, bf16[64,16,384]{2,1,0:T(8,128)(2,1)S(1)}, u32[]{:S(2)}, u32[]{:S(2)}) collective-permute-start(bf16[64,16,384]{2,1,0:T(8,128)(2,1)S(1)} %shard_map.84.refs_8_), channel_id=1, source_target_pairs={{0,128},{1,129},{2,130},{3,131},{4,132},{5,133},{6,134},{7,135},{8... | collective-permute-start | bytes 2359304 | tf_op jit(solution)/shard_map/ppermute | solution.py:62
  151.7 93.1 %collective-permute-start.15 = (bf16[128,48,128]{2,1,0:T(8,128)(2,1)S(1)}, bf16[128,48,128]{2,1,0:T(8,128)(2,1)S(1)}, u32[]{:S(2)}, u32[]{:S(2)}) collective-permute-start(bf16[128,48,128]{2,1,0:T(8,128)(2,1)S(1)} %collective-permute-done.12), channel_id=1, source_target_pairs={{0,15},{1,0},{2,1},{3,2},{4,3},{5,4},{6,5},{7,6},{8,7},{9,8},{10,9... | collective-permute-start | bytes 4718600 | tf_op jit(solution)/shard_map/ppermute | solution.py:62
  156.4 110.5 %collective-permute-start.13 = (bf16[128,80,128]{2,1,0:T(8,128)(2,1)}, bf16[128,80,128]{2,1,0:T(8,128)(2,1)}, u32[]{:S(2)}, u32[]{:S(2)}) collective-permute-start(bf16[128,80,128]{2,1,0:T(8,128)(2,1)} %collective-permute-done), channel_id=1, source_target_pairs={{0,15},{1,0},{2,1},{3,2},{4,3},{5,4},{6,5},{7,6},{8,7},{9,8},{10,9... | collective-permute-start | bytes 7864328 | tf_op jit(solution)/shard_map/ppermute | solution.py:62
  206.7 22.1 %collective-permute-start.17 = (bf16[64,16,384]{2,1,0:T(8,128)(2,1)S(1)}, bf16[64,16,384]{2,1,0:T(8,128)(2,1)}, u32[]{:S(2)}, u32[]{:S(2)}) collective-permute-start(bf16[64,16,384]{2,1,0:T(8,128)(2,1)S(1)} %shard_map.84.refs_8_), channel_id=1, source_target_pairs={{0,64},{1,65},{2,66},{3,67},{4,68},{5,69},{6,70},{7,71},{8,72},{9,... | collective-permute-start | bytes 2359304 | tf_op jit(solution)/shard_map/ppermute | solution.py:62
  209.0 35.3 %collective-permute-start.23 = (bf16[64,16,384]{2,1,0:T(8,128)(2,1)S(1)}, bf16[64,16,384]{2,1,0:T(8,128)(2,1)}, u32[]{:S(2)}, u32[]{:S(2)}) collective-permute-start(bf16[64,16,384]{2,1,0:T(8,128)(2,1)S(1)} %collective-permute-done.9.refs_16_), channel_id=1, source_target_pairs={{0,96},{1,97},{2,98},{3,99},{4,100},{5,101},{6,102},{7,103},{8,104... | collective-permute-start | bytes 2359304 | tf_op jit(solution)/shard_map/ppermute | solution.py:62
  209.0 35.5 %collective-permute-start.21 = (bf16[64,16,384]{2,1,0:T(8,128)(2,1)S(1)}, bf16[64,16,384]{2,1,0:T(8,128)(2,1)}, u32[]{:S(2)}, u32[]{:S(2)}) collective-permute-start(bf16[64,16,384]{2,1,0:T(8,128)(2,1)S(1)} %collective-permute-done.9.refs_16_), channel_id=1, source_target_pairs={{0,32},{1,33},{2,34},{3,35},{4,36},{5,37},{6,38},{7,39},{8,40},{9,... | collective-permute-start | bytes 2359304 | tf_op jit(solution)/shard_map/ppermute | solution.py:62
  228.8 18.4 %collective-permute-start.19 = (bf16[64,16,384]{2,1,0:T(8,128)(2,1)S(1)}, bf16[64,16,384]{2,1,0:T(8,128)(2,1)S(1)}, u32[]{:S(2)}, u32[]{:S(2)}) collective-permute-start(bf16[64,16,384]{2,1,0:T(8,128)(2,1)S(1)} %collective-permute-done.11.refs_14_), channel_id=1, source_target_pairs={{0,16},{1,17},{2,18},{3,19},{4,20},{5,21},{6,22},{7,23},{8,24},{9,... | collective-permute-start | bytes 2359304 | tf_op jit(solution)/shard_map/ppermute | solution.py:62
  244.8 21.3 %collective-permute-start.24 = (bf16[64,16,384]{2,1,0:T(8,128)(2,1)S(1)}, bf16[64,16,384]{2,1,0:T(8,128)(2,1)}, u32[]{:S(2)}, u32[]{:S(2)}) collective-permute-start(bf16[64,16,384]{2,1,0:T(8,128)(2,1)S(1)} %collective-permute-done.9.refs_16_), channel_id=1, source_target_pairs={{0,64},{1,65},{2,66},{3,67},{4,68},{5,69},{6,70},{7,71},{8,72},{9,... | collective-permute-start | bytes 2359304 | tf_op jit(solution)/shard_map/ppermute | solution.py:62
  247.2 19.6 %collective-permute-start.18 = (bf16[64,16,384]{2,1,0:T(8,128)(2,1)}, bf16[64,16,384]{2,1,0:T(8,128)(2,1)}, u32[]{:S(2)}, u32[]{:S(2)}) collective-permute-start(bf16[64,16,384]{2,1,0:T(8,128)(2,1)} %collective-permute-done.17.refs_12_), channel_id=1, source_target_pairs={{0,16},{1,17},{2,18},{3,19},{4,20},{5,21},{6,22},{7,23},{8,24},{9,... | collective-permute-start | bytes 2359304 | tf_op jit(solution)/shard_map/ppermute | solution.py:62
  247.4 19.5 %collective-permute-start.26 = (bf16[64,16,384]{2,1,0:T(8,128)(2,1)}, bf16[64,16,384]{2,1,0:T(8,128)(2,1)}, u32[]{:S(2)}, u32[]{:S(2)}) collective-permute-start(bf16[64,16,384]{2,1,0:T(8,128)(2,1)} %collective-permute-done.23.refs_22_), channel_id=1, source_target_pairs={{0,16},{1,17},{2,18},{3,19},{4,20},{5,21},{6,22},{7,23},{8,24},{9,... | collective-permute-start | bytes 2359304 | tf_op jit(solution)/shard_map/ppermute | solution.py:62
  247.9 19.0 %collective-permute-start.22 = (bf16[64,16,384]{2,1,0:T(8,128)(2,1)}, bf16[64,16,384]{2,1,0:T(8,128)(2,1)}, u32[]{:S(2)}, u32[]{:S(2)}) collective-permute-start(bf16[64,16,384]{2,1,0:T(8,128)(2,1)} %collective-permute-done.21.refs_18_), channel_id=1, source_target_pairs={{0,16},{1,17},{2,18},{3,19},{4,20},{5,21},{6,22},{7,23},{8,24},{9,... | collective-permute-start | bytes 2359304 | tf_op jit(solution)/shard_map/ppermute | solution.py:62
  (26 other events, 1138.6 us)

commit v3 on v2

--- a/solution.py
+++ b/solution.py
@@ -12,7 +12,7 @@
 NT = (((1,), (1,)), ((), ()))
 TN = (((0,), (0,)), ((), ()))
 AXES = ("row", "col")
-BIG, SMALL = (0, 80), (80, 48)
+BIG, SMALL = (0, 96), (96, 32)
 
 
 def place(r, c):
@@ -304,12 +304,12 @@
     swapped_mine = send(mine, everyone(swap))
     for n in (4, 1, 3):
         got[n] = exchange(mine, n)
-    small_twice = one_back(after(small_once, swapped_mine))
     stage = after(got[4], got[1], got[3], small_once)
     got[5], got[7] = exchange(stage, 1), exchange(stage, 3)
     got[2] = exchange(after(mine, stage), 2)
     big_twice = one_back(after(big_once, stage))
-    stage = after(got[4], got[5], got[7], got[2], small_twice)
+    small_twice = one_back(after(small_once, got[5], got[2]))
+    stage = after(got[4], got[5], got[7], got[2])
     got[6] = exchange(stage, 2)
     rights = [mine, swapped_mine]
     for n in range(1, 8):

time: 294 us -> 287 us (0.976)
  starting transfers between devices: 147 us -> 119 us
  waiting for transfers between devices: 88.8 us -> 108 us
    ppermute x27, starting transfers between devices: 147 us -> 119 us  [send(): return lax.ppermute(value, AXES, pairs)]
    ppermute x27, waiting for transfers between devices: 88.8 us -> 108 us  [send(): return lax.ppermute(value, AXES, pairs)]
  transfers between devices with their start and end apart: 27 -> 27, of which waited for: 8 -> 13; matrix products, arithmetic and copies ran while one was open for 3% -> 4% of each run, Pallas kernels for 6% -> 3%
where the time goes in v3:
time: 287 us; the launch traced here: 285 us
  starting transfers between devices  119 us (41%)
  waiting for transfers between devices  108 us (38%)
  Pallas kernels  40.5 us (14%)
  local copies, waits for them, and re-layouts  10.1 us (4%)
  other arithmetic  6.97 us (2%)
    ppermute x27, starting transfers between devices, send(): return lax.ppermute(value, AXES, pairs)  119 us
    ppermute x27, waiting for transfers between devices, send(): return lax.ppermute(value, AXES, pairs)  108 us
    pallas_call x1, Pallas kernels, final(): pl.pallas_call(functools.partial(final_kernel, subs=subs, aliased=len(ali...  21.9 us
    pallas_call x2, Pallas kernels, left_and_gate(): pl.pallas_call(left_kernel, out_shape=[jax.ShapeDtypeStruct((128, rows, 1...  15.2 us
  transfers between devices with their start and end apart: 27, of which 13 were waited for; matrix products, arithmetic and copies ran while one was open for 4% of the time, Pallas kernels for 3%

profile of v3, /device:TPU:8, one launch (start us, length us, event | category | flops | bytes accessed | tf_op | source)
XLA Modules:
  0.0 285.0 jit_solution(15166300007871329987)
XLA Ops:
  3.0 11.1 %shard_map.82 = (bf16[128,96,128]{2,1,0:T(8,128)(2,1)S(1)}, f32[96,128,128]{2,1,0:T(8,128)}) custom-call(bf16[128,128,128]{2,1,0:T(8,128)(2,1)} %x_ref.3, f32[1,128]{1,0:T(1,128)S(1)} %bitcast.17, f32[1,128]{1,0:T(1,128)S(1)} %bitcast.20, bf16[256,128]{1,0:T(8,128)(2,1)S(1)} %bitcast.15, bf16[128,128]{1,0:T(8,128)(2,1)S(1)} %copy-done.4), custom_call_target="tpu_custom_call" | custom-call | flops 2415919104 | bytes 12582912 | tf_op jit(solution)/shard_map/pallas_call | solution.py:102
  14.2 6.9 %collective-permute-start = (bf16[128,96,128]{2,1,0:T(8,128)(2,1)S(1)}, bf16[128,96,128]{2,1,0:T(8,128)(2,1)}, u32[]{:S(2)}, u32[]{:S(2)}) collective-permute-start(bf16[128,96,128]{2,1,0:T(8,128)(2,1)S(1)} %get-tuple-element.17), channel_id=1, source_target_pairs={{0,15},{1,0},{2,1},{3,2},{4,3},{5,4},{6,5},{7,6},{8,7},{9,8},{10,9... | collective-permute-start | bytes 9437192 | tf_op jit(solution)/shard_map/ppermute | solution.py:62
  27.5 4.0 %shard_map.83 = (bf16[128,32,128]{2,1,0:T(8,128)(2,1)S(1)}, f32[32,128,128]{2,1,0:T(8,128)S(1)}) custom-call(bf16[128,128,128]{2,1,0:T(8,128)(2,1)} %x_ref.3, f32[1,128]{1,0:T(1,128)S(1)} %bitcast.18, f32[1,128]{1,0:T(1,128)S(1)} %bitcast.21, bf16[256,128]{1,0:T(8,128)(2,1)S(1)} %bitcast.16, bf16[128,128]{1,0:T(8,128)(2,1)S(1)} %copy-done.5), custom_call_target="tpu_custom_call" | custom-call | flops 805306368 | bytes 4194304 | tf_op jit(solution)/shard_map/pallas_call | solution.py:102
  31.5 8.3 %collective-permute-done.3 = bf16[32,128,128]{2,1,0:T(8,128)(2,1)} collective-permute-done((bf16[32,128,128]{2,1,0:T(8,128)(2,1)}, bf16[32,128,128]{2,1,0:T(8,128)(2,1)}, u32[]{:S(2)}, u32[]{:S(2)}) %collective-permute-start.3) | collective-permute-done | bytes 1048608 | tf_op jit(solution)/shard_map/ppermute | solution.py:62
  39.8 2.5 select_select_fusion.1
  46.4 39.5 %collective-permute-start.4 = (bf16[16,128,128]{2,1,0:T(8,128)(2,1)}, bf16[16,128,128]{2,1,0:T(8,128)(2,1)}, u32[]{:S(2)}, u32[]{:S(2)}) collective-permute-start(bf16[16,128,128]{2,1,0:T(8,128)(2,1)} %slice.37), channel_id=1, source_target_pairs={{0,128},{1,129},{2,130},{3,131},{4,132},{5,133},{6,134},{7,135},{1... | collective-permute-start | bytes 1572872 | tf_op jit(solution)/shard_map/ppermute | solution.py:62
  85.9 9.0 %collective-permute-done.6 = bf16[16,128,128]{2,1,0:T(8,128)(2,1)} collective-permute-done((bf16[16,128,128]{2,1,0:T(8,128)(2,1)}, bf16[16,128,128]{2,1,0:T(8,128)(2,1)}, u32[]{:S(2)}, u32[]{:S(2)}) %collective-permute-start.6) | collective-permute-done | bytes 524320 | tf_op jit(solution)/shard_map/ppermute | solution.py:62
  96.8 10.4 %collective-permute-start.5 = (bf16[16,128,128]{2,1,0:T(8,128)(2,1)S(1)}, bf16[16,128,128]{2,1,0:T(8,128)(2,1)S(1)}, u32[]{:S(2)}, u32[]{:S(2)}) collective-permute-start(bf16[16,128,128]{2,1,0:T(8,128)(2,1)S(1)} %get-tuple-element.30), channel_id=1, source_target_pairs={{0,16},{1,17},{2,18},{3,19},{4,20},{5,21},{6,22},{7,23},{8,24},{9,... | collective-permute-start | bytes 1572872 | tf_op jit(solution)/shard_map/ppermute | solution.py:62
  109.5 4.6 %collective-permute-start.8 = (bf16[16,128,128]{2,1,0:T(8,128)(2,1)}, bf16[16,128,128]{2,1,0:T(8,128)(2,1)S(1)}, u32[]{:S(2)}, u32[]{:S(2)}) collective-permute-start(bf16[16,128,128]{2,1,0:T(8,128)(2,1)} %collective-permute-done.7), channel_id=1, source_target_pairs={{0,16},{1,17},{2,18},{3,19},{4,20},{5,21},{6,22},{7,23},{8,24},{9,... | collective-permute-start | bytes 1572872 | tf_op jit(solution)/shard_map/ppermute | solution.py:62
  114.4 10.3 %collective-permute-start.12 = (bf16[128,32,128]{2,1,0:T(8,128)(2,1)}, bf16[128,32,128]{2,1,0:T(8,128)(2,1)}, u32[]{:S(2)}, u32[]{:S(2)}) collective-permute-start(bf16[128,32,128]{2,1,0:T(8,128)(2,1)} %copy-done.3), channel_id=1, source_target_pairs={{0,15},{1,0},{2,1},{3,2},{4,3},{5,4},{6,5},{7,6},{8,7},{9,8},{10,9... | collective-permute-start | bytes 3145736 | tf_op jit(solution)/shard_map/ppermute | solution.py:62
  127.2 3.4 %shard_map.84.refs_8_ = bf16[64,16,384]{2,1,0:T(8,128)(2,1)S(1)} custom-call(bf16[48,128,128]{2,1,0:T(8,128)(2,1)S(1)} %pad_maximum_fusion.x_ref, f32[1,128]{1,0:T(1,128)S(1)} %bitcast.19, f32[1,128]{1,0:T(1,128)S(1)} %bitcast.22, bf16[128,128]{1,0:T(8,128)(2,1)S(1)} %maximum_bitcast_fusion.wt_ref), custom_call_target="tpu_custom_call" | custom-call | flops 603979776 | bytes 3145728 | tf_op jit(solution)/shard_map/pallas_call | solution.py:144
  132.3 2.7 collective-permute-start.10
  135.0 12.7 %collective-permute-done.12 = bf16[128,32,128]{2,1,0:T(8,128)(2,1)} collective-permute-done((bf16[128,32,128]{2,1,0:T(8,128)(2,1)}, bf16[128,32,128]{2,1,0:T(8,128)(2,1)}, u32[]{:S(2)}, u32[]{:S(2)}) %collective-permute-start.12) | collective-permute-done | bytes 1048608 | tf_op jit(solution)/shard_map/ppermute | solution.py:62
  147.7 2.2 collective-permute-done.11.refs_14_
  149.9 3.1 %collective-permute-done.10.refs_10_ = bf16[64,16,384]{2,1,0:T(8,128)(2,1)S(1)} collective-permute-done((bf16[64,16,384]{2,1,0:T(8,128)(2,1)S(1)}, bf16[64,16,384]{2,1,0:T(8,128)(2,1)S(1)}, u32[]{:S(2)}, u32[]{:S(2)}) %collective-permute-start.10) | collective-permute-done | bytes 786464 | tf_op jit(solution)/shard_map/ppermute | solution.py:62
  153.0 3.0 %collective-permute-done.9.refs_16_ = bf16[64,16,384]{2,1,0:T(8,128)(2,1)S(1)} collective-permute-done((bf16[64,16,384]{2,1,0:T(8,128)(2,1)S(1)}, bf16[64,16,384]{2,1,0:T(8,128)(2,1)S(1)}, u32[]{:S(2)}, u32[]{:S(2)}) %collective-permute-start.9) | collective-permute-done | bytes 786464 | tf_op jit(solution)/shard_map/ppermute | solution.py:62
  155.9 2.0 collective-permute-start.15
  157.9 13.4 %collective-permute-start.13 = (bf16[128,96,128]{2,1,0:T(8,128)(2,1)}, bf16[128,96,128]{2,1,0:T(8,128)(2,1)}, u32[]{:S(2)}, u32[]{:S(2)}) collective-permute-start(bf16[128,96,128]{2,1,0:T(8,128)(2,1)} %collective-permute-done), channel_id=1, source_target_pairs={{0,15},{1,0},{2,1},{3,2},{4,3},{5,4},{6,5},{7,6},{8,7},{9,8},{10,9... | collective-permute-start | bytes 9437192 | tf_op jit(solution)/shard_map/ppermute | solution.py:62
  171.3 3.2 %collective-permute-start.23 = (bf16[64,16,384]{2,1,0:T(8,128)(2,1)S(1)}, bf16[64,16,384]{2,1,0:T(8,128)(2,1)}, u32[]{:S(2)}, u32[]{:S(2)}) collective-permute-start(bf16[64,16,384]{2,1,0:T(8,128)(2,1)S(1)} %collective-permute-done.9.refs_16_), channel_id=1, source_target_pairs={{0,96},{1,97},{2,98},{3,99},{4,100},{5,101},{6,102},{7,103},{8,104... | collective-permute-start | bytes 2359304 | tf_op jit(solution)/shard_map/ppermute | solution.py:62
  176.1 16.8 %collective-permute-done.23.refs_22_ = bf16[64,16,384]{2,1,0:T(8,128)(2,1)} collective-permute-done((bf16[64,16,384]{2,1,0:T(8,128)(2,1)S(1)}, bf16[64,16,384]{2,1,0:T(8,128)(2,1)}, u32[]{:S(2)}, u32[]{:S(2)}) %collective-permute-start.23) | collective-permute-done | bytes 786464 | tf_op jit(solution)/shard_map/ppermute | solution.py:62
  195.5 15.5 %collective-permute-start.16 = (bf16[128,32,128]{2,1,0:T(8,128)(2,1)}, bf16[128,32,128]{2,1,0:T(8,128)(2,1)S(1)}, u32[]{:S(2)}, u32[]{:S(2)}) collective-permute-start(bf16[128,32,128]{2,1,0:T(8,128)(2,1)} %collective-permute-done.12), channel_id=1, source_target_pairs={{0,15},{1,0},{2,1},{3,2},{4,3},{5,4},{6,5},{7,6},{8,7},{9,8},{10,9... | collective-permute-start | bytes 3145736 | tf_op jit(solution)/shard_map/ppermute | solution.py:62
  211.6 3.5 %collective-permute-done.24.refs_20_ = bf16[64,16,384]{2,1,0:T(8,128)(2,1)} collective-permute-done((bf16[64,16,384]{2,1,0:T(8,128)(2,1)S(1)}, bf16[64,16,384]{2,1,0:T(8,128)(2,1)}, u32[]{:S(2)}, u32[]{:S(2)}) %collective-permute-start.24) | collective-permute-done | bytes 786464 | tf_op jit(solution)/shard_map/ppermute | solution.py:62
  215.8 45.5 %collective-permute-done.16 = bf16[128,32,128]{2,1,0:T(8,128)(2,1)S(1)} collective-permute-done((bf16[128,32,128]{2,1,0:T(8,128)(2,1)}, bf16[128,32,128]{2,1,0:T(8,128)(2,1)S(1)}, u32[]{:S(2)}, u32[]{:S(2)}) %collective-permute-start.16) | collective-permute-done | bytes 1048608 | tf_op jit(solution)/shard_map/ppermute | solution.py:62
  262.9 21.9 %shard_map.85 = bf16[128,128,128]{2,1,0:T(8,128)(2,1)} custom-call(s32[2]{0:T(128)} %pad_add_fusion.place_ref, bf16[2,64,96,128]{3,2,1,0:T(8,128)(2,1)} %bitcast.13, bf16[2,64,96,128]{3,2,1,0:T(8,128)(2,1)} %bitcast.6.refs_1_, bf16[2,64,96,128]{3,2,1,0:T(8,128)(2,1)} %bitcast.8.refs_2_, f32[96,128,128]{2,1,0:T(8,128)} %get-tuple-element.24.refs_3_, ...), custom_call_target="tpu_custom_call" | custom-call | flops 2147483648 | bytes 39845888 | tf_op jit(solution)/shard_map/pallas_call | solution.py:229
  (107 shorter events, 28.9 us)
Async XLA Ops:
  14.2 94.5 %collective-permute-start = (bf16[128,96,128]{2,1,0:T(8,128)(2,1)S(1)}, bf16[128,96,128]{2,1,0:T(8,128)(2,1)}, u32[]{:S(2)}, u32[]{:S(2)}) collective-permute-start(bf16[128,96,128]{2,1,0:T(8,128)(2,1)S(1)} %get-tuple-element.17), channel_id=1, source_target_pairs={{0,15},{1,0},{2,1},{3,2},{4,3},{5,4},{6,5},{7,6},{8,7},{9,8},{10,9... | collective-permute-start | bytes 9437192 | tf_op jit(solution)/shard_map/ppermute | solution.py:62
  22.8 17.0 %collective-permute-start.3 = (bf16[32,128,128]{2,1,0:T(8,128)(2,1)}, bf16[32,128,128]{2,1,0:T(8,128)(2,1)}, u32[]{:S(2)}, u32[]{:S(2)}) collective-permute-start(bf16[32,128,128]{2,1,0:T(8,128)(2,1)} %get-tuple-element.33), channel_id=1, source_target_pairs={{0,32},{1,33},{2,34},{17,49},{18,50},{19,51},{34,2},{35,3},{36,4},... | collective-permute-start | bytes 3145736 | tf_op jit(solution)/shard_map/ppermute | solution.py:62
  24.1 15.7 %collective-permute-start.2 = (bf16[32,128,128]{2,1,0:T(8,128)(2,1)}, bf16[32,128,128]{2,1,0:T(8,128)(2,1)}, u32[]{:S(2)}, u32[]{:S(2)}) collective-permute-start(bf16[32,128,128]{2,1,0:T(8,128)(2,1)} %get-tuple-element.34), channel_id=1, source_target_pairs={{0,64},{1,65},{2,66},{17,81},{18,82},{19,83},{34,98},{35,99},{36,1... | collective-permute-start | bytes 3145736 | tf_op jit(solution)/shard_map/ppermute | solution.py:62
  25.8 14.1 %collective-permute-start.1 = (bf16[32,128,128]{2,1,0:T(8,128)(2,1)}, bf16[32,128,128]{2,1,0:T(8,128)(2,1)}, u32[]{:S(2)}, u32[]{:S(2)}) collective-permute-start(bf16[32,128,128]{2,1,0:T(8,128)(2,1)} %get-tuple-element.35), channel_id=1, source_target_pairs={{0,96},{1,97},{2,98},{17,113},{18,114},{19,115},{34,66},{35,67},{3... | collective-permute-start | bytes 3145736 | tf_op jit(solution)/shard_map/ppermute | solution.py:62
  45.1 49.8 %collective-permute-start.6 = (bf16[16,128,128]{2,1,0:T(8,128)(2,1)}, bf16[16,128,128]{2,1,0:T(8,128)(2,1)}, u32[]{:S(2)}, u32[]{:S(2)}) collective-permute-start(bf16[16,128,128]{2,1,0:T(8,128)(2,1)} %slice.39), channel_id=1, source_target_pairs={{2,130},{4,132},{6,134},{8,136},{19,147},{21,149},{23,151},{25,153... | collective-permute-start | bytes 1572872 | tf_op jit(solution)/shard_map/ppermute | solution.py:62
  46.4 48.5 %collective-permute-start.4 = (bf16[16,128,128]{2,1,0:T(8,128)(2,1)}, bf16[16,128,128]{2,1,0:T(8,128)(2,1)}, u32[]{:S(2)}, u32[]{:S(2)}) collective-permute-start(bf16[16,128,128]{2,1,0:T(8,128)(2,1)} %slice.37), channel_id=1, source_target_pairs={{0,128},{1,129},{2,130},{3,131},{4,132},{5,133},{6,134},{7,135},{1... | collective-permute-start | bytes 1572872 | tf_op jit(solution)/shard_map/ppermute | solution.py:62
  96.4 11.7 %collective-permute-start.7 = (bf16[16,128,128]{2,1,0:T(8,128)(2,1)S(1)}, bf16[16,128,128]{2,1,0:T(8,128)(2,1)}, u32[]{:S(2)}, u32[]{:S(2)}) collective-permute-start(bf16[16,128,128]{2,1,0:T(8,128)(2,1)S(1)} %get-tuple-element.29), channel_id=1, source_target_pairs={{0,14},{1,16},{2,0},{3,18},{4,2},{5,20},{6,4},{7,22},{8,6},{9,24},... | collective-permute-start | bytes 1572872 | tf_op jit(solution)/shard_map/ppermute | solution.py:62
  96.8 11.9 %collective-permute-start.5 = (bf16[16,128,128]{2,1,0:T(8,128)(2,1)S(1)}, bf16[16,128,128]{2,1,0:T(8,128)(2,1)S(1)}, u32[]{:S(2)}, u32[]{:S(2)}) collective-permute-start(bf16[16,128,128]{2,1,0:T(8,128)(2,1)S(1)} %get-tuple-element.30), channel_id=1, source_target_pairs={{0,16},{1,17},{2,18},{3,19},{4,20},{5,21},{6,22},{7,23},{8,24},{9,... | collective-permute-start | bytes 1572872 | tf_op jit(solution)/shard_map/ppermute | solution.py:62
  109.5 16.3 %collective-permute-start.8 = (bf16[16,128,128]{2,1,0:T(8,128)(2,1)}, bf16[16,128,128]{2,1,0:T(8,128)(2,1)S(1)}, u32[]{:S(2)}, u32[]{:S(2)}) collective-permute-start(bf16[16,128,128]{2,1,0:T(8,128)(2,1)} %collective-permute-done.7), channel_id=1, source_target_pairs={{0,16},{1,17},{2,18},{3,19},{4,20},{5,21},{6,22},{7,23},{8,24},{9,... | collective-permute-start | bytes 1572872 | tf_op jit(solution)/shard_map/ppermute | solution.py:62
  114.4 33.3 %collective-permute-start.12 = (bf16[128,32,128]{2,1,0:T(8,128)(2,1)}, bf16[128,32,128]{2,1,0:T(8,128)(2,1)}, u32[]{:S(2)}, u32[]{:S(2)}) collective-permute-start(bf16[128,32,128]{2,1,0:T(8,128)(2,1)} %copy-done.3), channel_id=1, source_target_pairs={{0,15},{1,0},{2,1},{3,2},{4,3},{5,4},{6,5},{7,6},{8,7},{9,8},{10,9... | collective-permute-start | bytes 3145736 | tf_op jit(solution)/shard_map/ppermute | solution.py:62
  130.6 19.3 %collective-permute-start.11 = (bf16[64,16,384]{2,1,0:T(8,128)(2,1)S(1)}, bf16[64,16,384]{2,1,0:T(8,128)(2,1)S(1)}, u32[]{:S(2)}, u32[]{:S(2)}) collective-permute-start(bf16[64,16,384]{2,1,0:T(8,128)(2,1)S(1)} %shard_map.84.refs_8_), channel_id=1, source_target_pairs={{0,96},{1,97},{2,98},{3,99},{4,100},{5,101},{6,102},{7,103},{8,104... | collective-permute-start | bytes 2359304 | tf_op jit(solution)/shard_map/ppermute | solution.py:62
  132.3 20.6 %collective-permute-start.10 = (bf16[64,16,384]{2,1,0:T(8,128)(2,1)S(1)}, bf16[64,16,384]{2,1,0:T(8,128)(2,1)S(1)}, u32[]{:S(2)}, u32[]{:S(2)}) collective-permute-start(bf16[64,16,384]{2,1,0:T(8,128)(2,1)S(1)} %shard_map.84.refs_8_), channel_id=1, source_target_pairs={{0,32},{1,33},{2,34},{3,35},{4,36},{5,37},{6,38},{7,39},{8,40},{9,... | collective-permute-start | bytes 2359304 | tf_op jit(solution)/shard_map/ppermute | solution.py:62
  135.0 20.9 %collective-permute-start.9 = (bf16[64,16,384]{2,1,0:T(8,128)(2,1)S(1)}, bf16[64,16,384]{2,1,0:T(8,128)(2,1)S(1)}, u32[]{:S(2)}, u32[]{:S(2)}) collective-permute-start(bf16[64,16,384]{2,1,0:T(8,128)(2,1)S(1)} %shard_map.84.refs_8_), channel_id=1, source_target_pairs={{0,128},{1,129},{2,130},{3,131},{4,132},{5,133},{6,134},{7,135},{8... | collective-permute-start | bytes 2359304 | tf_op jit(solution)/shard_map/ppermute | solution.py:62
  155.9 20.1 %collective-permute-start.15 = (bf16[64,16,384]{2,1,0:T(8,128)(2,1)S(1)}, bf16[64,16,384]{2,1,0:T(8,128)(2,1)S(1)}, u32[]{:S(2)}, u32[]{:S(2)}) collective-permute-start(bf16[64,16,384]{2,1,0:T(8,128)(2,1)S(1)} %shard_map.84.refs_8_), channel_id=1, source_target_pairs={{0,64},{1,65},{2,66},{3,67},{4,68},{5,69},{6,70},{7,71},{8,72},{9,... | collective-permute-start | bytes 2359304 | tf_op jit(solution)/shard_map/ppermute | solution.py:62
  157.9 103.4 %collective-permute-start.13 = (bf16[128,96,128]{2,1,0:T(8,128)(2,1)}, bf16[128,96,128]{2,1,0:T(8,128)(2,1)}, u32[]{:S(2)}, u32[]{:S(2)}) collective-permute-start(bf16[128,96,128]{2,1,0:T(8,128)(2,1)} %collective-permute-done), channel_id=1, source_target_pairs={{0,15},{1,0},{2,1},{3,2},{4,3},{5,4},{6,5},{7,6},{8,7},{9,8},{10,9... | collective-permute-start | bytes 9437192 | tf_op jit(solution)/shard_map/ppermute | solution.py:62
  171.3 21.7 %collective-permute-start.23 = (bf16[64,16,384]{2,1,0:T(8,128)(2,1)S(1)}, bf16[64,16,384]{2,1,0:T(8,128)(2,1)}, u32[]{:S(2)}, u32[]{:S(2)}) collective-permute-start(bf16[64,16,384]{2,1,0:T(8,128)(2,1)S(1)} %collective-permute-done.9.refs_16_), channel_id=1, source_target_pairs={{0,96},{1,97},{2,98},{3,99},{4,100},{5,101},{6,102},{7,103},{8,104... | collective-permute-start | bytes 2359304 | tf_op jit(solution)/shard_map/ppermute | solution.py:62
  174.5 18.9 %collective-permute-start.14 = (bf16[64,16,384]{2,1,0:T(8,128)(2,1)S(1)}, bf16[64,16,384]{2,1,0:T(8,128)(2,1)}, u32[]{:S(2)}, u32[]{:S(2)}) collective-permute-start(bf16[64,16,384]{2,1,0:T(8,128)(2,1)S(1)} %collective-permute-done.9.refs_16_), channel_id=1, source_target_pairs={{0,32},{1,33},{2,34},{3,35},{4,36},{5,37},{6,38},{7,39},{8,40},{9,... | collective-permute-start | bytes 2359304 | tf_op jit(solution)/shard_map/ppermute | solution.py:62
  174.5 18.9 %collective-permute-start.17 = (bf16[64,16,384]{2,1,0:T(8,128)(2,1)S(1)}, bf16[64,16,384]{2,1,0:T(8,128)(2,1)S(1)}, u32[]{:S(2)}, u32[]{:S(2)}) collective-permute-start(bf16[64,16,384]{2,1,0:T(8,128)(2,1)S(1)} %shard_map.84.refs_8_), channel_id=1, source_target_pairs={{0,16},{1,17},{2,18},{3,19},{4,20},{5,21},{6,22},{7,23},{8,24},{9,... | collective-permute-start | bytes 2359304 | tf_op jit(solution)/shard_map/ppermute | solution.py:62
  176.1 17.8 %collective-permute-start.20 = (bf16[64,16,384]{2,1,0:T(8,128)(2,1)S(1)}, bf16[64,16,384]{2,1,0:T(8,128)(2,1)S(1)}, u32[]{:S(2)}, u32[]{:S(2)}) collective-permute-start(bf16[64,16,384]{2,1,0:T(8,128)(2,1)S(1)} %collective-permute-done.11.refs_14_), channel_id=1, source_target_pairs={{0,16},{1,17},{2,18},{3,19},{4,20},{5,21},{6,22},{7,23},{8,24},{9,... | collective-permute-start | bytes 2359304 | tf_op jit(solution)/shard_map/ppermute | solution.py:62
  193.4 17.6 %collective-permute-start.21 = (bf16[64,16,384]{2,1,0:T(8,128)(2,1)S(1)}, bf16[64,16,384]{2,1,0:T(8,128)(2,1)S(1)}, u32[]{:S(2)}, u32[]{:S(2)}) collective-permute-start(bf16[64,16,384]{2,1,0:T(8,128)(2,1)S(1)} %collective-permute-done.9.refs_16_), channel_id=1, source_target_pairs={{0,16},{1,17},{2,18},{3,19},{4,20},{5,21},{6,22},{7,23},{8,24},{9,... | collective-permute-start | bytes 2359304 | tf_op jit(solution)/shard_map/ppermute | solution.py:62
  193.4 17.6 %collective-permute-start.19 = (bf16[64,16,384]{2,1,0:T(8,128)(2,1)S(1)}, bf16[64,16,384]{2,1,0:T(8,128)(2,1)S(1)}, u32[]{:S(2)}, u32[]{:S(2)}) collective-permute-start(bf16[64,16,384]{2,1,0:T(8,128)(2,1)S(1)} %collective-permute-done.15.refs_12_), channel_id=1, source_target_pairs={{0,16},{1,17},{2,18},{3,19},{4,20},{5,21},{6,22},{7,23},{8,24},{9,... | collective-permute-start | bytes 2359304 | tf_op jit(solution)/shard_map/ppermute | solution.py:62
  193.9 21.2 %collective-permute-start.24 = (bf16[64,16,384]{2,1,0:T(8,128)(2,1)S(1)}, bf16[64,16,384]{2,1,0:T(8,128)(2,1)}, u32[]{:S(2)}, u32[]{:S(2)}) collective-permute-start(bf16[64,16,384]{2,1,0:T(8,128)(2,1)S(1)} %collective-permute-done.9.refs_16_), channel_id=1, source_target_pairs={{0,64},{1,65},{2,66},{3,67},{4,68},{5,69},{6,70},{7,71},{8,72},{9,... | collective-permute-start | bytes 2359304 | tf_op jit(solution)/shard_map/ppermute | solution.py:62
  195.5 65.8 %collective-permute-start.16 = (bf16[128,32,128]{2,1,0:T(8,128)(2,1)}, bf16[128,32,128]{2,1,0:T(8,128)(2,1)S(1)}, u32[]{:S(2)}, u32[]{:S(2)}) collective-permute-start(bf16[128,32,128]{2,1,0:T(8,128)(2,1)} %collective-permute-done.12), channel_id=1, source_target_pairs={{0,15},{1,0},{2,1},{3,2},{4,3},{5,4},{6,5},{7,6},{8,7},{9,8},{10,9... | collective-permute-start | bytes 3145736 | tf_op jit(solution)/shard_map/ppermute | solution.py:62
  215.1 46.2 %collective-permute-start.25 = (bf16[64,16,384]{2,1,0:T(8,128)(2,1)}, bf16[64,16,384]{2,1,0:T(8,128)(2,1)}, u32[]{:S(2)}, u32[]{:S(2)}) collective-permute-start(bf16[64,16,384]{2,1,0:T(8,128)(2,1)} %collective-permute-done.24.refs_20_), channel_id=1, source_target_pairs={{0,16},{1,17},{2,18},{3,19},{4,20},{5,21},{6,22},{7,23},{8,24},{9,... | collective-permute-start | bytes 2359304 | tf_op jit(solution)/shard_map/ppermute | solution.py:62
  (31 other events, 898.0 us)

commit v4 on v3

--- a/solution.py
+++ b/solution.py
@@ -12,7 +12,7 @@
 NT = (((1,), (1,)), ((), ()))
 TN = (((0,), (0,)), ((), ()))
 AXES = ("row", "col")
-BIG, SMALL = (0, 96), (96, 32)
+BIG, SMALL, RING = (0, 96), (96, 16), (112, 16)
 
 
 def place(r, c):
@@ -21,6 +21,18 @@
 
 def everyone(move):
     return [(place(r, c), place(*move(r, c))) for r in range(16) for c in range(16)]
+
+
+def after_hops(c, hops):
+    return (c - 8 + hops) % 16 if hops >= 6 else c // 8 * 8 + (c + hops) % 8
+
+
+def ring_pairs(hop):
+    return everyone_from(lambda c: after_hops(c, hop - 1), lambda c: after_hops(c, hop))
+
+
+def everyone_from(source, target):
+    return [(place(r, source(c)), place(r, target(c))) for r in range(16) for c in range(16)]
 
 
 def side(row):
@@ -261,7 +273,9 @@
     big, big_gate = left_of(BIG, pair)
     big_once = one_back(big)
     small, small_gate = left_of(SMALL, pair)
-    quarters[1] = after(quarters[1], big, small)
+    whirl, whirl_gate = left_of(RING, pair)
+    ring = [whirl, send(whirl, ring_pairs(1))]
+    quarters[1] = after(quarters[1], big, small, whirl)
     even = core == col % 2
     y, x_side = chip % 4, chip // 4
 
@@ -274,16 +288,19 @@
 
     one = jnp.where(even, quarter_of(0), quarter_of(1))
     two = quarter_of(2)
+    ring.append(send(after(ring[1], two), ring_pairs(2)))
     one_across = send(one[16:], across_pairs(False))
     two_across = send(two[16:], across_pairs(True))
     d_one = jnp.where(even, 0, 1)
     one = jnp.where(x_side == (col - d_one) % 16 // 8, one[:16], one_across)
     two = jnp.where(x_side == (col - 2) % 16 // 8, two[:16], two_across)
-    moving = jnp.where(even, two, one)
+    moving = after(jnp.where(even, two, one), ring[1])
+    ring.append(send(after(ring[2], moving), ring_pairs(3)))
     shifted = send(moving, shift_pairs())
     swapped_one = send(one, everyone(swap))
     small_once = one_back(after(small, swapped_one))
-    shifted = after(shifted, big_once, swapped_one, small)
+    shifted = after(shifted, big_once, swapped_one, small, ring[2])
+    ring.append(send(after(ring[3], shifted), ring_pairs(4)))
     swapped = send(shifted, everyone(swap))
     first, swapped_first = one, swapped_one
     raw = jnp.concatenate(
@@ -296,6 +313,8 @@
     )
     half = [lax.dynamic_slice_in_dim(w_proj, 256 + 128 * v + 64 * core, 64, 1) for v in range(2)]
     mine = right_piece(raw, gain, bias, jnp.concatenate(half, axis=1).T)
+    mine = after(mine, ring[3])
+    ring.append(send(after(ring[4], mine), ring_pairs(5)))
     got = {0: mine}
 
     def exchange(value, n):
@@ -304,13 +323,15 @@
     swapped_mine = send(mine, everyone(swap))
     for n in (4, 1, 3):
         got[n] = exchange(mine, n)
-    stage = after(got[4], got[1], got[3], small_once)
+    stage = after(got[4], got[1], got[3], small_once, ring[4])
     got[5], got[7] = exchange(stage, 1), exchange(stage, 3)
     got[2] = exchange(after(mine, stage), 2)
     big_twice = one_back(after(big_once, stage))
     small_twice = one_back(after(small_once, got[5], got[2]))
-    stage = after(got[4], got[5], got[7], got[2])
+    stage = after(got[4], got[5], got[7], got[2], ring[5])
+    ring.append(send(after(ring[5], stage), ring_pairs(6)))
     got[6] = exchange(stage, 2)
+    ring.append(send(after(ring[6], got[6]), ring_pairs(7)))
     rights = [mine, swapped_mine]
     for n in range(1, 8):
         rights += [got[n], send(got[n], everyone(swap))]
@@ -320,6 +341,7 @@
     out_b = jnp.broadcast_to(out_bias[:, None], (128, 128))
 
     groups = [(big, big_once, big_twice, big_gate), (small, small_once, small_twice, small_gate)]
+    groups.append((whirl, ring[7], ring[6], whirl_gate))
     return final(where, groups, rights, out_g, out_b, w_out, None, 0)
 
 

time: 287 us -> 308 us (1.073)
  waiting for transfers between devices: 108 us -> 136 us
  starting transfers between devices: 119 us -> 109 us
  local copies, waits for them, and re-layouts: 10.1 us -> 14.1 us
    ppermute x27 -> x34, waiting for transfers between devices: 108 us -> 136 us  [send(): return lax.ppermute(value, AXES, pairs)]
    ppermute x27 -> x34, starting transfers between devices: 119 us -> 109 us  [send(): return lax.ppermute(value, AXES, pairs)]
    unnamed x59 -> x69, local copies, waits for them, and re-layouts: 4.18 us -> 8.25 us
    pallas_call x2 -> x3, Pallas kernels: 15.2 us -> 14.8 us  [left_and_gate(): pl.pallas_call(left_kernel, out_shape=[jax.ShapeDtypeStruct((128, rows, 1...]
  transfers between devices with their start and end apart: 27 -> 34, of which waited for: 13 -> 15; matrix products, arithmetic and copies ran while one was open for 4% -> 3% of each run, Pallas kernels for 3% -> 2%
where the time goes in v4:
time: 308 us; the launch traced here: 306 us
  waiting for transfers between devices  136 us (44%)
  starting transfers between devices  109 us (35%)
  Pallas kernels  40 us (13%)
  local copies, waits for them, and re-layouts  14.1 us (5%)
  other arithmetic  6.77 us (2%)
    ppermute x34, waiting for transfers between devices, send(): return lax.ppermute(value, AXES, pairs)  136 us
    ppermute x34, starting transfers between devices, send(): return lax.ppermute(value, AXES, pairs)  109 us
    pallas_call x1, Pallas kernels, final(): pl.pallas_call(functools.partial(final_kernel, subs=subs, aliased=len(ali...  21.7 us
    pallas_call x3, Pallas kernels, left_and_gate(): pl.pallas_call(left_kernel, out_shape=[jax.ShapeDtypeStruct((128, rows, 1...  14.8 us
    unnamed x69, local copies, waits for them, and re-layouts  8.25 us
  transfers between devices with their start and end apart: 34, of which 15 were waited for; matrix products, arithmetic and copies ran while one was open for 3% of the time, Pallas kernels for 2%

profile of v4, /device:TPU:8, one launch (start us, length us, event | category | flops | bytes accessed | tf_op | source)
XLA Modules:
  0.0 306.5 jit_solution(7082729082174067936)
XLA Ops:
  3.0 11.1 %shard_map.82 = (bf16[128,96,128]{2,1,0:T(8,128)(2,1)S(1)}, f32[96,128,128]{2,1,0:T(8,128)}) custom-call(bf16[128,128,128]{2,1,0:T(8,128)(2,1)} %x_ref.5, f32[1,128]{1,0:T(1,128)S(1)} %bitcast.21, f32[1,128]{1,0:T(1,128)S(1)} %bitcast.25, bf16[256,128]{1,0:T(8,128)(2,1)S(1)} %bitcast.17, bf16[128,128]{1,0:T(8,128)(2,1)S(1)} %copy-done.8), custom_call_target="tpu_custom_call" | custom-call | flops 2415919104 | bytes 12582912 | tf_op jit(solution)/shard_map/pallas_call | solution.py:114
  14.2 6.8 %collective-permute-start = (bf16[128,96,128]{2,1,0:T(8,128)(2,1)S(1)}, bf16[128,96,128]{2,1,0:T(8,128)(2,1)}, u32[]{:S(2)}, u32[]{:S(2)}) collective-permute-start(bf16[128,96,128]{2,1,0:T(8,128)(2,1)S(1)} %get-tuple-element.27), channel_id=1, source_target_pairs={{0,15},{1,0},{2,1},{3,2},{4,3},{5,4},{6,5},{7,6},{8,7},{9,8},{10,9... | collective-permute-start | bytes 9437192 | tf_op jit(solution)/shard_map/ppermute | solution.py:74
  27.5 2.2 shard_map.84
  34.4 5.5 %collective-permute-done.3 = bf16[32,128,128]{2,1,0:T(8,128)(2,1)} collective-permute-done((bf16[32,128,128]{2,1,0:T(8,128)(2,1)}, bf16[32,128,128]{2,1,0:T(8,128)(2,1)}, u32[]{:S(2)}, u32[]{:S(2)}) %collective-permute-start.3) | collective-permute-done | bytes 1048608 | tf_op jit(solution)/shard_map/ppermute | solution.py:74
  39.9 2.3 select_select_fusion.1
  46.2 39.5 %collective-permute-start.4 = (bf16[16,128,128]{2,1,0:T(8,128)(2,1)}, bf16[16,128,128]{2,1,0:T(8,128)(2,1)}, u32[]{:S(2)}, u32[]{:S(2)}) collective-permute-start(bf16[16,128,128]{2,1,0:T(8,128)(2,1)} %slice.37), channel_id=1, source_target_pairs={{0,128},{1,129},{2,130},{3,131},{4,132},{5,133},{6,134},{7,135},{1... | collective-permute-start | bytes 1572872 | tf_op jit(solution)/shard_map/ppermute | solution.py:74
  85.7 9.0 %collective-permute-done.6 = bf16[16,128,128]{2,1,0:T(8,128)(2,1)} collective-permute-done((bf16[16,128,128]{2,1,0:T(8,128)(2,1)}, bf16[16,128,128]{2,1,0:T(8,128)(2,1)}, u32[]{:S(2)}, u32[]{:S(2)}) %collective-permute-start.6) | collective-permute-done | bytes 524320 | tf_op jit(solution)/shard_map/ppermute | solution.py:74
  96.7 10.4 %collective-permute-start.5 = (bf16[16,128,128]{2,1,0:T(8,128)(2,1)S(1)}, bf16[16,128,128]{2,1,0:T(8,128)(2,1)S(1)}, u32[]{:S(2)}, u32[]{:S(2)}) collective-permute-start(bf16[16,128,128]{2,1,0:T(8,128)(2,1)S(1)} %get-tuple-element.50), channel_id=1, source_target_pairs={{0,16},{1,17},{2,18},{3,19},{4,20},{5,21},{6,22},{7,23},{8,24},{9,... | collective-permute-start | bytes 1572872 | tf_op jit(solution)/shard_map/ppermute | solution.py:74
  110.0 4.1 %collective-permute-start.10 = (bf16[16,128,128]{2,1,0:T(8,128)(2,1)}, bf16[16,128,128]{2,1,0:T(8,128)(2,1)S(1)}, u32[]{:S(2)}, u32[]{:S(2)}) collective-permute-start(bf16[16,128,128]{2,1,0:T(8,128)(2,1)} %collective-permute-done.8), channel_id=1, source_target_pairs={{0,16},{1,17},{2,18},{3,19},{4,20},{5,21},{6,22},{7,23},{8,24},{9,... | collective-permute-start | bytes 1572872 | tf_op jit(solution)/shard_map/ppermute | solution.py:74
  114.4 6.5 %collective-permute-start.11 = (bf16[128,16,128]{2,1,0:T(8,128)(2,1)}, bf16[128,16,128]{2,1,0:T(8,128)(2,1)S(1)}, u32[]{:S(2)}, u32[]{:S(2)}) collective-permute-start(bf16[128,16,128]{2,1,0:T(8,128)(2,1)} %copy-done.32), channel_id=1, source_target_pairs={{2,3},{3,4},{4,5},{5,6},{6,7},{7,0},{0,1},{1,2},{10,11},{11,12},{1... | collective-permute-start | bytes 1572872 | tf_op jit(solution)/shard_map/ppermute | solution.py:74
  123.3 3.4 %shard_map.85.refs_12_ = bf16[64,16,384]{2,1,0:T(8,128)(2,1)S(1)} custom-call(bf16[48,128,128]{2,1,0:T(8,128)(2,1)S(1)} %pad_maximum_fusion.x_ref, f32[1,128]{1,0:T(1,128)S(1)} %bitcast.24, f32[1,128]{1,0:T(1,128)S(1)} %bitcast.28, bf16[128,128]{1,0:T(8,128)(2,1)S(1)} %maximum_bitcast_fusion.wt_ref), custom_call_target="tpu_custom_call" | custom-call | flops 603979776 | bytes 3145728 | tf_op jit(solution)/shard_map/pallas_call | solution.py:156
  126.8 7.4 %collective-permute-done.11 = bf16[128,16,128]{2,1,0:T(8,128)(2,1)S(1)} collective-permute-done((bf16[128,16,128]{2,1,0:T(8,128)(2,1)}, bf16[128,16,128]{2,1,0:T(8,128)(2,1)S(1)}, u32[]{:S(2)}, u32[]{:S(2)}) %collective-permute-start.11) | collective-permute-done | bytes 524320 | tf_op jit(solution)/shard_map/ppermute | solution.py:74
  134.1 3.0 collective-permute-start.14
  137.1 2.5 collective-permute-start.13
  139.6 2.7 collective-permute-start.12
  144.3 11.2 %collective-permute-done.15 = bf16[128,16,128]{2,1,0:T(8,128)(2,1)S(1)} collective-permute-done((bf16[128,16,128]{2,1,0:T(8,128)(2,1)S(1)}, bf16[128,16,128]{2,1,0:T(8,128)(2,1)S(1)}, u32[]{:S(2)}, u32[]{:S(2)}) %collective-permute-start.15) | collective-permute-done | bytes 524320 | tf_op jit(solution)/shard_map/ppermute | solution.py:74
  159.6 15.5 %collective-permute-start.17 = (bf16[128,96,128]{2,1,0:T(8,128)(2,1)}, bf16[128,96,128]{2,1,0:T(8,128)(2,1)}, u32[]{:S(2)}, u32[]{:S(2)}) collective-permute-start(bf16[128,96,128]{2,1,0:T(8,128)(2,1)} %collective-permute-done), channel_id=1, source_target_pairs={{0,15},{1,0},{2,1},{3,2},{4,3},{5,4},{6,5},{7,6},{8,7},{9,8},{10,9... | collective-permute-start | bytes 9437192 | tf_op jit(solution)/shard_map/ppermute | solution.py:74
  177.5 2.3 collective-permute-start.18
  179.8 12.7 %collective-permute-done.21 = bf16[128,16,128]{2,1,0:T(8,128)(2,1)S(1)} collective-permute-done((bf16[128,16,128]{2,1,0:T(8,128)(2,1)S(1)}, bf16[128,16,128]{2,1,0:T(8,128)(2,1)S(1)}, u32[]{:S(2)}, u32[]{:S(2)}) %collective-permute-start.21) | collective-permute-done | bytes 524320 | tf_op jit(solution)/shard_map/ppermute | solution.py:74
  192.6 4.6 %collective-permute-done.19.refs_16_ = bf16[64,16,384]{2,1,0:T(8,128)(2,1)S(1)} collective-permute-done((bf16[64,16,384]{2,1,0:T(8,128)(2,1)S(1)}, bf16[64,16,384]{2,1,0:T(8,128)(2,1)S(1)}, u32[]{:S(2)}, u32[]{:S(2)}) %collective-permute-start.19) | collective-permute-done | bytes 786464 | tf_op jit(solution)/shard_map/ppermute | solution.py:74
  197.1 14.4 %collective-permute-done.22.refs_26_ = bf16[64,16,384]{2,1,0:T(8,128)(2,1)} collective-permute-done((bf16[64,16,384]{2,1,0:T(8,128)(2,1)S(1)}, bf16[64,16,384]{2,1,0:T(8,128)(2,1)}, u32[]{:S(2)}, u32[]{:S(2)}) %collective-permute-start.22) | collective-permute-done | bytes 786464 | tf_op jit(solution)/shard_map/ppermute | solution.py:74
  216.3 47.8 %collective-permute-done.20 = bf16[128,16,128]{2,1,0:T(8,128)(2,1)S(1)} collective-permute-done((bf16[128,16,128]{2,1,0:T(8,128)(2,1)S(1)}, bf16[128,16,128]{2,1,0:T(8,128)(2,1)S(1)}, u32[]{:S(2)}, u32[]{:S(2)}) %collective-permute-start.20) | collective-permute-done | bytes 524320 | tf_op jit(solution)/shard_map/ppermute | solution.py:74
  267.8 15.3 %collective-permute-done.25 = bf16[128,16,128]{2,1,0:T(8,128)(2,1)} collective-permute-done((bf16[128,16,128]{2,1,0:T(8,128)(2,1)}, bf16[128,16,128]{2,1,0:T(8,128)(2,1)}, u32[]{:S(2)}, u32[]{:S(2)}) %collective-permute-start.25) | collective-permute-done | bytes 524320 | tf_op jit(solution)/shard_map/ppermute | solution.py:74
  284.6 21.7 %shard_map.86 = bf16[128,128,128]{2,1,0:T(8,128)(2,1)} custom-call(s32[2]{0:T(128)} %pad_add_fusion.place_ref, bf16[2,64,96,128]{3,2,1,0:T(8,128)(2,1)} %bitcast.16, bf16[2,64,96,128]{3,2,1,0:T(8,128)(2,1)} %bitcast.6.refs_1_, bf16[2,64,96,128]{3,2,1,0:T(8,128)(2,1)} %bitcast.8.refs_2_, f32[96,128,128]{2,1,0:T(8,128)} %get-tuple-element.40.refs_3_, ...), custom_call_target="tpu_custom_call" | custom-call | flops 2147483648 | bytes 39845888 | tf_op jit(solution)/shard_map/pallas_call | solution.py:241
  (132 shorter events, 44.0 us)
Async XLA Ops:
  14.2 95.0 %collective-permute-start = (bf16[128,96,128]{2,1,0:T(8,128)(2,1)S(1)}, bf16[128,96,128]{2,1,0:T(8,128)(2,1)}, u32[]{:S(2)}, u32[]{:S(2)}) collective-permute-start(bf16[128,96,128]{2,1,0:T(8,128)(2,1)S(1)} %get-tuple-element.27), channel_id=1, source_target_pairs={{0,15},{1,0},{2,1},{3,2},{4,3},{5,4},{6,5},{7,6},{8,7},{9,8},{10,9... | collective-permute-start | bytes 9437192 | tf_op jit(solution)/shard_map/ppermute | solution.py:74
  22.8 17.1 %collective-permute-start.3 = (bf16[32,128,128]{2,1,0:T(8,128)(2,1)}, bf16[32,128,128]{2,1,0:T(8,128)(2,1)}, u32[]{:S(2)}, u32[]{:S(2)}) collective-permute-start(bf16[32,128,128]{2,1,0:T(8,128)(2,1)} %get-tuple-element.53), channel_id=1, source_target_pairs={{0,32},{1,33},{2,34},{17,49},{18,50},{19,51},{34,2},{35,3},{36,4},... | collective-permute-start | bytes 3145736 | tf_op jit(solution)/shard_map/ppermute | solution.py:74
  24.2 15.7 %collective-permute-start.2 = (bf16[32,128,128]{2,1,0:T(8,128)(2,1)}, bf16[32,128,128]{2,1,0:T(8,128)(2,1)}, u32[]{:S(2)}, u32[]{:S(2)}) collective-permute-start(bf16[32,128,128]{2,1,0:T(8,128)(2,1)} %get-tuple-element.54), channel_id=1, source_target_pairs={{0,64},{1,65},{2,66},{17,81},{18,82},{19,83},{34,98},{35,99},{36,1... | collective-permute-start | bytes 3145736 | tf_op jit(solution)/shard_map/ppermute | solution.py:74
  30.7 55.0 %collective-permute-start.7 = (bf16[128,16,128]{2,1,0:T(8,128)(2,1)}, bf16[128,16,128]{2,1,0:T(8,128)(2,1)}, u32[]{:S(2)}, u32[]{:S(2)}) collective-permute-start(bf16[128,16,128]{2,1,0:T(8,128)(2,1)} %get-tuple-element.29), channel_id=1, source_target_pairs={{0,1},{1,2},{2,3},{3,4},{4,5},{5,6},{6,7},{7,0},{8,9},{9,10},{10,1... | collective-permute-start | bytes 1572872 | tf_op jit(solution)/shard_map/ppermute | solution.py:74
  44.9 49.8 %collective-permute-start.6 = (bf16[16,128,128]{2,1,0:T(8,128)(2,1)}, bf16[16,128,128]{2,1,0:T(8,128)(2,1)}, u32[]{:S(2)}, u32[]{:S(2)}) collective-permute-start(bf16[16,128,128]{2,1,0:T(8,128)(2,1)} %slice.39), channel_id=1, source_target_pairs={{2,130},{4,132},{6,134},{8,136},{19,147},{21,149},{23,151},{25,153... | collective-permute-start | bytes 1572872 | tf_op jit(solution)/shard_map/ppermute | solution.py:74
  46.2 48.5 %collective-permute-start.4 = (bf16[16,128,128]{2,1,0:T(8,128)(2,1)}, bf16[16,128,128]{2,1,0:T(8,128)(2,1)}, u32[]{:S(2)}, u32[]{:S(2)}) collective-permute-start(bf16[16,128,128]{2,1,0:T(8,128)(2,1)} %slice.37), channel_id=1, source_target_pairs={{0,128},{1,129},{2,130},{3,131},{4,132},{5,133},{6,134},{7,135},{1... | collective-permute-start | bytes 1572872 | tf_op jit(solution)/shard_map/ppermute | solution.py:74
  85.7 21.4 %collective-permute-start.9 = (bf16[128,16,128]{2,1,0:T(8,128)(2,1)}, bf16[128,16,128]{2,1,0:T(8,128)(2,1)S(1)}, u32[]{:S(2)}, u32[]{:S(2)}) collective-permute-start(bf16[128,16,128]{2,1,0:T(8,128)(2,1)} %collective-permute-done.7), channel_id=1, source_target_pairs={{1,2},{2,3},{3,4},{4,5},{5,6},{6,7},{7,0},{0,1},{9,10},{10,11},{11... | collective-permute-start | bytes 1572872 | tf_op jit(solution)/shard_map/ppermute | solution.py:74
  114.4 19.8 %collective-permute-start.11 = (bf16[128,16,128]{2,1,0:T(8,128)(2,1)}, bf16[128,16,128]{2,1,0:T(8,128)(2,1)S(1)}, u32[]{:S(2)}, u32[]{:S(2)}) collective-permute-start(bf16[128,16,128]{2,1,0:T(8,128)(2,1)} %copy-done.32), channel_id=1, source_target_pairs={{2,3},{3,4},{4,5},{5,6},{6,7},{7,0},{0,1},{1,2},{10,11},{11,12},{1... | collective-permute-start | bytes 1572872 | tf_op jit(solution)/shard_map/ppermute | solution.py:74
  134.1 23.6 %collective-permute-start.14 = (bf16[64,16,384]{2,1,0:T(8,128)(2,1)S(1)}, bf16[64,16,384]{2,1,0:T(8,128)(2,1)S(1)}, u32[]{:S(2)}, u32[]{:S(2)}) collective-permute-start(bf16[64,16,384]{2,1,0:T(8,128)(2,1)S(1)} %shard_map.85.refs_12_), channel_id=1, source_target_pairs={{0,96},{1,97},{2,98},{3,99},{4,100},{5,101},{6,102},{7,103},{8,104... | collective-permute-start | bytes 2359304 | tf_op jit(solution)/shard_map/ppermute | solution.py:74
  137.1 20.6 %collective-permute-start.13 = (bf16[64,16,384]{2,1,0:T(8,128)(2,1)S(1)}, bf16[64,16,384]{2,1,0:T(8,128)(2,1)S(1)}, u32[]{:S(2)}, u32[]{:S(2)}) collective-permute-start(bf16[64,16,384]{2,1,0:T(8,128)(2,1)S(1)} %shard_map.85.refs_12_), channel_id=1, source_target_pairs={{0,32},{1,33},{2,34},{3,35},{4,36},{5,37},{6,38},{7,39},{8,40},{9,... | collective-permute-start | bytes 2359304 | tf_op jit(solution)/shard_map/ppermute | solution.py:74
  139.6 20.0 %collective-permute-start.12 = (bf16[64,16,384]{2,1,0:T(8,128)(2,1)S(1)}, bf16[64,16,384]{2,1,0:T(8,128)(2,1)S(1)}, u32[]{:S(2)}, u32[]{:S(2)}) collective-permute-start(bf16[64,16,384]{2,1,0:T(8,128)(2,1)S(1)} %shard_map.85.refs_12_), channel_id=1, source_target_pairs={{0,128},{1,129},{2,130},{3,131},{4,132},{5,133},{6,134},{7,135},{8... | collective-permute-start | bytes 2359304 | tf_op jit(solution)/shard_map/ppermute | solution.py:74
  143.5 14.2 %collective-permute-start.16 = (bf16[128,16,128]{2,1,0:T(8,128)(2,1)S(1)}, bf16[128,16,128]{2,1,0:T(8,128)(2,1)S(1)}, u32[]{:S(2)}, u32[]{:S(2)}) collective-permute-start(bf16[128,16,128]{2,1,0:T(8,128)(2,1)S(1)} %collective-permute-done.11), channel_id=1, source_target_pairs={{3,4},{4,5},{5,6},{6,7},{7,0},{0,1},{1,2},{2,3},{11,12},{12,13},{1... | collective-permute-start | bytes 1572872 | tf_op jit(solution)/shard_map/ppermute | solution.py:74
  159.6 123.5 %collective-permute-start.17 = (bf16[128,96,128]{2,1,0:T(8,128)(2,1)}, bf16[128,96,128]{2,1,0:T(8,128)(2,1)}, u32[]{:S(2)}, u32[]{:S(2)}) collective-permute-start(bf16[128,96,128]{2,1,0:T(8,128)(2,1)} %collective-permute-done), channel_id=1, source_target_pairs={{0,15},{1,0},{2,1},{3,2},{4,3},{5,4},{6,5},{7,6},{8,7},{9,8},{10,9... | collective-permute-start | bytes 9437192 | tf_op jit(solution)/shard_map/ppermute | solution.py:74
  175.1 22.0 %collective-permute-start.19 = (bf16[64,16,384]{2,1,0:T(8,128)(2,1)S(1)}, bf16[64,16,384]{2,1,0:T(8,128)(2,1)S(1)}, u32[]{:S(2)}, u32[]{:S(2)}) collective-permute-start(bf16[64,16,384]{2,1,0:T(8,128)(2,1)S(1)} %shard_map.85.refs_12_), channel_id=1, source_target_pairs={{0,64},{1,65},{2,66},{3,67},{4,68},{5,69},{6,70},{7,71},{8,72},{9,... | collective-permute-start | bytes 2359304 | tf_op jit(solution)/shard_map/ppermute | solution.py:74
  177.2 34.4 %collective-permute-start.22 = (bf16[64,16,384]{2,1,0:T(8,128)(2,1)S(1)}, bf16[64,16,384]{2,1,0:T(8,128)(2,1)}, u32[]{:S(2)}, u32[]{:S(2)}) collective-permute-start(bf16[64,16,384]{2,1,0:T(8,128)(2,1)S(1)} %collective-permute-done.12.refs_20_), channel_id=1, source_target_pairs={{0,96},{1,97},{2,98},{3,99},{4,100},{5,101},{6,102},{7,103},{8,104... | collective-permute-start | bytes 2359304 | tf_op jit(solution)/shard_map/ppermute | solution.py:74
  177.5 35.0 %collective-permute-start.18 = (bf16[64,16,384]{2,1,0:T(8,128)(2,1)S(1)}, bf16[64,16,384]{2,1,0:T(8,128)(2,1)}, u32[]{:S(2)}, u32[]{:S(2)}) collective-permute-start(bf16[64,16,384]{2,1,0:T(8,128)(2,1)S(1)} %collective-permute-done.12.refs_20_), channel_id=1, source_target_pairs={{0,32},{1,33},{2,34},{3,35},{4,36},{5,37},{6,38},{7,39},{8,40},{9,... | collective-permute-start | bytes 2359304 | tf_op jit(solution)/shard_map/ppermute | solution.py:74
  192.6 19.9 %collective-permute-start.26 = (bf16[64,16,384]{2,1,0:T(8,128)(2,1)S(1)}, bf16[64,16,384]{2,1,0:T(8,128)(2,1)S(1)}, u32[]{:S(2)}, u32[]{:S(2)}) collective-permute-start(bf16[64,16,384]{2,1,0:T(8,128)(2,1)S(1)} %shard_map.85.refs_12_), channel_id=1, source_target_pairs={{0,16},{1,17},{2,18},{3,19},{4,20},{5,21},{6,22},{7,23},{8,24},{9,... | collective-permute-start | bytes 2359304 | tf_op jit(solution)/shard_map/ppermute | solution.py:74
  197.1 17.0 %collective-permute-start.29 = (bf16[64,16,384]{2,1,0:T(8,128)(2,1)S(1)}, bf16[64,16,384]{2,1,0:T(8,128)(2,1)S(1)}, u32[]{:S(2)}, u32[]{:S(2)}) collective-permute-start(bf16[64,16,384]{2,1,0:T(8,128)(2,1)S(1)} %collective-permute-done.14.refs_18_), channel_id=1, source_target_pairs={{0,16},{1,17},{2,18},{3,19},{4,20},{5,21},{6,22},{7,23},{8,24},{9,... | collective-permute-start | bytes 2359304 | tf_op jit(solution)/shard_map/ppermute | solution.py:74
  212.5 52.1 %collective-permute-start.24 = (bf16[64,16,384]{2,1,0:T(8,128)(2,1)S(1)}, bf16[64,16,384]{2,1,0:T(8,128)(2,1)}, u32[]{:S(2)}, u32[]{:S(2)}) collective-permute-start(bf16[64,16,384]{2,1,0:T(8,128)(2,1)S(1)} %collective-permute-done.12.refs_20_), channel_id=1, source_target_pairs={{0,64},{1,65},{2,66},{3,67},{4,68},{5,69},{6,70},{7,71},{8,72},{9,... | collective-permute-start | bytes 2359304 | tf_op jit(solution)/shard_map/ppermute | solution.py:74
  214.2 49.9 %collective-permute-start.20 = (bf16[128,16,128]{2,1,0:T(8,128)(2,1)S(1)}, bf16[128,16,128]{2,1,0:T(8,128)(2,1)S(1)}, u32[]{:S(2)}, u32[]{:S(2)}) collective-permute-start(bf16[128,16,128]{2,1,0:T(8,128)(2,1)S(1)} %collective-permute-done.15), channel_id=1, source_target_pairs={{0,15},{1,0},{2,1},{3,2},{4,3},{5,4},{6,5},{7,6},{8,7},{9,8},{10,9... | collective-permute-start | bytes 1572872 | tf_op jit(solution)/shard_map/ppermute | solution.py:74
  214.5 49.6 %collective-permute-start.23 = (bf16[128,16,128]{2,1,0:T(8,128)(2,1)S(1)}, bf16[128,16,128]{2,1,0:T(8,128)(2,1)}, u32[]{:S(2)}, u32[]{:S(2)}) collective-permute-start(bf16[128,16,128]{2,1,0:T(8,128)(2,1)S(1)} %collective-permute-done.21), channel_id=1, source_target_pairs={{5,14},{6,15},{7,0},{0,1},{1,2},{2,3},{3,4},{4,5},{13,6},{14,7},{1... | collective-permute-start | bytes 1572872 | tf_op jit(solution)/shard_map/ppermute | solution.py:74
  216.3 48.7 %collective-permute-start.28 = (bf16[64,16,384]{2,1,0:T(8,128)(2,1)S(1)}, bf16[64,16,384]{2,1,0:T(8,128)(2,1)S(1)}, u32[]{:S(2)}, u32[]{:S(2)}) collective-permute-start(bf16[64,16,384]{2,1,0:T(8,128)(2,1)S(1)} %collective-permute-done.19.refs_16_), channel_id=1, source_target_pairs={{0,16},{1,17},{2,18},{3,19},{4,20},{5,21},{6,22},{7,23},{8,24},{9,... | collective-permute-start | bytes 2359304 | tf_op jit(solution)/shard_map/ppermute | solution.py:74
  264.6 18.5 %collective-permute-start.32 = (bf16[64,16,384]{2,1,0:T(8,128)(2,1)}, bf16[64,16,384]{2,1,0:T(8,128)(2,1)}, u32[]{:S(2)}, u32[]{:S(2)}) collective-permute-start(bf16[64,16,384]{2,1,0:T(8,128)(2,1)} %collective-permute-done.24.refs_24_), channel_id=1, source_target_pairs={{0,16},{1,17},{2,18},{3,19},{4,20},{5,21},{6,22},{7,23},{8,24},{9,... | collective-permute-start | bytes 2359304 | tf_op jit(solution)/shard_map/ppermute | solution.py:74
  265.9 17.2 %collective-permute-start.25 = (bf16[128,16,128]{2,1,0:T(8,128)(2,1)}, bf16[128,16,128]{2,1,0:T(8,128)(2,1)}, u32[]{:S(2)}, u32[]{:S(2)}) collective-permute-start(bf16[128,16,128]{2,1,0:T(8,128)(2,1)} %collective-permute-done.23), channel_id=1, source_target_pairs={{14,15},{15,0},{0,1},{1,2},{2,3},{3,4},{4,5},{5,6},{6,7},{7,8},{8,... | collective-permute-start | bytes 1572872 | tf_op jit(solution)/shard_map/ppermute | solution.py:74
  (43 other events, 1459.1 us)

commit v5 on v4

--- a/solution.py
+++ b/solution.py
@@ -299,7 +299,7 @@
     shifted = send(moving, shift_pairs())
     swapped_one = send(one, everyone(swap))
     small_once = one_back(after(small, swapped_one))
-    shifted = after(shifted, big_once, swapped_one, small, ring[2])
+    shifted = after(shifted, big_once, swapped_one, small, ring[3])
     ring.append(send(after(ring[3], shifted), ring_pairs(4)))
     swapped = send(shifted, everyone(swap))
     first, swapped_first = one, swapped_one
@@ -313,7 +313,7 @@
     )
     half = [lax.dynamic_slice_in_dim(w_proj, 256 + 128 * v + 64 * core, 64, 1) for v in range(2)]
     mine = right_piece(raw, gain, bias, jnp.concatenate(half, axis=1).T)
-    mine = after(mine, ring[3])
+    mine = after(mine, ring[4])
     ring.append(send(after(ring[4], mine), ring_pairs(5)))
     got = {0: mine}
 
@@ -323,15 +323,15 @@
     swapped_mine = send(mine, everyone(swap))
     for n in (4, 1, 3):
         got[n] = exchange(mine, n)
-    stage = after(got[4], got[1], got[3], small_once, ring[4])
+    stage = after(got[4], got[1], got[3], small_once, ring[5])
+    ring.append(send(after(ring[5], stage), ring_pairs(6)))
     got[5], got[7] = exchange(stage, 1), exchange(stage, 3)
     got[2] = exchange(after(mine, stage), 2)
     big_twice = one_back(after(big_once, stage))
-    small_twice = one_back(after(small_once, got[5], got[2]))
-    stage = after(got[4], got[5], got[7], got[2], ring[5])
-    ring.append(send(after(ring[5], stage), ring_pairs(6)))
+    stage = after(got[4], got[5], got[7], got[2], ring[6])
+    ring.append(send(after(ring[6], stage), ring_pairs(7)))
     got[6] = exchange(stage, 2)
-    ring.append(send(after(ring[6], got[6]), ring_pairs(7)))
+    small_twice = one_back(after(small_once, got[6]))
     rights = [mine, swapped_mine]
     for n in range(1, 8):
         rights += [got[n], send(got[n], everyone(swap))]

time: 308 us -> 290 us (0.942)
  starting transfers between devices: 109 us -> 95.3 us
  waiting for transfers between devices: 136 us -> 132 us
    ppermute x34, starting transfers between devices: 109 us -> 95.3 us  [send(): return lax.ppermute(value, AXES, pairs)]
    ppermute x34, waiting for transfers between devices: 136 us -> 132 us  [send(): return lax.ppermute(value, AXES, pairs)]
  transfers between devices with their start and end apart: 34 -> 34, of which waited for: 15 -> 17; matrix products, arithmetic and copies ran while one was open for 3% -> 4% of each run, Pallas kernels for 2% -> 2%
where the time goes in v5:
time: 290 us; the launch traced here: 289 us
  waiting for transfers between devices  132 us (46%)
  starting transfers between devices  95.3 us (33%)
  Pallas kernels  40 us (14%)
  local copies, waits for them, and re-layouts  14.1 us (5%)
  other arithmetic  6.77 us (2%)
    ppermute x34, waiting for transfers between devices, send(): return lax.ppermute(value, AXES, pairs)  132 us
    ppermute x34, starting transfers between devices, send(): return lax.ppermute(value, AXES, pairs)  95.3 us
    pallas_call x1, Pallas kernels, final(): pl.pallas_call(functools.partial(final_kernel, subs=subs, aliased=len(ali...  21.7 us
    pallas_call x3, Pallas kernels, left_and_gate(): pl.pallas_call(left_kernel, out_shape=[jax.ShapeDtypeStruct((128, rows, 1...  14.8 us
    unnamed x69, local copies, waits for them, and re-layouts  8.24 us
  transfers between devices with their start and end apart: 34, of which 17 were waited for; matrix products, arithmetic and copies ran while one was open for 4% of the time, Pallas kernels for 2%

profile of v5, /device:TPU:8, one launch (start us, length us, event | category | flops | bytes accessed | tf_op | source)
XLA Modules:
  0.0 289.1 jit_solution(17720352612731688868)
XLA Ops:
  3.0 11.1 %shard_map.82 = (bf16[128,96,128]{2,1,0:T(8,128)(2,1)S(1)}, f32[96,128,128]{2,1,0:T(8,128)}) custom-call(bf16[128,128,128]{2,1,0:T(8,128)(2,1)} %x_ref.5, f32[1,128]{1,0:T(1,128)S(1)} %bitcast.21, f32[1,128]{1,0:T(1,128)S(1)} %bitcast.25, bf16[256,128]{1,0:T(8,128)(2,1)S(1)} %bitcast.17, bf16[128,128]{1,0:T(8,128)(2,1)S(1)} %copy-done.8), custom_call_target="tpu_custom_call" | custom-call | flops 2415919104 | bytes 12582912 | tf_op jit(solution)/shard_map/pallas_call | solution.py:114
  14.2 6.8 %collective-permute-start = (bf16[128,96,128]{2,1,0:T(8,128)(2,1)S(1)}, bf16[128,96,128]{2,1,0:T(8,128)(2,1)}, u32[]{:S(2)}, u32[]{:S(2)}) collective-permute-start(bf16[128,96,128]{2,1,0:T(8,128)(2,1)S(1)} %get-tuple-element.27), channel_id=1, source_target_pairs={{0,15},{1,0},{2,1},{3,2},{4,3},{5,4},{6,5},{7,6},{8,7},{9,8},{10,9... | collective-permute-start | bytes 9437192 | tf_op jit(solution)/shard_map/ppermute | solution.py:74
  27.5 2.2 shard_map.84
  30.7 2.2 copy-done.1
  34.4 5.5 %collective-permute-done.3 = bf16[32,128,128]{2,1,0:T(8,128)(2,1)} collective-permute-done((bf16[32,128,128]{2,1,0:T(8,128)(2,1)}, bf16[32,128,128]{2,1,0:T(8,128)(2,1)}, u32[]{:S(2)}, u32[]{:S(2)}) %collective-permute-start.3) | collective-permute-done | bytes 1048608 | tf_op jit(solution)/shard_map/ppermute | solution.py:74
  39.9 2.3 select_select_fusion.1
  46.2 39.5 %collective-permute-start.4 = (bf16[16,128,128]{2,1,0:T(8,128)(2,1)}, bf16[16,128,128]{2,1,0:T(8,128)(2,1)}, u32[]{:S(2)}, u32[]{:S(2)}) collective-permute-start(bf16[16,128,128]{2,1,0:T(8,128)(2,1)} %slice.37), channel_id=1, source_target_pairs={{0,128},{1,129},{2,130},{3,131},{4,132},{5,133},{6,134},{7,135},{1... | collective-permute-start | bytes 1572872 | tf_op jit(solution)/shard_map/ppermute | solution.py:74
  85.7 9.0 %collective-permute-done.6 = bf16[16,128,128]{2,1,0:T(8,128)(2,1)} collective-permute-done((bf16[16,128,128]{2,1,0:T(8,128)(2,1)}, bf16[16,128,128]{2,1,0:T(8,128)(2,1)}, u32[]{:S(2)}, u32[]{:S(2)}) %collective-permute-start.6) | collective-permute-done | bytes 524320 | tf_op jit(solution)/shard_map/ppermute | solution.py:74
  96.8 10.4 %collective-permute-start.5 = (bf16[16,128,128]{2,1,0:T(8,128)(2,1)S(1)}, bf16[16,128,128]{2,1,0:T(8,128)(2,1)S(1)}, u32[]{:S(2)}, u32[]{:S(2)}) collective-permute-start(bf16[16,128,128]{2,1,0:T(8,128)(2,1)S(1)} %get-tuple-element.50), channel_id=1, source_target_pairs={{0,16},{1,17},{2,18},{3,19},{4,20},{5,21},{6,22},{7,23},{8,24},{9,... | collective-permute-start | bytes 1572872 | tf_op jit(solution)/shard_map/ppermute | solution.py:74
  107.1 6.4 %collective-permute-start.10 = (bf16[128,16,128]{2,1,0:T(8,128)(2,1)}, bf16[128,16,128]{2,1,0:T(8,128)(2,1)S(1)}, u32[]{:S(2)}, u32[]{:S(2)}) collective-permute-start(bf16[128,16,128]{2,1,0:T(8,128)(2,1)} %collective-permute-done.9), channel_id=1, source_target_pairs={{2,3},{3,4},{4,5},{5,6},{6,7},{7,0},{0,1},{1,2},{10,11},{11,12},{1... | collective-permute-start | bytes 1572872 | tf_op jit(solution)/shard_map/ppermute | solution.py:74
  113.5 11.7 %collective-permute-done.10 = bf16[128,16,128]{2,1,0:T(8,128)(2,1)S(1)} collective-permute-done((bf16[128,16,128]{2,1,0:T(8,128)(2,1)}, bf16[128,16,128]{2,1,0:T(8,128)(2,1)S(1)}, u32[]{:S(2)}, u32[]{:S(2)}) %collective-permute-start.10) | collective-permute-done | bytes 524320 | tf_op jit(solution)/shard_map/ppermute | solution.py:74
  126.3 2.6 collective-permute-start.12
  131.4 3.4 %shard_map.85.refs_12_ = bf16[64,16,384]{2,1,0:T(8,128)(2,1)S(1)} custom-call(bf16[48,128,128]{2,1,0:T(8,128)(2,1)S(1)} %pad_maximum_fusion.x_ref, f32[1,128]{1,0:T(1,128)S(1)} %bitcast.24, f32[1,128]{1,0:T(1,128)S(1)} %bitcast.28, bf16[128,128]{1,0:T(8,128)(2,1)S(1)} %maximum_bitcast_fusion.wt_ref), custom_call_target="tpu_custom_call" | custom-call | flops 603979776 | bytes 3145728 | tf_op jit(solution)/shard_map/pallas_call | solution.py:156
  134.8 7.5 %collective-permute-done.12 = bf16[128,16,128]{2,1,0:T(8,128)(2,1)S(1)} collective-permute-done((bf16[128,16,128]{2,1,0:T(8,128)(2,1)}, bf16[128,16,128]{2,1,0:T(8,128)(2,1)S(1)}, u32[]{:S(2)}, u32[]{:S(2)}) %collective-permute-start.12) | collective-permute-done | bytes 524320 | tf_op jit(solution)/shard_map/ppermute | solution.py:74
  148.6 10.8 %collective-permute-done.16 = bf16[128,16,128]{2,1,0:T(8,128)(2,1)} collective-permute-done((bf16[128,16,128]{2,1,0:T(8,128)(2,1)S(1)}, bf16[128,16,128]{2,1,0:T(8,128)(2,1)}, u32[]{:S(2)}, u32[]{:S(2)}) %collective-permute-start.16) | collective-permute-done | bytes 524320 | tf_op jit(solution)/shard_map/ppermute | solution.py:74
  162.9 3.0 %collective-permute-done.13.refs_20_ = bf16[64,16,384]{2,1,0:T(8,128)(2,1)S(1)} collective-permute-done((bf16[64,16,384]{2,1,0:T(8,128)(2,1)S(1)}, bf16[64,16,384]{2,1,0:T(8,128)(2,1)S(1)}, u32[]{:S(2)}, u32[]{:S(2)}) %collective-permute-start.13) | collective-permute-done | bytes 786464 | tf_op jit(solution)/shard_map/ppermute | solution.py:74
  165.9 11.4 %collective-permute-start.18 = (bf16[128,96,128]{2,1,0:T(8,128)(2,1)}, bf16[128,96,128]{2,1,0:T(8,128)(2,1)}, u32[]{:S(2)}, u32[]{:S(2)}) collective-permute-start(bf16[128,96,128]{2,1,0:T(8,128)(2,1)} %collective-permute-done), channel_id=1, source_target_pairs={{0,15},{1,0},{2,1},{3,2},{4,3},{5,4},{6,5},{7,6},{8,7},{9,8},{10,9... | collective-permute-start | bytes 9437192 | tf_op jit(solution)/shard_map/ppermute | solution.py:74
  181.4 10.8 %collective-permute-done.22 = bf16[128,16,128]{2,1,0:T(8,128)(2,1)S(1)} collective-permute-done((bf16[128,16,128]{2,1,0:T(8,128)(2,1)S(1)}, bf16[128,16,128]{2,1,0:T(8,128)(2,1)S(1)}, u32[]{:S(2)}, u32[]{:S(2)}) %collective-permute-start.22) | collective-permute-done | bytes 524320 | tf_op jit(solution)/shard_map/ppermute | solution.py:74
  192.3 7.6 %collective-permute-done.21.refs_16_ = bf16[64,16,384]{2,1,0:T(8,128)(2,1)S(1)} collective-permute-done((bf16[64,16,384]{2,1,0:T(8,128)(2,1)S(1)}, bf16[64,16,384]{2,1,0:T(8,128)(2,1)S(1)}, u32[]{:S(2)}, u32[]{:S(2)}) %collective-permute-start.21) | collective-permute-done | bytes 786464 | tf_op jit(solution)/shard_map/ppermute | solution.py:74
  199.8 11.9 %collective-permute-done.20.refs_26_ = bf16[64,16,384]{2,1,0:T(8,128)(2,1)} collective-permute-done((bf16[64,16,384]{2,1,0:T(8,128)(2,1)S(1)}, bf16[64,16,384]{2,1,0:T(8,128)(2,1)}, u32[]{:S(2)}, u32[]{:S(2)}) %collective-permute-start.20) | collective-permute-done | bytes 786464 | tf_op jit(solution)/shard_map/ppermute | solution.py:74
  215.9 14.2 %collective-permute-done.25 = bf16[128,16,128]{2,1,0:T(8,128)(2,1)S(1)} collective-permute-done((bf16[128,16,128]{2,1,0:T(8,128)(2,1)S(1)}, bf16[128,16,128]{2,1,0:T(8,128)(2,1)S(1)}, u32[]{:S(2)}, u32[]{:S(2)}) %collective-permute-start.25) | collective-permute-done | bytes 524320 | tf_op jit(solution)/shard_map/ppermute | solution.py:74
  230.2 4.9 %collective-permute-done.23.refs_24_ = bf16[64,16,384]{2,1,0:T(8,128)(2,1)} collective-permute-done((bf16[64,16,384]{2,1,0:T(8,128)(2,1)S(1)}, bf16[64,16,384]{2,1,0:T(8,128)(2,1)}, u32[]{:S(2)}, u32[]{:S(2)}) %collective-permute-start.23) | collective-permute-done | bytes 786464 | tf_op jit(solution)/shard_map/ppermute | solution.py:74
  237.0 28.8 %collective-permute-done.24 = bf16[128,16,128]{2,1,0:T(8,128)(2,1)} collective-permute-done((bf16[128,16,128]{2,1,0:T(8,128)(2,1)}, bf16[128,16,128]{2,1,0:T(8,128)(2,1)}, u32[]{:S(2)}, u32[]{:S(2)}) %collective-permute-start.24) | collective-permute-done | bytes 524320 | tf_op jit(solution)/shard_map/ppermute | solution.py:74
  267.2 21.7 %shard_map.86 = bf16[128,128,128]{2,1,0:T(8,128)(2,1)} custom-call(s32[2]{0:T(128)} %pad_add_fusion.place_ref, bf16[2,64,96,128]{3,2,1,0:T(8,128)(2,1)} %bitcast.16, bf16[2,64,96,128]{3,2,1,0:T(8,128)(2,1)} %bitcast.6.refs_1_, bf16[2,64,96,128]{3,2,1,0:T(8,128)(2,1)} %bitcast.8.refs_2_, f32[96,128,128]{2,1,0:T(8,128)} %get-tuple-element.41.refs_3_, ...), custom_call_target="tpu_custom_call" | custom-call | flops 2147483648 | bytes 39845888 | tf_op jit(solution)/shard_map/pallas_call | solution.py:241
  (132 shorter events, 42.8 us)
Async XLA Ops:
  14.2 111.0 %collective-permute-start = (bf16[128,96,128]{2,1,0:T(8,128)(2,1)S(1)}, bf16[128,96,128]{2,1,0:T(8,128)(2,1)}, u32[]{:S(2)}, u32[]{:S(2)}) collective-permute-start(bf16[128,96,128]{2,1,0:T(8,128)(2,1)S(1)} %get-tuple-element.27), channel_id=1, source_target_pairs={{0,15},{1,0},{2,1},{3,2},{4,3},{5,4},{6,5},{7,6},{8,7},{9,8},{10,9... | collective-permute-start | bytes 9437192 | tf_op jit(solution)/shard_map/ppermute | solution.py:74
  22.8 17.1 %collective-permute-start.3 = (bf16[32,128,128]{2,1,0:T(8,128)(2,1)}, bf16[32,128,128]{2,1,0:T(8,128)(2,1)}, u32[]{:S(2)}, u32[]{:S(2)}) collective-permute-start(bf16[32,128,128]{2,1,0:T(8,128)(2,1)} %get-tuple-element.53), channel_id=1, source_target_pairs={{0,32},{1,33},{2,34},{17,49},{18,50},{19,51},{34,2},{35,3},{36,4},... | collective-permute-start | bytes 3145736 | tf_op jit(solution)/shard_map/ppermute | solution.py:74
  30.7 55.0 %collective-permute-start.7 = (bf16[128,16,128]{2,1,0:T(8,128)(2,1)}, bf16[128,16,128]{2,1,0:T(8,128)(2,1)}, u32[]{:S(2)}, u32[]{:S(2)}) collective-permute-start(bf16[128,16,128]{2,1,0:T(8,128)(2,1)} %get-tuple-element.29), channel_id=1, source_target_pairs={{0,1},{1,2},{2,3},{3,4},{4,5},{5,6},{6,7},{7,0},{8,9},{9,10},{10,1... | collective-permute-start | bytes 1572872 | tf_op jit(solution)/shard_map/ppermute | solution.py:74
  44.9 49.8 %collective-permute-start.6 = (bf16[16,128,128]{2,1,0:T(8,128)(2,1)}, bf16[16,128,128]{2,1,0:T(8,128)(2,1)}, u32[]{:S(2)}, u32[]{:S(2)}) collective-permute-start(bf16[16,128,128]{2,1,0:T(8,128)(2,1)} %slice.39), channel_id=1, source_target_pairs={{2,130},{4,132},{6,134},{8,136},{19,147},{21,149},{23,151},{25,153... | collective-permute-start | bytes 1572872 | tf_op jit(solution)/shard_map/ppermute | solution.py:74
  46.2 48.5 %collective-permute-start.4 = (bf16[16,128,128]{2,1,0:T(8,128)(2,1)}, bf16[16,128,128]{2,1,0:T(8,128)(2,1)}, u32[]{:S(2)}, u32[]{:S(2)}) collective-permute-start(bf16[16,128,128]{2,1,0:T(8,128)(2,1)} %slice.37), channel_id=1, source_target_pairs={{0,128},{1,129},{2,130},{3,131},{4,132},{5,133},{6,134},{7,135},{1... | collective-permute-start | bytes 1572872 | tf_op jit(solution)/shard_map/ppermute | solution.py:74
  85.7 21.4 %collective-permute-start.9 = (bf16[128,16,128]{2,1,0:T(8,128)(2,1)}, bf16[128,16,128]{2,1,0:T(8,128)(2,1)}, u32[]{:S(2)}, u32[]{:S(2)}) collective-permute-start(bf16[128,16,128]{2,1,0:T(8,128)(2,1)} %collective-permute-done.7), channel_id=1, source_target_pairs={{1,2},{2,3},{3,4},{4,5},{5,6},{6,7},{7,0},{0,1},{9,10},{10,11},{11... | collective-permute-start | bytes 1572872 | tf_op jit(solution)/shard_map/ppermute | solution.py:74
  96.2 17.4 %collective-permute-start.8 = (bf16[16,128,128]{2,1,0:T(8,128)(2,1)S(1)}, bf16[16,128,128]{2,1,0:T(8,128)(2,1)}, u32[]{:S(2)}, u32[]{:S(2)}) collective-permute-start(bf16[16,128,128]{2,1,0:T(8,128)(2,1)S(1)} %get-tuple-element.31), channel_id=1, source_target_pairs={{0,14},{1,16},{2,0},{3,18},{4,2},{5,20},{6,4},{7,22},{8,6},{9,24},... | collective-permute-start | bytes 1572872 | tf_op jit(solution)/shard_map/ppermute | solution.py:74
  96.8 16.8 %collective-permute-start.5 = (bf16[16,128,128]{2,1,0:T(8,128)(2,1)S(1)}, bf16[16,128,128]{2,1,0:T(8,128)(2,1)S(1)}, u32[]{:S(2)}, u32[]{:S(2)}) collective-permute-start(bf16[16,128,128]{2,1,0:T(8,128)(2,1)S(1)} %get-tuple-element.50), channel_id=1, source_target_pairs={{0,16},{1,17},{2,18},{3,19},{4,20},{5,21},{6,22},{7,23},{8,24},{9,... | collective-permute-start | bytes 1572872 | tf_op jit(solution)/shard_map/ppermute | solution.py:74
  107.1 18.1 %collective-permute-start.10 = (bf16[128,16,128]{2,1,0:T(8,128)(2,1)}, bf16[128,16,128]{2,1,0:T(8,128)(2,1)S(1)}, u32[]{:S(2)}, u32[]{:S(2)}) collective-permute-start(bf16[128,16,128]{2,1,0:T(8,128)(2,1)} %collective-permute-done.9), channel_id=1, source_target_pairs={{2,3},{3,4},{4,5},{5,6},{6,7},{7,0},{0,1},{1,2},{10,11},{11,12},{1... | collective-permute-start | bytes 1572872 | tf_op jit(solution)/shard_map/ppermute | solution.py:74
  126.3 16.0 %collective-permute-start.12 = (bf16[128,16,128]{2,1,0:T(8,128)(2,1)}, bf16[128,16,128]{2,1,0:T(8,128)(2,1)S(1)}, u32[]{:S(2)}, u32[]{:S(2)}) collective-permute-start(bf16[128,16,128]{2,1,0:T(8,128)(2,1)} %copy-done.32), channel_id=1, source_target_pairs={{3,4},{4,5},{5,6},{6,7},{7,0},{0,1},{1,2},{2,3},{11,12},{12,13},{1... | collective-permute-start | bytes 1572872 | tf_op jit(solution)/shard_map/ppermute | solution.py:74
  142.3 19.2 %collective-permute-start.15 = (bf16[64,16,384]{2,1,0:T(8,128)(2,1)S(1)}, bf16[64,16,384]{2,1,0:T(8,128)(2,1)S(1)}, u32[]{:S(2)}, u32[]{:S(2)}) collective-permute-start(bf16[64,16,384]{2,1,0:T(8,128)(2,1)S(1)} %shard_map.85.refs_12_), channel_id=1, source_target_pairs={{0,96},{1,97},{2,98},{3,99},{4,100},{5,101},{6,102},{7,103},{8,104... | collective-permute-start | bytes 2359304 | tf_op jit(solution)/shard_map/ppermute | solution.py:74
  143.9 19.0 %collective-permute-start.14 = (bf16[64,16,384]{2,1,0:T(8,128)(2,1)S(1)}, bf16[64,16,384]{2,1,0:T(8,128)(2,1)S(1)}, u32[]{:S(2)}, u32[]{:S(2)}) collective-permute-start(bf16[64,16,384]{2,1,0:T(8,128)(2,1)S(1)} %shard_map.85.refs_12_), channel_id=1, source_target_pairs={{0,32},{1,33},{2,34},{3,35},{4,36},{5,37},{6,38},{7,39},{8,40},{9,... | collective-permute-start | bytes 2359304 | tf_op jit(solution)/shard_map/ppermute | solution.py:74
  145.8 20.1 %collective-permute-start.13 = (bf16[64,16,384]{2,1,0:T(8,128)(2,1)S(1)}, bf16[64,16,384]{2,1,0:T(8,128)(2,1)S(1)}, u32[]{:S(2)}, u32[]{:S(2)}) collective-permute-start(bf16[64,16,384]{2,1,0:T(8,128)(2,1)S(1)} %shard_map.85.refs_12_), channel_id=1, source_target_pairs={{0,128},{1,129},{2,130},{3,131},{4,132},{5,133},{6,134},{7,135},{8... | collective-permute-start | bytes 2359304 | tf_op jit(solution)/shard_map/ppermute | solution.py:74
  165.9 99.9 %collective-permute-start.18 = (bf16[128,96,128]{2,1,0:T(8,128)(2,1)}, bf16[128,96,128]{2,1,0:T(8,128)(2,1)}, u32[]{:S(2)}, u32[]{:S(2)}) collective-permute-start(bf16[128,96,128]{2,1,0:T(8,128)(2,1)} %collective-permute-done), channel_id=1, source_target_pairs={{0,15},{1,0},{2,1},{3,2},{4,3},{5,4},{6,5},{7,6},{8,7},{9,8},{10,9... | collective-permute-start | bytes 9437192 | tf_op jit(solution)/shard_map/ppermute | solution.py:74
  177.3 34.4 %collective-permute-start.20 = (bf16[64,16,384]{2,1,0:T(8,128)(2,1)S(1)}, bf16[64,16,384]{2,1,0:T(8,128)(2,1)}, u32[]{:S(2)}, u32[]{:S(2)}) collective-permute-start(bf16[64,16,384]{2,1,0:T(8,128)(2,1)S(1)} %collective-permute-done.13.refs_20_), channel_id=1, source_target_pairs={{0,96},{1,97},{2,98},{3,99},{4,100},{5,101},{6,102},{7,103},{8,104... | collective-permute-start | bytes 2359304 | tf_op jit(solution)/shard_map/ppermute | solution.py:74
  177.8 22.0 %collective-permute-start.21 = (bf16[64,16,384]{2,1,0:T(8,128)(2,1)S(1)}, bf16[64,16,384]{2,1,0:T(8,128)(2,1)S(1)}, u32[]{:S(2)}, u32[]{:S(2)}) collective-permute-start(bf16[64,16,384]{2,1,0:T(8,128)(2,1)S(1)} %shard_map.85.refs_12_), channel_id=1, source_target_pairs={{0,64},{1,65},{2,66},{3,67},{4,68},{5,69},{6,70},{7,71},{8,72},{9,... | collective-permute-start | bytes 2359304 | tf_op jit(solution)/shard_map/ppermute | solution.py:74
  179.7 33.9 %collective-permute-start.19 = (bf16[64,16,384]{2,1,0:T(8,128)(2,1)S(1)}, bf16[64,16,384]{2,1,0:T(8,128)(2,1)}, u32[]{:S(2)}, u32[]{:S(2)}) collective-permute-start(bf16[64,16,384]{2,1,0:T(8,128)(2,1)S(1)} %collective-permute-done.13.refs_20_), channel_id=1, source_target_pairs={{0,32},{1,33},{2,34},{3,35},{4,36},{5,37},{6,38},{7,39},{8,40},{9,... | collective-permute-start | bytes 2359304 | tf_op jit(solution)/shard_map/ppermute | solution.py:74
  192.2 21.3 %collective-permute-start.26 = (bf16[64,16,384]{2,1,0:T(8,128)(2,1)S(1)}, bf16[64,16,384]{2,1,0:T(8,128)(2,1)S(1)}, u32[]{:S(2)}, u32[]{:S(2)}) collective-permute-start(bf16[64,16,384]{2,1,0:T(8,128)(2,1)S(1)} %shard_map.85.refs_12_), channel_id=1, source_target_pairs={{0,16},{1,17},{2,18},{3,19},{4,20},{5,21},{6,22},{7,23},{8,24},{9,... | collective-permute-start | bytes 2359304 | tf_op jit(solution)/shard_map/ppermute | solution.py:74
  213.5 21.6 %collective-permute-start.23 = (bf16[64,16,384]{2,1,0:T(8,128)(2,1)S(1)}, bf16[64,16,384]{2,1,0:T(8,128)(2,1)}, u32[]{:S(2)}, u32[]{:S(2)}) collective-permute-start(bf16[64,16,384]{2,1,0:T(8,128)(2,1)S(1)} %collective-permute-done.13.refs_20_), channel_id=1, source_target_pairs={{0,64},{1,65},{2,66},{3,67},{4,68},{5,69},{6,70},{7,71},{8,72},{9,... | collective-permute-start | bytes 2359304 | tf_op jit(solution)/shard_map/ppermute | solution.py:74
  214.1 16.1 %collective-permute-start.25 = (bf16[128,16,128]{2,1,0:T(8,128)(2,1)S(1)}, bf16[128,16,128]{2,1,0:T(8,128)(2,1)S(1)}, u32[]{:S(2)}, u32[]{:S(2)}) collective-permute-start(bf16[128,16,128]{2,1,0:T(8,128)(2,1)S(1)} %collective-permute-done.22), channel_id=1, source_target_pairs={{14,15},{15,0},{0,1},{1,2},{2,3},{3,4},{4,5},{5,6},{6,7},{7,8},{8,... | collective-permute-start | bytes 1572872 | tf_op jit(solution)/shard_map/ppermute | solution.py:74
  214.1 21.0 %collective-permute-start.28 = (bf16[64,16,384]{2,1,0:T(8,128)(2,1)S(1)}, bf16[64,16,384]{2,1,0:T(8,128)(2,1)S(1)}, u32[]{:S(2)}, u32[]{:S(2)}) collective-permute-start(bf16[64,16,384]{2,1,0:T(8,128)(2,1)S(1)} %collective-permute-done.21.refs_16_), channel_id=1, source_target_pairs={{0,16},{1,17},{2,18},{3,19},{4,20},{5,21},{6,22},{7,23},{8,24},{9,... | collective-permute-start | bytes 2359304 | tf_op jit(solution)/shard_map/ppermute | solution.py:74
  215.8 21.2 %collective-permute-start.33 = (bf16[64,16,384]{2,1,0:T(8,128)(2,1)}, bf16[64,16,384]{2,1,0:T(8,128)(2,1)}, u32[]{:S(2)}, u32[]{:S(2)}) collective-permute-start(bf16[64,16,384]{2,1,0:T(8,128)(2,1)} %collective-permute-done.20.refs_26_), channel_id=1, source_target_pairs={{0,16},{1,17},{2,18},{3,19},{4,20},{5,21},{6,22},{7,23},{8,24},{9,... | collective-permute-start | bytes 2359304 | tf_op jit(solution)/shard_map/ppermute | solution.py:74
  235.1 30.7 %collective-permute-start.32 = (bf16[64,16,384]{2,1,0:T(8,128)(2,1)}, bf16[64,16,384]{2,1,0:T(8,128)(2,1)}, u32[]{:S(2)}, u32[]{:S(2)}) collective-permute-start(bf16[64,16,384]{2,1,0:T(8,128)(2,1)} %collective-permute-done.23.refs_24_), channel_id=1, source_target_pairs={{0,16},{1,17},{2,18},{3,19},{4,20},{5,21},{6,22},{7,23},{8,24},{9,... | collective-permute-start | bytes 2359304 | tf_op jit(solution)/shard_map/ppermute | solution.py:74
  236.1 29.7 %collective-permute-start.24 = (bf16[128,16,128]{2,1,0:T(8,128)(2,1)}, bf16[128,16,128]{2,1,0:T(8,128)(2,1)}, u32[]{:S(2)}, u32[]{:S(2)}) collective-permute-start(bf16[128,16,128]{2,1,0:T(8,128)(2,1)} %collective-permute-done.16), channel_id=1, source_target_pairs={{0,15},{1,0},{2,1},{3,2},{4,3},{5,4},{6,5},{7,6},{8,7},{9,8},{10,9... | collective-permute-start | bytes 1572872 | tf_op jit(solution)/shard_map/ppermute | solution.py:74
  (43 other events, 1173.3 us)

commit v6 on v3

--- a/solution.py
+++ b/solution.py
@@ -12,7 +12,7 @@
 NT = (((1,), (1,)), ((), ()))
 TN = (((0,), (0,)), ((), ()))
 AXES = ("row", "col")
-BIG, SMALL = (0, 96), (96, 32)
+BIG, SMALL = (0, 112), (112, 16)
 
 
 def place(r, c):
@@ -308,9 +308,9 @@
     got[5], got[7] = exchange(stage, 1), exchange(stage, 3)
     got[2] = exchange(after(mine, stage), 2)
     big_twice = one_back(after(big_once, stage))
-    small_twice = one_back(after(small_once, got[5], got[2]))
     stage = after(got[4], got[5], got[7], got[2])
     got[6] = exchange(stage, 2)
+    small_twice = one_back(after(small_once, got[6]))
     rights = [mine, swapped_mine]
     for n in range(1, 8):
         rights += [got[n], send(got[n], everyone(swap))]

time: 287 us -> 291 us (1.014)
  starting transfers between devices: 119 us -> 123 us
  waiting for transfers between devices: 108 us -> 111 us
    ppermute x27, starting transfers between devices: 119 us -> 123 us  [send(): return lax.ppermute(value, AXES, pairs)]
    ppermute x27, waiting for transfers between devices: 108 us -> 111 us  [send(): return lax.ppermute(value, AXES, pairs)]
    unnamed x59 -> x55, local copies, waits for them, and re-layouts: 4.18 us -> 6.46 us
  transfers between devices with their start and end apart: 27 -> 27, of which waited for: 13 -> 10; matrix products, arithmetic and copies ran while one was open for 4% -> 2% of each run, Pallas kernels for 3% -> 0%
where the time goes in v6:
time: 291 us; the launch traced here: 290 us
  starting transfers between devices  123 us (42%)
  waiting for transfers between devices  111 us (38%)
  Pallas kernels  39.4 us (14%)
  local copies, waits for them, and re-layouts  11.5 us (4%)
  other arithmetic  4.35 us (1%)
    ppermute x27, starting transfers between devices, send(): return lax.ppermute(value, AXES, pairs)  123 us
    ppermute x27, waiting for transfers between devices, send(): return lax.ppermute(value, AXES, pairs)  111 us
    pallas_call x1, Pallas kernels, final(): pl.pallas_call(functools.partial(final_kernel, subs=subs, aliased=len(ali...  22 us
    pallas_call x2, Pallas kernels, left_and_gate(): pl.pallas_call(left_kernel, out_shape=[jax.ShapeDtypeStruct((128, rows, 1...  14 us
    unnamed x55, local copies, waits for them, and re-layouts  6.46 us
  transfers between devices with their start and end apart: 27, of which 10 were waited for; matrix products, arithmetic and copies ran while one was open for 2% of the time, Pallas kernels for 0%

profile of v6, /device:TPU:8, one launch (start us, length us, event | category | flops | bytes accessed | tf_op | source)
XLA Modules:
  0.0 290.2 jit_solution(17961895057275352951)
XLA Ops:
  3.0 12.6 %shard_map.82 = (bf16[128,112,128]{2,1,0:T(8,128)(2,1)}, f32[112,128,128]{2,1,0:T(8,128)}) custom-call(bf16[128,128,128]{2,1,0:T(8,128)(2,1)} %x_ref.3, f32[1,128]{1,0:T(1,128)S(1)} %bitcast.16, f32[1,128]{1,0:T(1,128)S(1)} %bitcast.19, bf16[256,128]{1,0:T(8,128)(2,1)S(1)} %bitcast.14, bf16[128,128]{1,0:T(8,128)(2,1)S(1)} %copy-done.5), custom_call_target="tpu_custom_call" | custom-call | flops 2818572288 | bytes 14680064 | tf_op jit(solution)/shard_map/pallas_call | solution.py:102
  15.6 6.9 %collective-permute-start = (bf16[128,112,128]{2,1,0:T(8,128)(2,1)}, bf16[128,112,128]{2,1,0:T(8,128)(2,1)}, u32[]{:S(2)}, u32[]{:S(2)}) collective-permute-start(bf16[128,112,128]{2,1,0:T(8,128)(2,1)} %get-tuple-element.17), channel_id=1, source_target_pairs={{0,15},{1,0},{2,1},{3,2},{4,3},{5,4},{6,5},{7,6},{8,7},{9,8},{10,9... | collective-permute-start | bytes 11010056 | tf_op jit(solution)/shard_map/ppermute | solution.py:62
  22.5 1.7 fusion.1
  25.5 1.7 collective-permute-start.2
  28.8 2.2 copy-done.1
  32.4 8.6 %collective-permute-done.3 = bf16[32,128,128]{2,1,0:T(8,128)(2,1)S(1)} collective-permute-done((bf16[32,128,128]{2,1,0:T(8,128)(2,1)}, bf16[32,128,128]{2,1,0:T(8,128)(2,1)S(1)}, u32[]{:S(2)}, u32[]{:S(2)}) %collective-permute-start.3) | collective-permute-done | bytes 1048608 | tf_op jit(solution)/shard_map/ppermute | solution.py:62
  42.0 2.3 select_select_fusion.1
  46.5 38.7 %collective-permute-start.4 = (bf16[16,128,128]{2,1,0:T(8,128)(2,1)S(1)}, bf16[16,128,128]{2,1,0:T(8,128)(2,1)}, u32[]{:S(2)}, u32[]{:S(2)}) collective-permute-start(bf16[16,128,128]{2,1,0:T(8,128)(2,1)S(1)} %slice.37), channel_id=1, source_target_pairs={{0,128},{1,129},{2,130},{3,131},{4,132},{5,133},{6,134},{7,135},{1... | collective-permute-start | bytes 1572872 | tf_op jit(solution)/shard_map/ppermute | solution.py:62
  85.2 8.8 %collective-permute-done.6 = bf16[16,128,128]{2,1,0:T(8,128)(2,1)} collective-permute-done((bf16[16,128,128]{2,1,0:T(8,128)(2,1)}, bf16[16,128,128]{2,1,0:T(8,128)(2,1)}, u32[]{:S(2)}, u32[]{:S(2)}) %collective-permute-start.6) | collective-permute-done | bytes 524320 | tf_op jit(solution)/shard_map/ppermute | solution.py:62
  95.3 24.5 %collective-permute-start.5 = (bf16[16,128,128]{2,1,0:T(8,128)(2,1)S(1)}, bf16[16,128,128]{2,1,0:T(8,128)(2,1)S(1)}, u32[]{:S(2)}, u32[]{:S(2)}) collective-permute-start(bf16[16,128,128]{2,1,0:T(8,128)(2,1)S(1)} %get-tuple-element.30), channel_id=1, source_target_pairs={{0,16},{1,17},{2,18},{3,19},{4,20},{5,21},{6,22},{7,23},{8,24},{9,... | collective-permute-start | bytes 1572872 | tf_op jit(solution)/shard_map/ppermute | solution.py:62
  121.3 4.6 %collective-permute-start.8 = (bf16[16,128,128]{2,1,0:T(8,128)(2,1)S(1)}, bf16[16,128,128]{2,1,0:T(8,128)(2,1)S(1)}, u32[]{:S(2)}, u32[]{:S(2)}) collective-permute-start(bf16[16,128,128]{2,1,0:T(8,128)(2,1)S(1)} %collective-permute-done.7), channel_id=1, source_target_pairs={{0,16},{1,17},{2,18},{3,19},{4,20},{5,21},{6,22},{7,23},{8,24},{9,... | collective-permute-start | bytes 1572872 | tf_op jit(solution)/shard_map/ppermute | solution.py:62
  127.7 3.4 %shard_map.84.refs_8_ = bf16[64,16,384]{2,1,0:T(8,128)(2,1)S(1)} custom-call(bf16[48,128,128]{2,1,0:T(8,128)(2,1)S(1)} %pad_maximum_fusion.x_ref, f32[1,128]{1,0:T(1,128)S(1)} %bitcast.18, f32[1,128]{1,0:T(1,128)S(1)} %bitcast.21, bf16[128,128]{1,0:T(8,128)(2,1)S(1)} %maximum_bitcast_fusion.wt_ref), custom_call_target="tpu_custom_call" | custom-call | flops 603979776 | bytes 3145728 | tf_op jit(solution)/shard_map/pallas_call | solution.py:144
  132.9 1.9 collective-permute-start.10
  134.8 10.1 %collective-permute-start.12 = (bf16[128,16,128]{2,1,0:T(8,128)(2,1)S(1)}, bf16[128,16,128]{2,1,0:T(8,128)(2,1)S(1)}, u32[]{:S(2)}, u32[]{:S(2)}) collective-permute-start(bf16[128,16,128]{2,1,0:T(8,128)(2,1)S(1)} %get-tuple-element.21), channel_id=1, source_target_pairs={{0,15},{1,0},{2,1},{3,2},{4,3},{5,4},{6,5},{7,6},{8,7},{9,8},{10,9... | collective-permute-start | bytes 1572872 | tf_op jit(solution)/shard_map/ppermute | solution.py:62
  144.9 11.2 %collective-permute-done.12 = bf16[128,16,128]{2,1,0:T(8,128)(2,1)S(1)} collective-permute-done((bf16[128,16,128]{2,1,0:T(8,128)(2,1)S(1)}, bf16[128,16,128]{2,1,0:T(8,128)(2,1)S(1)}, u32[]{:S(2)}, u32[]{:S(2)}) %collective-permute-start.12) | collective-permute-done | bytes 524320 | tf_op jit(solution)/shard_map/ppermute | solution.py:62
  156.1 20.7 %collective-permute-start.13 = (bf16[128,112,128]{2,1,0:T(8,128)(2,1)}, bf16[128,112,128]{2,1,0:T(8,128)(2,1)}, u32[]{:S(2)}, u32[]{:S(2)}) collective-permute-start(bf16[128,112,128]{2,1,0:T(8,128)(2,1)} %collective-permute-done), channel_id=1, source_target_pairs={{0,15},{1,0},{2,1},{3,2},{4,3},{5,4},{6,5},{7,6},{8,7},{9,8},{10,9... | collective-permute-start | bytes 11010056 | tf_op jit(solution)/shard_map/ppermute | solution.py:62
  176.9 1.7 collective-permute-start.15
  178.6 3.0 %collective-permute-start.14 = (bf16[64,16,384]{2,1,0:T(8,128)(2,1)S(1)}, bf16[64,16,384]{2,1,0:T(8,128)(2,1)}, u32[]{:S(2)}, u32[]{:S(2)}) collective-permute-start(bf16[64,16,384]{2,1,0:T(8,128)(2,1)S(1)} %collective-permute-done.9.refs_16_), channel_id=1, source_target_pairs={{0,32},{1,33},{2,34},{3,35},{4,36},{5,37},{6,38},{7,39},{8,40},{9,... | collective-permute-start | bytes 2359304 | tf_op jit(solution)/shard_map/ppermute | solution.py:62
  181.6 17.3 %collective-permute-done.16.refs_12_ = bf16[64,16,384]{2,1,0:T(8,128)(2,1)S(1)} collective-permute-done((bf16[64,16,384]{2,1,0:T(8,128)(2,1)S(1)}, bf16[64,16,384]{2,1,0:T(8,128)(2,1)S(1)}, u32[]{:S(2)}, u32[]{:S(2)}) %collective-permute-start.16) | collective-permute-done | bytes 786464 | tf_op jit(solution)/shard_map/ppermute | solution.py:62
  198.9 13.5 %collective-permute-done.15.refs_22_ = bf16[64,16,384]{2,1,0:T(8,128)(2,1)} collective-permute-done((bf16[64,16,384]{2,1,0:T(8,128)(2,1)S(1)}, bf16[64,16,384]{2,1,0:T(8,128)(2,1)}, u32[]{:S(2)}, u32[]{:S(2)}) %collective-permute-start.15) | collective-permute-done | bytes 786464 | tf_op jit(solution)/shard_map/ppermute | solution.py:62
  212.9 1.8 collective-permute-start.17
  216.0 18.1 %collective-permute-done.17.refs_20_ = bf16[64,16,384]{2,1,0:T(8,128)(2,1)} collective-permute-done((bf16[64,16,384]{2,1,0:T(8,128)(2,1)S(1)}, bf16[64,16,384]{2,1,0:T(8,128)(2,1)}, u32[]{:S(2)}, u32[]{:S(2)}) %collective-permute-start.17) | collective-permute-done | bytes 786464 | tf_op jit(solution)/shard_map/ppermute | solution.py:62
  236.1 30.4 %collective-permute-done.18 = bf16[128,16,128]{2,1,0:T(8,128)(2,1)S(1)} collective-permute-done((bf16[128,16,128]{2,1,0:T(8,128)(2,1)S(1)}, bf16[128,16,128]{2,1,0:T(8,128)(2,1)S(1)}, u32[]{:S(2)}, u32[]{:S(2)}) %collective-permute-start.18) | collective-permute-done | bytes 524320 | tf_op jit(solution)/shard_map/ppermute | solution.py:62
  268.0 22.0 %shard_map.85 = bf16[128,128,128]{2,1,0:T(8,128)(2,1)} custom-call(s32[2]{0:T(128)} %pad_add_fusion.place_ref, bf16[2,64,112,128]{3,2,1,0:T(8,128)(2,1)} %bitcast.5.refs_0_, bf16[2,64,112,128]{3,2,1,0:T(8,128)(2,1)} %bitcast.6.refs_1_, bf16[2,64,112,128]{3,2,1,0:T(8,128)(2,1)} %bitcast.8.refs_2_, f32[112,128,128]{2,1,0:T(8,128)} %get-tuple-element.24.refs_3_, ...), custom_call_target="tpu_custom_call" | custom-call | flops 2147483648 | bytes 39845888 | tf_op jit(solution)/shard_map/pallas_call | solution.py:229
  (103 shorter events, 22.1 us)
Async XLA Ops:
  15.6 105.7 %collective-permute-start = (bf16[128,112,128]{2,1,0:T(8,128)(2,1)}, bf16[128,112,128]{2,1,0:T(8,128)(2,1)}, u32[]{:S(2)}, u32[]{:S(2)}) collective-permute-start(bf16[128,112,128]{2,1,0:T(8,128)(2,1)} %get-tuple-element.17), channel_id=1, source_target_pairs={{0,15},{1,0},{2,1},{3,2},{4,3},{5,4},{6,5},{7,6},{8,7},{9,8},{10,9... | collective-permute-start | bytes 11010056 | tf_op jit(solution)/shard_map/ppermute | solution.py:62
  24.2 16.9 %collective-permute-start.3 = (bf16[32,128,128]{2,1,0:T(8,128)(2,1)}, bf16[32,128,128]{2,1,0:T(8,128)(2,1)S(1)}, u32[]{:S(2)}, u32[]{:S(2)}) collective-permute-start(bf16[32,128,128]{2,1,0:T(8,128)(2,1)} %get-tuple-element.33), channel_id=1, source_target_pairs={{0,32},{1,33},{2,34},{17,49},{18,50},{19,51},{34,2},{35,3},{36,4},... | collective-permute-start | bytes 3145736 | tf_op jit(solution)/shard_map/ppermute | solution.py:62
  25.5 15.6 %collective-permute-start.2 = (bf16[32,128,128]{2,1,0:T(8,128)(2,1)}, bf16[32,128,128]{2,1,0:T(8,128)(2,1)}, u32[]{:S(2)}, u32[]{:S(2)}) collective-permute-start(bf16[32,128,128]{2,1,0:T(8,128)(2,1)} %get-tuple-element.34), channel_id=1, source_target_pairs={{0,64},{1,65},{2,66},{17,81},{18,82},{19,83},{34,98},{35,99},{36,1... | collective-permute-start | bytes 3145736 | tf_op jit(solution)/shard_map/ppermute | solution.py:62
  27.2 14.9 %collective-permute-start.1 = (bf16[32,128,128]{2,1,0:T(8,128)(2,1)S(1)}, bf16[32,128,128]{2,1,0:T(8,128)(2,1)}, u32[]{:S(2)}, u32[]{:S(2)}) collective-permute-start(bf16[32,128,128]{2,1,0:T(8,128)(2,1)S(1)} %get-tuple-element.35), channel_id=1, source_target_pairs={{0,96},{1,97},{2,98},{17,113},{18,114},{19,115},{34,66},{35,67},{3... | collective-permute-start | bytes 3145736 | tf_op jit(solution)/shard_map/ppermute | solution.py:62
  45.2 48.7 %collective-permute-start.6 = (bf16[16,128,128]{2,1,0:T(8,128)(2,1)}, bf16[16,128,128]{2,1,0:T(8,128)(2,1)}, u32[]{:S(2)}, u32[]{:S(2)}) collective-permute-start(bf16[16,128,128]{2,1,0:T(8,128)(2,1)} %slice.39), channel_id=1, source_target_pairs={{2,130},{4,132},{6,134},{8,136},{19,147},{21,149},{23,151},{25,153... | collective-permute-start | bytes 1572872 | tf_op jit(solution)/shard_map/ppermute | solution.py:62
  46.5 47.4 %collective-permute-start.4 = (bf16[16,128,128]{2,1,0:T(8,128)(2,1)S(1)}, bf16[16,128,128]{2,1,0:T(8,128)(2,1)}, u32[]{:S(2)}, u32[]{:S(2)}) collective-permute-start(bf16[16,128,128]{2,1,0:T(8,128)(2,1)S(1)} %slice.37), channel_id=1, source_target_pairs={{0,128},{1,129},{2,130},{3,131},{4,132},{5,133},{6,134},{7,135},{1... | collective-permute-start | bytes 1572872 | tf_op jit(solution)/shard_map/ppermute | solution.py:62
  95.2 24.6 %collective-permute-start.7 = (bf16[16,128,128]{2,1,0:T(8,128)(2,1)S(1)}, bf16[16,128,128]{2,1,0:T(8,128)(2,1)S(1)}, u32[]{:S(2)}, u32[]{:S(2)}) collective-permute-start(bf16[16,128,128]{2,1,0:T(8,128)(2,1)S(1)} %get-tuple-element.29), channel_id=1, source_target_pairs={{0,14},{1,16},{2,0},{3,18},{4,2},{5,20},{6,4},{7,22},{8,6},{9,24},... | collective-permute-start | bytes 1572872 | tf_op jit(solution)/shard_map/ppermute | solution.py:62
  95.3 26.1 %collective-permute-start.5 = (bf16[16,128,128]{2,1,0:T(8,128)(2,1)S(1)}, bf16[16,128,128]{2,1,0:T(8,128)(2,1)S(1)}, u32[]{:S(2)}, u32[]{:S(2)}) collective-permute-start(bf16[16,128,128]{2,1,0:T(8,128)(2,1)S(1)} %get-tuple-element.30), channel_id=1, source_target_pairs={{0,16},{1,17},{2,18},{3,19},{4,20},{5,21},{6,22},{7,23},{8,24},{9,... | collective-permute-start | bytes 1572872 | tf_op jit(solution)/shard_map/ppermute | solution.py:62
  131.2 24.9 %collective-permute-start.11 = (bf16[64,16,384]{2,1,0:T(8,128)(2,1)S(1)}, bf16[64,16,384]{2,1,0:T(8,128)(2,1)S(1)}, u32[]{:S(2)}, u32[]{:S(2)}) collective-permute-start(bf16[64,16,384]{2,1,0:T(8,128)(2,1)S(1)} %shard_map.84.refs_8_), channel_id=1, source_target_pairs={{0,96},{1,97},{2,98},{3,99},{4,100},{5,101},{6,102},{7,103},{8,104... | collective-permute-start | bytes 2359304 | tf_op jit(solution)/shard_map/ppermute | solution.py:62
  132.9 23.2 %collective-permute-start.10 = (bf16[64,16,384]{2,1,0:T(8,128)(2,1)S(1)}, bf16[64,16,384]{2,1,0:T(8,128)(2,1)S(1)}, u32[]{:S(2)}, u32[]{:S(2)}) collective-permute-start(bf16[64,16,384]{2,1,0:T(8,128)(2,1)S(1)} %shard_map.84.refs_8_), channel_id=1, source_target_pairs={{0,32},{1,33},{2,34},{3,35},{4,36},{5,37},{6,38},{7,39},{8,40},{9,... | collective-permute-start | bytes 2359304 | tf_op jit(solution)/shard_map/ppermute | solution.py:62
  134.7 21.4 %collective-permute-start.9 = (bf16[64,16,384]{2,1,0:T(8,128)(2,1)S(1)}, bf16[64,16,384]{2,1,0:T(8,128)(2,1)S(1)}, u32[]{:S(2)}, u32[]{:S(2)}) collective-permute-start(bf16[64,16,384]{2,1,0:T(8,128)(2,1)S(1)} %shard_map.84.refs_8_), channel_id=1, source_target_pairs={{0,128},{1,129},{2,130},{3,131},{4,132},{5,133},{6,134},{7,135},{8... | collective-permute-start | bytes 2359304 | tf_op jit(solution)/shard_map/ppermute | solution.py:62
  134.8 21.3 %collective-permute-start.12 = (bf16[128,16,128]{2,1,0:T(8,128)(2,1)S(1)}, bf16[128,16,128]{2,1,0:T(8,128)(2,1)S(1)}, u32[]{:S(2)}, u32[]{:S(2)}) collective-permute-start(bf16[128,16,128]{2,1,0:T(8,128)(2,1)S(1)} %get-tuple-element.21), channel_id=1, source_target_pairs={{0,15},{1,0},{2,1},{3,2},{4,3},{5,4},{6,5},{7,6},{8,7},{9,8},{10,9... | collective-permute-start | bytes 1572872 | tf_op jit(solution)/shard_map/ppermute | solution.py:62
  156.1 110.4 %collective-permute-start.13 = (bf16[128,112,128]{2,1,0:T(8,128)(2,1)}, bf16[128,112,128]{2,1,0:T(8,128)(2,1)}, u32[]{:S(2)}, u32[]{:S(2)}) collective-permute-start(bf16[128,112,128]{2,1,0:T(8,128)(2,1)} %collective-permute-done), channel_id=1, source_target_pairs={{0,15},{1,0},{2,1},{3,2},{4,3},{5,4},{6,5},{7,6},{8,7},{9,8},{10,9... | collective-permute-start | bytes 11010056 | tf_op jit(solution)/shard_map/ppermute | solution.py:62
  176.9 22.0 %collective-permute-start.16 = (bf16[64,16,384]{2,1,0:T(8,128)(2,1)S(1)}, bf16[64,16,384]{2,1,0:T(8,128)(2,1)S(1)}, u32[]{:S(2)}, u32[]{:S(2)}) collective-permute-start(bf16[64,16,384]{2,1,0:T(8,128)(2,1)S(1)} %shard_map.84.refs_8_), channel_id=1, source_target_pairs={{0,64},{1,65},{2,66},{3,67},{4,68},{5,69},{6,70},{7,71},{8,72},{9,... | collective-permute-start | bytes 2359304 | tf_op jit(solution)/shard_map/ppermute | solution.py:62
  176.9 35.5 %collective-permute-start.15 = (bf16[64,16,384]{2,1,0:T(8,128)(2,1)S(1)}, bf16[64,16,384]{2,1,0:T(8,128)(2,1)}, u32[]{:S(2)}, u32[]{:S(2)}) collective-permute-start(bf16[64,16,384]{2,1,0:T(8,128)(2,1)S(1)} %collective-permute-done.9.refs_16_), channel_id=1, source_target_pairs={{0,96},{1,97},{2,98},{3,99},{4,100},{5,101},{6,102},{7,103},{8,104... | collective-permute-start | bytes 2359304 | tf_op jit(solution)/shard_map/ppermute | solution.py:62
  178.6 33.8 %collective-permute-start.14 = (bf16[64,16,384]{2,1,0:T(8,128)(2,1)S(1)}, bf16[64,16,384]{2,1,0:T(8,128)(2,1)}, u32[]{:S(2)}, u32[]{:S(2)}) collective-permute-start(bf16[64,16,384]{2,1,0:T(8,128)(2,1)S(1)} %collective-permute-done.9.refs_16_), channel_id=1, source_target_pairs={{0,32},{1,33},{2,34},{3,35},{4,36},{5,37},{6,38},{7,39},{8,40},{9,... | collective-permute-start | bytes 2359304 | tf_op jit(solution)/shard_map/ppermute | solution.py:62
  181.6 31.4 %collective-permute-start.19 = (bf16[64,16,384]{2,1,0:T(8,128)(2,1)S(1)}, bf16[64,16,384]{2,1,0:T(8,128)(2,1)S(1)}, u32[]{:S(2)}, u32[]{:S(2)}) collective-permute-start(bf16[64,16,384]{2,1,0:T(8,128)(2,1)S(1)} %shard_map.84.refs_8_), channel_id=1, source_target_pairs={{0,16},{1,17},{2,18},{3,19},{4,20},{5,21},{6,22},{7,23},{8,24},{9,... | collective-permute-start | bytes 2359304 | tf_op jit(solution)/shard_map/ppermute | solution.py:62
  198.9 15.9 %collective-permute-start.22 = (bf16[64,16,384]{2,1,0:T(8,128)(2,1)S(1)}, bf16[64,16,384]{2,1,0:T(8,128)(2,1)S(1)}, u32[]{:S(2)}, u32[]{:S(2)}) collective-permute-start(bf16[64,16,384]{2,1,0:T(8,128)(2,1)S(1)} %collective-permute-done.11.refs_14_), channel_id=1, source_target_pairs={{0,16},{1,17},{2,18},{3,19},{4,20},{5,21},{6,22},{7,23},{8,24},{9,... | collective-permute-start | bytes 2359304 | tf_op jit(solution)/shard_map/ppermute | solution.py:62
  212.9 21.2 %collective-permute-start.17 = (bf16[64,16,384]{2,1,0:T(8,128)(2,1)S(1)}, bf16[64,16,384]{2,1,0:T(8,128)(2,1)}, u32[]{:S(2)}, u32[]{:S(2)}) collective-permute-start(bf16[64,16,384]{2,1,0:T(8,128)(2,1)S(1)} %collective-permute-done.9.refs_16_), channel_id=1, source_target_pairs={{0,64},{1,65},{2,66},{3,67},{4,68},{5,69},{6,70},{7,71},{8,72},{9,... | collective-permute-start | bytes 2359304 | tf_op jit(solution)/shard_map/ppermute | solution.py:62
  214.7 19.4 %collective-permute-start.21 = (bf16[64,16,384]{2,1,0:T(8,128)(2,1)S(1)}, bf16[64,16,384]{2,1,0:T(8,128)(2,1)S(1)}, u32[]{:S(2)}, u32[]{:S(2)}) collective-permute-start(bf16[64,16,384]{2,1,0:T(8,128)(2,1)S(1)} %collective-permute-done.16.refs_12_), channel_id=1, source_target_pairs={{0,16},{1,17},{2,18},{3,19},{4,20},{5,21},{6,22},{7,23},{8,24},{9,... | collective-permute-start | bytes 2359304 | tf_op jit(solution)/shard_map/ppermute | solution.py:62
  214.8 21.4 %collective-permute-start.26 = (bf16[64,16,384]{2,1,0:T(8,128)(2,1)}, bf16[64,16,384]{2,1,0:T(8,128)(2,1)}, u32[]{:S(2)}, u32[]{:S(2)}) collective-permute-start(bf16[64,16,384]{2,1,0:T(8,128)(2,1)} %collective-permute-done.15.refs_22_), channel_id=1, source_target_pairs={{0,16},{1,17},{2,18},{3,19},{4,20},{5,21},{6,22},{7,23},{8,24},{9,... | collective-permute-start | bytes 2359304 | tf_op jit(solution)/shard_map/ppermute | solution.py:62
  215.8 20.3 %collective-permute-start.24 = (bf16[64,16,384]{2,1,0:T(8,128)(2,1)}, bf16[64,16,384]{2,1,0:T(8,128)(2,1)}, u32[]{:S(2)}, u32[]{:S(2)}) collective-permute-start(bf16[64,16,384]{2,1,0:T(8,128)(2,1)} %collective-permute-done.14.refs_18_), channel_id=1, source_target_pairs={{0,16},{1,17},{2,18},{3,19},{4,20},{5,21},{6,22},{7,23},{8,24},{9,... | collective-permute-start | bytes 2359304 | tf_op jit(solution)/shard_map/ppermute | solution.py:62
  234.1 32.4 %collective-permute-start.25 = (bf16[64,16,384]{2,1,0:T(8,128)(2,1)}, bf16[64,16,384]{2,1,0:T(8,128)(2,1)}, u32[]{:S(2)}, u32[]{:S(2)}) collective-permute-start(bf16[64,16,384]{2,1,0:T(8,128)(2,1)} %collective-permute-done.17.refs_20_), channel_id=1, source_target_pairs={{0,16},{1,17},{2,18},{3,19},{4,20},{5,21},{6,22},{7,23},{8,24},{9,... | collective-permute-start | bytes 2359304 | tf_op jit(solution)/shard_map/ppermute | solution.py:62
  235.0 31.5 %collective-permute-start.18 = (bf16[128,16,128]{2,1,0:T(8,128)(2,1)S(1)}, bf16[128,16,128]{2,1,0:T(8,128)(2,1)S(1)}, u32[]{:S(2)}, u32[]{:S(2)}) collective-permute-start(bf16[128,16,128]{2,1,0:T(8,128)(2,1)S(1)} %collective-permute-done.12), channel_id=1, source_target_pairs={{0,15},{1,0},{2,1},{3,2},{4,3},{5,4},{6,5},{7,6},{8,7},{9,8},{10,9... | collective-permute-start | bytes 1572872 | tf_op jit(solution)/shard_map/ppermute | solution.py:62
  (29 other events, 1200.3 us)
